TPU v7x, 32 devices: a whole 2x2x4 slice. The times are simulated.
32 devices in a mesh: grp: 2 (over x), ex: 16 (over z, y, core).
Axes of the slice: x: 2, y: 2, z: 4, core: 2. Of those that a mesh axis runs over, the one named last changes fastest.
Arguments:
- layer_input: bfloat16 [4096, 2048], P(('grp', 'ex')), parts along dimension 0, may hold values from -6 to 6
- cotangent: bfloat16 [4096, 256], P(('grp', 'ex')), parts along dimension 0, may hold values from -6 to 6
- example_weight: bfloat16 [32], P('ex'), may hold values from 0.3984375 to 4
Outputs:
- kernel: float32 [64, 32], P(('grp', 'ex')), parts along dimension 0
- sq_norms: float32 [64], P(('grp', 'ex')), parts along dimension 0
There are 2 independent parts, one for each index of `grp`. A program takes and returns all parts, laid end to end along the dimension named above; an argument that names none is the same for every part. Nothing has to cross between parts.
All inputs are finite; a program needn't handle non-finite values.
Results may differ from a plain program's by a relative error of at most 0.0003.
Values may be sent and summed in bfloat16 or wider, within the bound.
No kernel may reach another device: no remote copies, remote signals or barrier semaphores. Data moves between devices by JAX's collectives and lax.ppermute only.
A program may use at most 64 MiB of HBM per device.

v0:
```python
import jax
import jax.numpy as jnp
from jax import lax
from jax.sharding import PartitionSpec as P


def shifted(value, axis, steps):
    count = lax.axis_size(axis)
    pairs = [(source, (source + steps) % count) for source in range(count)]
    return lax.ppermute(value, axis, pairs)


def pair_block(own_input, own_signal, own_weight, far_input, far_signal, far_weight):
    local_count = own_weight.shape[0]
    seq_length = own_input.shape[0] // local_count
    token_dots = jnp.einsum("td,ud->tu", own_input, far_input, preferred_element_type=jnp.float32)
    signal_dots = jnp.einsum(
        "th,uh->tu", own_signal, far_signal, preferred_element_type=jnp.float32
    )
    products = (token_dots * signal_dots).reshape(
        local_count, seq_length, far_weight.shape[0], seq_length
    )
    summed = jnp.sum(products, axis=(1, 3))
    return summed * (
        own_weight.astype(jnp.float32)[:, None] * far_weight.astype(jnp.float32)[None, :]
    )


def place(slot_sums, block_pair, partner, active, position):
    oriented = jnp.where(partner < position, block_pair, block_pair.T)
    chosen = (lax.iota(jnp.int32, slot_sums.shape[0]) == partner).astype(jnp.float32) * active
    return slot_sums + chosen[:, None, None] * oriented[None, :, :]


def body(layer_input, cotangent, example_weight):
    devices = lax.axis_size("ex")
    position = lax.axis_index("ex")
    half_cycle = devices // 2
    local_count = example_weight.shape[0]
    seq_length = layer_input.shape[0] // local_count
    width = layer_input.shape[1]
    window = width * cotangent.shape[1]
    empty = jnp.zeros((devices, local_count, local_count), jnp.float32)
    owner_side = (position < half_cycle).astype(jnp.float32)

    def advance_one(stride, carry):
        far_input, far_signal, far_weight, slot_sums = carry
        far_input, far_signal, far_weight = shifted((far_input, far_signal, far_weight), "ex", 1)
        active = jnp.where(stride == half_cycle, owner_side, jnp.float32(1.0))
        block_pair = pair_block(
            layer_input, cotangent, example_weight, far_input, far_signal, far_weight
        )
        partner = (position - stride) % devices
        slot_sums = place(slot_sums, block_pair, partner, active, position)
        return (far_input, far_signal, far_weight, slot_sums)

    start = (layer_input, cotangent, example_weight, empty)
    slot_sums = lax.fori_loop(1, half_cycle + 1, advance_one, start)[3]
    own_block = pair_block(
        layer_input, cotangent, example_weight, layer_input, cotangent, example_weight
    )
    columns = lax.iota(jnp.int32, devices)
    below = (columns < position).astype(jnp.float32)[:, None, None]
    mine = (columns == position).astype(jnp.float32)
    returned = lax.all_to_all(slot_sums, "ex", split_axis=0, concat_axis=0, tiled=True)
    row_blocks = (slot_sums + returned) * below
    rows_out = jnp.transpose(row_blocks, (1, 0, 2)).reshape(local_count, devices * local_count)
    own_lower = jnp.tril(own_block, -1)
    rows_out = rows_out + (own_lower[:, None, :] * mine[None, :, None]).reshape(
        local_count, devices * local_count
    )
    kernel = rows_out / (seq_length * jnp.sqrt(jnp.float32(window)))
    sq_norms = jnp.diagonal(own_block) / (seq_length * jnp.float32(window))
    return (kernel, sq_norms)


def solution(mesh):
    placed = (P(("grp", "ex"), None), P(("grp", "ex"), None), P("ex"))
    return jax.shard_map(
        body,
        mesh=mesh,
        in_specs=placed,
        out_specs=(P(("grp", "ex"), None), P(("grp", "ex"))),
        check_vma=False,
    )
```

profile of v0, /device:TPU:0, one launch (start us, length us, event | category | flops | bytes accessed | tf_op | source)
XLA Modules:
  0.0 121.6 jit_solution(6953684820849747140)
XLA Ops:
  0.7 1.1 copy.24
  1.8 0.6 copy-done.2
  2.5 107.7 %while.22 = (s32[]{:T(128)}, bf16[128,2048]{1,0:T(8,128)(2,1)S(1)}, bf16[128,256]{1,0:T(8,128)(2,1)S(1)}, bf16[2]{0:T(256)(128)(2,1)S(1)}, f32[16,2,2]{0,2,1:T(2...) while((s32[]{:T(128)}, bf16[128,2048]{1,0:T(8,128)(2,1)S(1)}, ...), condition=%wide.region_2.3_spmd.clone, body=%wide.region_0.2_spmd.clone.sunk | while | flops 75530480 | bytes 5113116 | solution.py:58
  2.5 0.5 collective-permute-start
  2.9 2.6 %collective-permute-start.1 = (bf16[128,256]{1,0:T(8,128)(2,1)S(1)}, bf16[128,256]{1,0:T(8,128)(2,1)S(1)}, u32[]{:S(2)}, u32[]{:S(2)}) collective-permute-start(bf16[128,256]{1,0:T(8,128)(2,1)S(1)} %get-tuple-element.381), channel_id=1, source_target_pairs={{0,1},{1,2},{2,3},{3,4},{4,5},{5,6},{6,7},{7,8},{8,9},{9,10},{10,1... | collective-permute-start | bytes 196616 | tf_op jit(solution)/shard_map/while/body/eval_jaxpr/ppermute | solution.py:10
  5.6 9.9 %collective-permute-done.2 = bf16[2]{0:T(256)(128)(2,1)S(1)} collective-permute-done((bf16[2]{0:T(256)(128)(2,1)S(1)}, bf16[2]{0:T(256)(128)(2,1)S(1)}, u32[]{:S(2)}, u32[]{:S(2)}) %collective-permute-start.2) | collective-permute-done | bytes 36 | tf_op jit(solution)/shard_map/while/body/eval_jaxpr/ppermute | solution.py:10
  15.6 0.1 fusion.21
  15.7 0.3 convolution_multiply_fusion.3
  16.0 0.1 reshape.96
  16.2 0.2 reduce_sum.31
  16.3 0.1 copy.21
  16.5 0.1 copy.22
  17.0 11.9 %collective-permute-done.2 = bf16[2]{0:T(256)(128)(2,1)S(1)} collective-permute-done((bf16[2]{0:T(256)(128)(2,1)S(1)}, bf16[2]{0:T(256)(128)(2,1)S(1)}, u32[]{:S(2)}, u32[]{:S(2)}) %collective-permute-start.2) | collective-permute-done | bytes 36 | tf_op jit(solution)/shard_map/while/body/eval_jaxpr/ppermute | solution.py:10
  28.9 0.1 fusion.21
  29.1 0.3 convolution_multiply_fusion.3
  29.4 0.1 reshape.96
  29.5 0.2 reduce_sum.31
  29.7 0.1 copy.21
  29.9 0.1 copy.22
  30.4 11.9 %collective-permute-done.2 = bf16[2]{0:T(256)(128)(2,1)S(1)} collective-permute-done((bf16[2]{0:T(256)(128)(2,1)S(1)}, bf16[2]{0:T(256)(128)(2,1)S(1)}, u32[]{:S(2)}, u32[]{:S(2)}) %collective-permute-start.2) | collective-permute-done | bytes 36 | tf_op jit(solution)/shard_map/while/body/eval_jaxpr/ppermute | solution.py:10
  42.2 0.1 fusion.21
  42.4 0.3 convolution_multiply_fusion.3
  42.7 0.1 reshape.96
  42.9 0.2 reduce_sum.31
  43.7 11.9 %collective-permute-done.2 = bf16[2]{0:T(256)(128)(2,1)S(1)} collective-permute-done((bf16[2]{0:T(256)(128)(2,1)S(1)}, bf16[2]{0:T(256)(128)(2,1)S(1)}, u32[]{:S(2)}, u32[]{:S(2)}) %collective-permute-start.2) | collective-permute-done | bytes 36 | tf_op jit(solution)/shard_map/while/body/eval_jaxpr/ppermute | solution.py:10
  55.6 0.1 fusion.21
  55.8 0.3 convolution_multiply_fusion.3
  56.1 0.1 reshape.96
  56.2 0.2 reduce_sum.31
  56.4 0.1 copy.21
  57.0 11.9 %collective-permute-done.2 = bf16[2]{0:T(256)(128)(2,1)S(1)} collective-permute-done((bf16[2]{0:T(256)(128)(2,1)S(1)}, bf16[2]{0:T(256)(128)(2,1)S(1)}, u32[]{:S(2)}, u32[]{:S(2)}) %collective-permute-start.2) | collective-permute-done | bytes 36 | tf_op jit(solution)/shard_map/while/body/eval_jaxpr/ppermute | solution.py:10
  68.9 0.1 fusion.21
  69.1 0.3 convolution_multiply_fusion.3
  69.4 0.1 reshape.96
  69.6 0.2 reduce_sum.31
  69.9 0.1 copy.22
  70.4 11.9 %collective-permute-done.2 = bf16[2]{0:T(256)(128)(2,1)S(1)} collective-permute-done((bf16[2]{0:T(256)(128)(2,1)S(1)}, bf16[2]{0:T(256)(128)(2,1)S(1)}, u32[]{:S(2)}, u32[]{:S(2)}) %collective-permute-start.2) | collective-permute-done | bytes 36 | tf_op jit(solution)/shard_map/while/body/eval_jaxpr/ppermute | solution.py:10
  82.3 0.1 fusion.21
  82.5 0.3 convolution_multiply_fusion.3
  82.8 0.1 reshape.96
  82.9 0.2 reduce_sum.31
  83.1 0.1 copy.21
  83.7 11.9 %collective-permute-done.2 = bf16[2]{0:T(256)(128)(2,1)S(1)} collective-permute-done((bf16[2]{0:T(256)(128)(2,1)S(1)}, bf16[2]{0:T(256)(128)(2,1)S(1)}, u32[]{:S(2)}, u32[]{:S(2)}) %collective-permute-start.2) | collective-permute-done | bytes 36 | tf_op jit(solution)/shard_map/while/body/eval_jaxpr/ppermute | solution.py:10
  95.6 0.1 fusion.21
  95.8 0.3 convolution_multiply_fusion.3
  96.1 0.1 reshape.96
  96.3 0.2 reduce_sum.31
  96.6 0.1 copy.22
  97.1 11.9 %collective-permute-done.2 = bf16[2]{0:T(256)(128)(2,1)S(1)} collective-permute-done((bf16[2]{0:T(256)(128)(2,1)S(1)}, bf16[2]{0:T(256)(128)(2,1)S(1)}, u32[]{:S(2)}, u32[]{:S(2)}) %collective-permute-start.2) | collective-permute-done | bytes 36 | tf_op jit(solution)/shard_map/while/body/eval_jaxpr/ppermute | solution.py:10
  109.0 0.1 fusion.21
  109.1 0.3 convolution_multiply_fusion.3
  109.5 0.1 reshape.96
  109.6 0.2 reduce_sum.31
  109.8 0.1 copy.21
  110.2 0.7 copy.16
  110.9 3.4 %all-to-all-start = ((f32[16,2,2]{2,1,0:T(2,128)}), f32[16,2,2]{2,1,0:T(2,128)S(1)}, u32[]{:S(2)}, u32[]{:S(2)}) async-start(f32[16,2,2]{2,1,0:T(2,128)} %copy.16), calls=%async_computation | async-start | bytes 32768 | tf_op jit(solution)/shard_map/all_to_all | solution.py:65
  114.3 0.3 fusion.2
  114.7 0.2 convolution_multiply_fusion.1
  114.8 0.1 reshape.87
  115.0 0.2 reduce_sum.27
  115.2 0.6 gather_fusion
  115.9 0.5 broadcast_multiply_fusion
  116.6 4.1 %all-to-all-done = f32[16,2,2]{2,1,0:T(2,128)S(1)} async-done(((f32[16,2,2]{2,1,0:T(2,128)}), f32[16,2,2]{2,1,0:T(2,128)S(1)}, u32[]{:S(2)}, u32[]{:S(2)}) %all-to-all-start) | async-done | bytes 288 | tf_op jit(solution)/shard_map/all_to_all | solution.py:65
  121.1 0.6 add_multiply_fusion
  (131 shorter events, 4.6 us)
Async XLA Ops:
  0.7 1.1 copy-start.1
  0.7 1.8 %copy-start = (bf16[128,2048]{1,0:T(8,128)(2,1)S(1)}, bf16[128,2048]{1,0:T(8,128)(2,1)}, u32[]{:S(2)}) copy-start(bf16[128,2048]{1,0:T(8,128)(2,1)} %param.5) | copy-start | bytes 1572868
  1.8 0.7 copy-start.2
  2.5 13.3 %collective-permute-start = (bf16[128,2048]{1,0:T(8,128)(2,1)S(1)}, bf16[128,2048]{1,0:T(8,128)(2,1)S(1)}, u32[]{:S(2)}, u32[]{:S(2)}) collective-permute-start(bf16[128,2048]{1,0:T(8,128)(2,1)S(1)} %get-tuple-element.380), channel_id=1, source_target_pairs={{0,1},{1,2},{2,3},{3,4},{4,5},{5,6},{6,7},{7,8},{8,9},{9,10},{10,1... | collective-permute-start | bytes 1572872 | tf_op jit(solution)/shard_map/while/body/eval_jaxpr/ppermute | solution.py:10
  2.9 12.6 %collective-permute-start.1 = (bf16[128,256]{1,0:T(8,128)(2,1)S(1)}, bf16[128,256]{1,0:T(8,128)(2,1)S(1)}, u32[]{:S(2)}, u32[]{:S(2)}) collective-permute-start(bf16[128,256]{1,0:T(8,128)(2,1)S(1)} %get-tuple-element.381), channel_id=1, source_target_pairs={{0,1},{1,2},{2,3},{3,4},{4,5},{5,6},{6,7},{7,8},{8,9},{9,10},{10,1... | collective-permute-start | bytes 196616 | tf_op jit(solution)/shard_map/while/body/eval_jaxpr/ppermute | solution.py:10
  5.5 10.0 %collective-permute-start.2 = (bf16[2]{0:T(256)(128)(2,1)S(1)}, bf16[2]{0:T(256)(128)(2,1)S(1)}, u32[]{:S(2)}, u32[]{:S(2)}) collective-permute-start(bf16[2]{0:T(256)(128)(2,1)S(1)} %get-tuple-element.382), channel_id=1, source_target_pairs={{0,1},{1,2},{2,3},{3,4},{4,5},{5,6},{6,7},{7,8},{8,9},{9,10},{10,1... | collective-permute-start | bytes 20 | tf_op jit(solution)/shard_map/while/body/eval_jaxpr/ppermute | solution.py:10
  16.8 12.3 %collective-permute-start = (bf16[128,2048]{1,0:T(8,128)(2,1)S(1)}, bf16[128,2048]{1,0:T(8,128)(2,1)S(1)}, u32[]{:S(2)}, u32[]{:S(2)}) collective-permute-start(bf16[128,2048]{1,0:T(8,128)(2,1)S(1)} %get-tuple-element.380), channel_id=1, source_target_pairs={{0,1},{1,2},{2,3},{3,4},{4,5},{5,6},{6,7},{7,8},{8,9},{9,10},{10,1... | collective-permute-start | bytes 1572872 | tf_op jit(solution)/shard_map/while/body/eval_jaxpr/ppermute | solution.py:10
  16.8 12.1 %collective-permute-start.1 = (bf16[128,256]{1,0:T(8,128)(2,1)S(1)}, bf16[128,256]{1,0:T(8,128)(2,1)S(1)}, u32[]{:S(2)}, u32[]{:S(2)}) collective-permute-start(bf16[128,256]{1,0:T(8,128)(2,1)S(1)} %get-tuple-element.381), channel_id=1, source_target_pairs={{0,1},{1,2},{2,3},{3,4},{4,5},{5,6},{6,7},{7,8},{8,9},{9,10},{10,1... | collective-permute-start | bytes 196616 | tf_op jit(solution)/shard_map/while/body/eval_jaxpr/ppermute | solution.py:10
  16.9 12.0 %collective-permute-start.2 = (bf16[2]{0:T(256)(128)(2,1)S(1)}, bf16[2]{0:T(256)(128)(2,1)S(1)}, u32[]{:S(2)}, u32[]{:S(2)}) collective-permute-start(bf16[2]{0:T(256)(128)(2,1)S(1)} %get-tuple-element.382), channel_id=1, source_target_pairs={{0,1},{1,2},{2,3},{3,4},{4,5},{5,6},{6,7},{7,8},{8,9},{9,10},{10,1... | collective-permute-start | bytes 20 | tf_op jit(solution)/shard_map/while/body/eval_jaxpr/ppermute | solution.py:10
  30.1 12.3 %collective-permute-start = (bf16[128,2048]{1,0:T(8,128)(2,1)S(1)}, bf16[128,2048]{1,0:T(8,128)(2,1)S(1)}, u32[]{:S(2)}, u32[]{:S(2)}) collective-permute-start(bf16[128,2048]{1,0:T(8,128)(2,1)S(1)} %get-tuple-element.380), channel_id=1, source_target_pairs={{0,1},{1,2},{2,3},{3,4},{4,5},{5,6},{6,7},{7,8},{8,9},{9,10},{10,1... | collective-permute-start | bytes 1572872 | tf_op jit(solution)/shard_map/while/body/eval_jaxpr/ppermute | solution.py:10
  30.2 12.1 %collective-permute-start.1 = (bf16[128,256]{1,0:T(8,128)(2,1)S(1)}, bf16[128,256]{1,0:T(8,128)(2,1)S(1)}, u32[]{:S(2)}, u32[]{:S(2)}) collective-permute-start(bf16[128,256]{1,0:T(8,128)(2,1)S(1)} %get-tuple-element.381), channel_id=1, source_target_pairs={{0,1},{1,2},{2,3},{3,4},{4,5},{5,6},{6,7},{7,8},{8,9},{9,10},{10,1... | collective-permute-start | bytes 196616 | tf_op jit(solution)/shard_map/while/body/eval_jaxpr/ppermute | solution.py:10
  30.2 12.0 %collective-permute-start.2 = (bf16[2]{0:T(256)(128)(2,1)S(1)}, bf16[2]{0:T(256)(128)(2,1)S(1)}, u32[]{:S(2)}, u32[]{:S(2)}) collective-permute-start(bf16[2]{0:T(256)(128)(2,1)S(1)} %get-tuple-element.382), channel_id=1, source_target_pairs={{0,1},{1,2},{2,3},{3,4},{4,5},{5,6},{6,7},{7,8},{8,9},{9,10},{10,1... | collective-permute-start | bytes 20 | tf_op jit(solution)/shard_map/while/body/eval_jaxpr/ppermute | solution.py:10
  43.4 12.3 %collective-permute-start = (bf16[128,2048]{1,0:T(8,128)(2,1)S(1)}, bf16[128,2048]{1,0:T(8,128)(2,1)S(1)}, u32[]{:S(2)}, u32[]{:S(2)}) collective-permute-start(bf16[128,2048]{1,0:T(8,128)(2,1)S(1)} %get-tuple-element.380), channel_id=1, source_target_pairs={{0,1},{1,2},{2,3},{3,4},{4,5},{5,6},{6,7},{7,8},{8,9},{9,10},{10,1... | collective-permute-start | bytes 1572872 | tf_op jit(solution)/shard_map/while/body/eval_jaxpr/ppermute | solution.py:10
  43.5 12.1 %collective-permute-start.1 = (bf16[128,256]{1,0:T(8,128)(2,1)S(1)}, bf16[128,256]{1,0:T(8,128)(2,1)S(1)}, u32[]{:S(2)}, u32[]{:S(2)}) collective-permute-start(bf16[128,256]{1,0:T(8,128)(2,1)S(1)} %get-tuple-element.381), channel_id=1, source_target_pairs={{0,1},{1,2},{2,3},{3,4},{4,5},{5,6},{6,7},{7,8},{8,9},{9,10},{10,1... | collective-permute-start | bytes 196616 | tf_op jit(solution)/shard_map/while/body/eval_jaxpr/ppermute | solution.py:10
  43.6 12.0 %collective-permute-start.2 = (bf16[2]{0:T(256)(128)(2,1)S(1)}, bf16[2]{0:T(256)(128)(2,1)S(1)}, u32[]{:S(2)}, u32[]{:S(2)}) collective-permute-start(bf16[2]{0:T(256)(128)(2,1)S(1)} %get-tuple-element.382), channel_id=1, source_target_pairs={{0,1},{1,2},{2,3},{3,4},{4,5},{5,6},{6,7},{7,8},{8,9},{9,10},{10,1... | collective-permute-start | bytes 20 | tf_op jit(solution)/shard_map/while/body/eval_jaxpr/ppermute | solution.py:10
  56.8 12.3 %collective-permute-start = (bf16[128,2048]{1,0:T(8,128)(2,1)S(1)}, bf16[128,2048]{1,0:T(8,128)(2,1)S(1)}, u32[]{:S(2)}, u32[]{:S(2)}) collective-permute-start(bf16[128,2048]{1,0:T(8,128)(2,1)S(1)} %get-tuple-element.380), channel_id=1, source_target_pairs={{0,1},{1,2},{2,3},{3,4},{4,5},{5,6},{6,7},{7,8},{8,9},{9,10},{10,1... | collective-permute-start | bytes 1572872 | tf_op jit(solution)/shard_map/while/body/eval_jaxpr/ppermute | solution.py:10
  56.9 12.1 %collective-permute-start.1 = (bf16[128,256]{1,0:T(8,128)(2,1)S(1)}, bf16[128,256]{1,0:T(8,128)(2,1)S(1)}, u32[]{:S(2)}, u32[]{:S(2)}) collective-permute-start(bf16[128,256]{1,0:T(8,128)(2,1)S(1)} %get-tuple-element.381), channel_id=1, source_target_pairs={{0,1},{1,2},{2,3},{3,4},{4,5},{5,6},{6,7},{7,8},{8,9},{9,10},{10,1... | collective-permute-start | bytes 196616 | tf_op jit(solution)/shard_map/while/body/eval_jaxpr/ppermute | solution.py:10
  56.9 12.0 %collective-permute-start.2 = (bf16[2]{0:T(256)(128)(2,1)S(1)}, bf16[2]{0:T(256)(128)(2,1)S(1)}, u32[]{:S(2)}, u32[]{:S(2)}) collective-permute-start(bf16[2]{0:T(256)(128)(2,1)S(1)} %get-tuple-element.382), channel_id=1, source_target_pairs={{0,1},{1,2},{2,3},{3,4},{4,5},{5,6},{6,7},{7,8},{8,9},{9,10},{10,1... | collective-permute-start | bytes 20 | tf_op jit(solution)/shard_map/while/body/eval_jaxpr/ppermute | solution.py:10
  70.1 12.3 %collective-permute-start = (bf16[128,2048]{1,0:T(8,128)(2,1)S(1)}, bf16[128,2048]{1,0:T(8,128)(2,1)S(1)}, u32[]{:S(2)}, u32[]{:S(2)}) collective-permute-start(bf16[128,2048]{1,0:T(8,128)(2,1)S(1)} %get-tuple-element.380), channel_id=1, source_target_pairs={{0,1},{1,2},{2,3},{3,4},{4,5},{5,6},{6,7},{7,8},{8,9},{9,10},{10,1... | collective-permute-start | bytes 1572872 | tf_op jit(solution)/shard_map/while/body/eval_jaxpr/ppermute | solution.py:10
  70.2 12.1 %collective-permute-start.1 = (bf16[128,256]{1,0:T(8,128)(2,1)S(1)}, bf16[128,256]{1,0:T(8,128)(2,1)S(1)}, u32[]{:S(2)}, u32[]{:S(2)}) collective-permute-start(bf16[128,256]{1,0:T(8,128)(2,1)S(1)} %get-tuple-element.381), channel_id=1, source_target_pairs={{0,1},{1,2},{2,3},{3,4},{4,5},{5,6},{6,7},{7,8},{8,9},{9,10},{10,1... | collective-permute-start | bytes 196616 | tf_op jit(solution)/shard_map/while/body/eval_jaxpr/ppermute | solution.py:10
  70.3 12.0 %collective-permute-start.2 = (bf16[2]{0:T(256)(128)(2,1)S(1)}, bf16[2]{0:T(256)(128)(2,1)S(1)}, u32[]{:S(2)}, u32[]{:S(2)}) collective-permute-start(bf16[2]{0:T(256)(128)(2,1)S(1)} %get-tuple-element.382), channel_id=1, source_target_pairs={{0,1},{1,2},{2,3},{3,4},{4,5},{5,6},{6,7},{7,8},{8,9},{9,10},{10,1... | collective-permute-start | bytes 20 | tf_op jit(solution)/shard_map/while/body/eval_jaxpr/ppermute | solution.py:10
  83.5 12.3 %collective-permute-start = (bf16[128,2048]{1,0:T(8,128)(2,1)S(1)}, bf16[128,2048]{1,0:T(8,128)(2,1)S(1)}, u32[]{:S(2)}, u32[]{:S(2)}) collective-permute-start(bf16[128,2048]{1,0:T(8,128)(2,1)S(1)} %get-tuple-element.380), channel_id=1, source_target_pairs={{0,1},{1,2},{2,3},{3,4},{4,5},{5,6},{6,7},{7,8},{8,9},{9,10},{10,1... | collective-permute-start | bytes 1572872 | tf_op jit(solution)/shard_map/while/body/eval_jaxpr/ppermute | solution.py:10
  83.6 12.1 %collective-permute-start.1 = (bf16[128,256]{1,0:T(8,128)(2,1)S(1)}, bf16[128,256]{1,0:T(8,128)(2,1)S(1)}, u32[]{:S(2)}, u32[]{:S(2)}) collective-permute-start(bf16[128,256]{1,0:T(8,128)(2,1)S(1)} %get-tuple-element.381), channel_id=1, source_target_pairs={{0,1},{1,2},{2,3},{3,4},{4,5},{5,6},{6,7},{7,8},{8,9},{9,10},{10,1... | collective-permute-start | bytes 196616 | tf_op jit(solution)/shard_map/while/body/eval_jaxpr/ppermute | solution.py:10
  83.6 12.0 %collective-permute-start.2 = (bf16[2]{0:T(256)(128)(2,1)S(1)}, bf16[2]{0:T(256)(128)(2,1)S(1)}, u32[]{:S(2)}, u32[]{:S(2)}) collective-permute-start(bf16[2]{0:T(256)(128)(2,1)S(1)} %get-tuple-element.382), channel_id=1, source_target_pairs={{0,1},{1,2},{2,3},{3,4},{4,5},{5,6},{6,7},{7,8},{8,9},{9,10},{10,1... | collective-permute-start | bytes 20 | tf_op jit(solution)/shard_map/while/body/eval_jaxpr/ppermute | solution.py:10
  96.8 12.3 %collective-permute-start = (bf16[128,2048]{1,0:T(8,128)(2,1)S(1)}, bf16[128,2048]{1,0:T(8,128)(2,1)S(1)}, u32[]{:S(2)}, u32[]{:S(2)}) collective-permute-start(bf16[128,2048]{1,0:T(8,128)(2,1)S(1)} %get-tuple-element.380), channel_id=1, source_target_pairs={{0,1},{1,2},{2,3},{3,4},{4,5},{5,6},{6,7},{7,8},{8,9},{9,10},{10,1... | collective-permute-start | bytes 1572872 | tf_op jit(solution)/shard_map/while/body/eval_jaxpr/ppermute | solution.py:10
  96.9 12.1 %collective-permute-start.1 = (bf16[128,256]{1,0:T(8,128)(2,1)S(1)}, bf16[128,256]{1,0:T(8,128)(2,1)S(1)}, u32[]{:S(2)}, u32[]{:S(2)}) collective-permute-start(bf16[128,256]{1,0:T(8,128)(2,1)S(1)} %get-tuple-element.381), channel_id=1, source_target_pairs={{0,1},{1,2},{2,3},{3,4},{4,5},{5,6},{6,7},{7,8},{8,9},{9,10},{10,1... | collective-permute-start | bytes 196616 | tf_op jit(solution)/shard_map/while/body/eval_jaxpr/ppermute | solution.py:10
  97.0 12.0 %collective-permute-start.2 = (bf16[2]{0:T(256)(128)(2,1)S(1)}, bf16[2]{0:T(256)(128)(2,1)S(1)}, u32[]{:S(2)}, u32[]{:S(2)}) collective-permute-start(bf16[2]{0:T(256)(128)(2,1)S(1)} %get-tuple-element.382), channel_id=1, source_target_pairs={{0,1},{1,2},{2,3},{3,4},{4,5},{5,6},{6,7},{7,8},{8,9},{9,10},{10,1... | collective-permute-start | bytes 20 | tf_op jit(solution)/shard_map/while/body/eval_jaxpr/ppermute | solution.py:10
  110.9 9.9 %all-to-all-start = ((f32[16,2,2]{2,1,0:T(2,128)}), f32[16,2,2]{2,1,0:T(2,128)S(1)}, u32[]{:S(2)}, u32[]{:S(2)}) async-start(f32[16,2,2]{2,1,0:T(2,128)} %copy.16), calls=%async_computation | async-start | bytes 32768 | tf_op jit(solution)/shard_map/all_to_all | solution.py:65
where the time goes:
time: 122 us
  waiting for transfers between devices  97.4 us (80%)
  starting transfers between devices  7.81 us (6%)
  local copies, waits for them, and re-layouts  6.72 us (6%)
  other arithmetic  4.04 us (3%)
  matrix products  3.97 us (3%)
    ppermute x24, waiting for transfers between devices, shifted(): return lax.ppermute(value, axis, pairs)  93.3 us
    ppermute x24, starting transfers between devices, shifted(): return lax.ppermute(value, axis, pairs)  4.36 us
    all_to_all x1, waiting for transfers between devices, body(): lax.all_to_all(slot_sums, 'ex', split_axis=0, concat_axis=0, tiled=True)  4.13 us
    all_to_all x1, starting transfers between devices, body(): lax.all_to_all(slot_sums, 'ex', split_axis=0, concat_axis=0, tiled=True)  3.45 us
    dot_general x9, matrix products, pair_block(): jnp.einsum('td,ud->tu', own_input, far_input, preferred_element_type=jnp....  2.82 us
  transfers between devices with their start and end apart: 25, of which 9 were waited for; matrix products, arithmetic and copies ran while one was open for 3% of the time, Pallas kernels for 0%

commit v1 on v0

v1 whole, which is shorter than its diff:
```python
import functools

import jax
import jax.numpy as jnp
from jax import lax
from jax.experimental import pallas as pl
from jax.experimental.pallas import tpu as pltpu
from jax.sharding import PartitionSpec as P

LANES = 128


def swapped(value, distance):
    count = lax.axis_size("ex")
    return lax.ppermute(value, "ex", [(i, i ^ distance) for i in range(count)])


def dot_t(a, b):
    return lax.dot_general(a, b, (((1,), (1,)), ((), ())), preferred_element_type=jnp.float32)


def split_dot(a, b):
    high = a.astype(jnp.bfloat16)
    rest = a - high.astype(jnp.float32)
    middle = rest.astype(jnp.bfloat16)
    low = (rest - middle.astype(jnp.float32)).astype(jnp.bfloat16)
    parts = [jnp.dot(p, b, preferred_element_type=jnp.float32) for p in (high, middle, low)]
    return parts[0] + (parts[1] + parts[2])


def gram_kernel(devices, local_count, me_ref, weight_ref, *refs):
    chips, planes = devices // 2, devices // 4
    x_refs, refs = refs[:chips], refs[chips:]
    z_refs, refs = refs[:planes], refs[planes:]
    y_ref, core_ref, out_ref, x_all, c_all, rows_ref = refs
    chip_rows = x_refs[0].shape[0]
    tokens = chip_rows // 2
    examples = 2 * local_count
    seq_length = tokens // local_count

    for s in range(chips):
        x_all[s] = x_refs[s][...]
    for z in range(planes):
        c_all[2 * z, :tokens] = z_refs[z][...]
        c_all[2 * z + 1, :tokens] = y_ref[z]
        c_all[2 * z, tokens:] = core_ref[0, z]
        c_all[2 * z + 1, tokens:] = core_ref[1, z]
    rows_ref[...] = jnp.zeros_like(rows_ref)

    def block(i, j):
        product = dot_t(x_all[i], x_all[j]) * dot_t(c_all[i], c_all[j])
        summed = jnp.sum(product.reshape(examples, seq_length, chip_rows), axis=1)
        rows_ref[i, j, :examples] = summed

    if chips <= 8:
        for i in range(chips):
            for j in range(i + 1):
                block(i, j)
    else:

        @pl.loop(0, chips)
        def _(i):
            @pl.loop(0, i + 1)
            def _(j):
                block(i, j)

    held = rows_ref.shape[2]
    count = chips * examples
    row = lax.broadcasted_iota(jnp.int32, (chip_rows, LANES), 0)
    column = lax.broadcasted_iota(jnp.int32, (chip_rows, LANES), 1)
    lower = jnp.zeros((chips * held, LANES), jnp.float32)
    for j in range(chips):
        group = (row // seq_length + j * examples == column).astype(jnp.bfloat16)
        lower += split_dot(rows_ref[:, j].reshape(chips * held, chip_rows), group)
    lower = lower.reshape(chips, held, LANES)[:, :examples].reshape(count, LANES)
    square = lower if count == LANES else jnp.concatenate([lower, jnp.zeros((LANES - count, LANES), jnp.float32)])
    row = lax.broadcasted_iota(jnp.int32, (LANES, LANES), 0)
    column = lax.broadcasted_iota(jnp.int32, (LANES, LANES), 1)
    gram = square + jnp.where(row // examples < column // examples, square.T, 0.0)
    to_global = (jnp.bitwise_xor(row, me_ref[0] * local_count) == column).astype(jnp.bfloat16)
    gram = split_dot(gram[:count], to_global)
    out_ref[:, :8] = gram.reshape(planes, 8, LANES)
    out_ref[:, 8:] = jnp.broadcast_to(weight_ref[...], (planes, 8, LANES))


def body(layer_input, cotangent, example_weight):
    devices = lax.axis_size("ex")
    me = lax.axis_index("ex")
    chips, planes = devices // 2, devices // 4
    chip, core = me // 2, me % 2
    local_count = example_weight.shape[0]
    tokens, width = layer_input.shape
    seq_length = tokens // local_count
    window = width * cotangent.shape[1]
    own_width = width // devices
    weight = example_weight.astype(jnp.float32)

    cot = {0: cotangent}
    for z in range(planes - 1, 0, -1):
        cot[z] = swapped(cotangent, 4 * z)

    columns = layer_input.reshape(tokens, chips, 2, own_width)
    columns = jnp.transpose(columns, (2, 1, 0, 3))
    keep = lax.dynamic_index_in_dim(columns, core, 0, keepdims=False)
    give = lax.dynamic_index_in_dim(columns, 1 - core, 0, keepdims=False)
    got = swapped(give, 1)
    pair = jnp.stack([keep, got], axis=1).reshape(chips, 2 * tokens, own_width)
    mine = {}
    for s in [0] + list(range(chips - 1, 0, -1)):
        part = lax.dynamic_index_in_dim(pair, chip ^ s, 0, keepdims=False)
        mine[s] = swapped(part, 2 * s) if s else part

    over_z = jnp.stack([cot[z] for z in range(planes)])
    over_y = swapped(over_z, 2)
    over_core = swapped(jnp.stack([over_z, over_y]), 1)

    lane = lax.broadcasted_iota(jnp.int32, (8, LANES), 1)
    slot = lane - me * local_count
    sublane = lax.broadcasted_iota(jnp.int32, (8, LANES), 0)
    weight_row = jnp.zeros((8, LANES), jnp.float32)
    for k in range(local_count):
        weight_row = jnp.where((slot == k) & (sublane == 0), weight[k], weight_row)

    smem = pl.BlockSpec(memory_space=pltpu.SMEM)
    vmem = pl.BlockSpec(memory_space=pltpu.VMEM)
    operands = [mine[s] for s in range(chips)] + [cot[z] for z in range(planes)] + [over_y, over_core]
    partial = pl.pallas_call(
        functools.partial(gram_kernel, devices, local_count),
        out_shape=jax.ShapeDtypeStruct((planes, 16, LANES), jnp.float32),
        in_specs=[smem, vmem] + [vmem] * len(operands),
        out_specs=vmem,
        scratch_shapes=[
            pltpu.VMEM((chips, 2 * tokens, own_width), layer_input.dtype),
            pltpu.VMEM((chips, 2 * tokens, cotangent.shape[1]), cotangent.dtype),
            pltpu.VMEM((chips, chips, 8, 2 * tokens), jnp.float32),
        ],
        compiler_params=pltpu.CompilerParams(vmem_limit_bytes=48 * 1024 * 1024),
        name="gram",
    )(me.astype(jnp.int32).reshape(1), weight_row, *operands)

    total = partial[0]
    for z in range(planes - 1, 0, -1):
        total = total + swapped(partial[z], 4 * z)
    rows = local_count
    sums = jnp.concatenate([total[:rows], total[8:9]])
    for q in (3, 2, 1):
        sums = sums + swapped(jnp.concatenate([total[q * rows : (q + 1) * rows], total[8:9]]), q)

    count = devices * local_count
    grams = sums[:rows, :count] * (weight[:, None] * sums[rows : rows + 1, :count])
    own = (me * local_count + lax.iota(jnp.int32, local_count))[:, None]
    column = lax.iota(jnp.int32, count)[None, :]
    kernel = jnp.where(column < own, grams, 0.0) / (seq_length * jnp.sqrt(jnp.float32(window)))
    sq_norms = jnp.sum(jnp.where(column == own, grams, 0.0), axis=1) / (seq_length * jnp.float32(window))
    return (kernel, sq_norms)


def solution(mesh):
    placed = (P(("grp", "ex"), None), P(("grp", "ex"), None), P("ex"))
    return jax.shard_map(
        body,
        mesh=mesh,
        in_specs=placed,
        out_specs=(P(("grp", "ex"), None), P(("grp", "ex"))),
        check_vma=False,
    )
```

time: 122 us -> 53.2 us (0.44)
  waiting for transfers between devices: 97.4 us -> 17.8 us
  starting transfers between devices: 7.81 us -> 25.3 us
  matrix products: 3.97 us -> 0 us
  local copies, waits for them, and re-layouts: 6.72 us -> 2.97 us
  Pallas kernels: 0 us -> 3.12 us
    ppermute x24 -> x19, waiting for transfers between devices: 93.3 us -> 17.8 us  [swapped(): return lax.ppermute(value, 'ex', [(i, i ^ distance) for i in range(count)])]
    ppermute x24 -> x19, starting transfers between devices: 4.36 us -> 25.3 us  [swapped(): return lax.ppermute(value, 'ex', [(i, i ^ distance) for i in range(count)])]
    all_to_all x1 -> x0, waiting for transfers between devices: 4.13 us -> none  [body(): lax.all_to_all(slot_sums, 'ex', split_axis=0, concat_axis=0, tiled=True)]
    dot_general x18 -> x0, matrix products: 3.97 us -> none  [the longest x9 2.82 us: pair_block(): jnp.einsum('td,ud->tu', own_input, far_input, preferred_element_type=jnp....]
    all_to_all x1 -> x0, starting transfers between devices: 3.45 us -> none  [body(): lax.all_to_all(slot_sums, 'ex', split_axis=0, concat_axis=0, tiled=True)]
    pallas_call x0 -> x1, Pallas kernels: none -> 3.12 us  [body(): pl.pallas_call(functools.partial(gram_kernel, devices, local_count), out_...]
    reduce_sum x9 -> x1, other arithmetic: 1.51 us -> 0.18 us  [body(): jnp.sum(jnp.where(column == own, grams, 0.0), axis=1)]
    reshape x10 -> x0, local copies, waits for them, and re-layouts: 1.24 us -> none  [the longest x9 1.15 us: pair_block(): (token_dots * signal_dots).reshape(local_count, seq_length, far_weight.sh...]
  transfers between devices with their start and end apart: 25 -> 19, of which waited for: 9 -> 9; matrix products, arithmetic and copies ran while one was open for 3% -> 7% of each run, Pallas kernels for 0% -> 0%
where the time goes in v1:
time: 53.2 us; the launch traced here: 53 us
  starting transfers between devices  25.3 us (48%)
  waiting for transfers between devices  17.8 us (33%)
  Pallas kernels  3.12 us (6%)
  local copies, waits for them, and re-layouts  2.97 us (6%)
  other arithmetic  2.91 us (5%)
  between operations  0.84 us (2%)
    ppermute x19, starting transfers between devices, swapped(): return lax.ppermute(value, 'ex', [(i, i ^ distance) for i in range(count)])  25.3 us
    ppermute x19, waiting for transfers between devices, swapped(): return lax.ppermute(value, 'ex', [(i, i ^ distance) for i in range(count)])  17.8 us
    pallas_call x1, Pallas kernels, body(): pl.pallas_call(functools.partial(gram_kernel, devices, local_count), out_...  3.12 us
    unnamed x5, local copies, waits for them, and re-layouts  1.99 us
    select_n x1, other arithmetic, body(): weight_row = jnp.where((slot == k) & (sublane == 0), weight[k], weight_row)  1.39 us
  transfers between devices with their start and end apart: 19, of which 9 were waited for; matrix products, arithmetic and copies ran while one was open for 7% of the time, Pallas kernels for 0%

profile of v1, /device:TPU:0, one launch (start us, length us, event | category | flops | bytes accessed | tf_op | source)
XLA Modules:
  0.0 53.0 jit_solution(16855030269771894397)
XLA Ops:
  0.6 3.1 %collective-permute-start.8 = (bf16[128,256]{1,0:T(8,128)(2,1)}, bf16[128,256]{1,0:T(8,128)(2,1)S(1)}, u32[]{:S(2)}, u32[]{:S(2)}) collective-permute-start(bf16[128,256]{1,0:T(8,128)(2,1)} %refs_8_.1), channel_id=1, source_target_pairs={{0,4},{1,5},{2,6},{3,7},{4,0},{5,1},{6,2},{7,3},{8,12},{9,13},{10,... | collective-permute-start | bytes 196616 | tf_op jit(solution)/shard_map/ppermute | solution.py:15
  3.7 2.6 %collective-permute-start.9 = (bf16[128,256]{1,0:T(8,128)(2,1)}, bf16[128,256]{1,0:T(8,128)(2,1)S(1)}, u32[]{:S(2)}, u32[]{:S(2)}) collective-permute-start(bf16[128,256]{1,0:T(8,128)(2,1)} %refs_8_.1), channel_id=1, source_target_pairs={{0,8},{1,9},{2,10},{3,11},{4,12},{5,13},{6,14},{7,15},{8,0},{9,1},... | collective-permute-start | bytes 196616 | tf_op jit(solution)/shard_map/ppermute | solution.py:15
  6.3 0.0 collective-permute-start.10
  6.3 0.0 copy-start
  6.3 1.3 %copy.7 = bf16[128,2048]{0,1:T(8,128)(2,1)S(1)} copy(bf16[128,2048]{1,0:T(8,128)(2,1)} %param.3) | data formatting | bytes 1048576 | tf_op args[0]
  7.7 0.0 collective-permute-done.8.refs_9_
  7.7 3.5 %collective-permute-done.9.refs_10_ = bf16[128,256]{1,0:T(8,128)(2,1)S(1)} collective-permute-done((bf16[128,256]{1,0:T(8,128)(2,1)}, bf16[128,256]{1,0:T(8,128)(2,1)S(1)}, u32[]{:S(2)}, u32[]{:S(2)}) %collective-permute-start.9) | collective-permute-done | bytes 65568 | tf_op jit(solution)/shard_map/ppermute | solution.py:15
  11.2 1.4 %collective-permute-done.10.refs_11_ = bf16[128,256]{1,0:T(8,128)(2,1)S(1)} collective-permute-done((bf16[128,256]{1,0:T(8,128)(2,1)}, bf16[128,256]{1,0:T(8,128)(2,1)S(1)}, u32[]{:S(2)}, u32[]{:S(2)}) %collective-permute-start.10) | collective-permute-done | bytes 65568 | tf_op jit(solution)/shard_map/ppermute | solution.py:15
  12.6 0.0 copy-done
  12.7 1.6 %collective-permute-start.11 = (bf16[4,128,256]{2,1,0:T(8,128)(2,1)S(1)}, bf16[4,128,256]{2,1,0:T(8,128)(2,1)S(1)}, u32[]{:S(2)}, u32[]{:S(2)}) collective-permute-start(bf16[4,128,256]{2,1,0:T(8,128)(2,1)S(1)} %get-tuple-element.15), channel_id=1, source_target_pairs={{0,2},{1,3},{2,0},{3,1},{4,6},{5,7},{6,4},{7,5},{8,10},{9,11},{10,... | collective-permute-start | bytes 786440 | tf_op jit(solution)/shard_map/ppermute | solution.py:15
  14.3 0.1 collective-permute-start
  14.4 0.0 copy-start.1
  14.5 0.6 %copy-done.1 = bf16[2]{0:T(256)(128)(2,1)S(1)} copy-done((bf16[2]{0:T(256)(128)(2,1)S(1)}, bf16[2]{0:T(256)(128)(2,1)}, u32[]{:S(2)}) %copy-start.1) | copy-done | bytes 28
  15.1 0.6 %fusion.12 = (f32[1]{0:T(128)}, f32[1]{0:T(128)}) fusion(bf16[2]{0:T(256)(128)(2,1)S(1)} %copy-done.1), kind=kLoop, calls=%fused_computation.41 | loop fusion | bytes 16 | tf_op jit(solution)/shard_map/slice | solution.py:122
  15.7 3.5 %collective-permute-done.11.refs_12_ = bf16[4,128,256]{2,1,0:T(8,128)(2,1)S(1)} collective-permute-done((bf16[4,128,256]{2,1,0:T(8,128)(2,1)S(1)}, bf16[4,128,256]{2,1,0:T(8,128)(2,1)S(1)}, u32[]{:S(2)}, u32[]{:S(2)}) %collective-permute-start.11) | collective-permute-done | bytes 262176 | tf_op jit(solution)/shard_map/ppermute | solution.py:15
  19.1 0.1 pad_maximum_fusion.1
  19.2 0.1 collective-permute-start.12
  19.3 0.0 collective-permute-done
  19.3 0.1 pad_maximum_fusion
  19.3 0.3 copy.10
  19.6 0.1 dynamic-slice_bitcast_fusion.2
  19.7 1.6 %collective-permute-start.1 = (bf16[256,128]{1,0:T(8,128)(2,1)S(1)}, bf16[256,128]{1,0:T(8,128)(2,1)S(1)}, u32[]{:S(2)}, u32[]{:S(2)}) collective-permute-start(bf16[256,128]{1,0:T(8,128)(2,1)S(1)} %get-tuple-element.10), channel_id=1, source_target_pairs={{0,2},{1,3},{2,0},{3,1},{4,6},{5,7},{6,4},{7,5},{8,10},{9,11},{10,... | collective-permute-start | bytes 196616 | tf_op jit(solution)/shard_map/ppermute | solution.py:15
  21.3 0.7 %collective-permute-start.2 = (bf16[256,128]{1,0:T(8,128)(2,1)S(1)}, bf16[256,128]{1,0:T(8,128)(2,1)S(1)}, u32[]{:S(2)}, u32[]{:S(2)}) collective-permute-start(bf16[256,128]{1,0:T(8,128)(2,1)S(1)} %get-tuple-element.9), channel_id=1, source_target_pairs={{0,4},{1,5},{2,6},{3,7},{4,0},{5,1},{6,2},{7,3},{8,12},{9,13},{10,... | collective-permute-start | bytes 196616 | tf_op jit(solution)/shard_map/ppermute | solution.py:15
  22.0 1.3 %collective-permute-start.3 = (bf16[256,128]{1,0:T(8,128)(2,1)S(1)}, bf16[256,128]{1,0:T(8,128)(2,1)S(1)}, u32[]{:S(2)}, u32[]{:S(2)}) collective-permute-start(bf16[256,128]{1,0:T(8,128)(2,1)S(1)} %get-tuple-element.8), channel_id=1, source_target_pairs={{0,6},{1,7},{2,4},{3,5},{4,2},{5,3},{6,0},{7,1},{8,14},{9,15},{10,... | collective-permute-start | bytes 196616 | tf_op jit(solution)/shard_map/ppermute | solution.py:15
  23.2 2.0 %collective-permute-start.4 = (bf16[256,128]{1,0:T(8,128)(2,1)S(1)}, bf16[256,128]{1,0:T(8,128)(2,1)S(1)}, u32[]{:S(2)}, u32[]{:S(2)}) collective-permute-start(bf16[256,128]{1,0:T(8,128)(2,1)S(1)} %get-tuple-element.7), channel_id=1, source_target_pairs={{0,8},{1,9},{2,10},{3,11},{4,12},{5,13},{6,14},{7,15},{8,0},{9,1},... | collective-permute-start | bytes 196616 | tf_op jit(solution)/shard_map/ppermute | solution.py:15
  25.3 0.0 collective-permute-done.1.refs_1_
  25.3 1.9 %collective-permute-start.5 = (bf16[256,128]{1,0:T(8,128)(2,1)S(1)}, bf16[256,128]{1,0:T(8,128)(2,1)S(1)}, u32[]{:S(2)}, u32[]{:S(2)}) collective-permute-start(bf16[256,128]{1,0:T(8,128)(2,1)S(1)} %get-tuple-element.6), channel_id=1, source_target_pairs={{0,10},{1,11},{2,8},{3,9},{4,14},{5,15},{6,12},{7,13},{8,2},{9,3},... | collective-permute-start | bytes 196616 | tf_op jit(solution)/shard_map/ppermute | solution.py:15
  27.2 0.0 collective-permute-done.2.refs_2_
  27.2 1.7 %collective-permute-start.6 = (bf16[256,128]{1,0:T(8,128)(2,1)S(1)}, bf16[256,128]{1,0:T(8,128)(2,1)S(1)}, u32[]{:S(2)}, u32[]{:S(2)}) collective-permute-start(bf16[256,128]{1,0:T(8,128)(2,1)S(1)} %get-tuple-element.5), channel_id=1, source_target_pairs={{0,12},{1,13},{2,14},{3,15},{4,8},{5,9},{6,10},{7,11},{8,4},{9,5},... | collective-permute-start | bytes 196616 | tf_op jit(solution)/shard_map/ppermute | solution.py:15
  28.9 0.0 collective-permute-done.3.refs_3_
  28.9 2.1 %collective-permute-start.7 = (bf16[256,128]{1,0:T(8,128)(2,1)S(1)}, bf16[256,128]{1,0:T(8,128)(2,1)S(1)}, u32[]{:S(2)}, u32[]{:S(2)}) collective-permute-start(bf16[256,128]{1,0:T(8,128)(2,1)S(1)} %get-tuple-element.4), channel_id=1, source_target_pairs={{0,14},{1,15},{2,12},{3,13},{4,10},{5,11},{6,8},{7,9},{8,6},{9,7},... | collective-permute-start | bytes 196616 | tf_op jit(solution)/shard_map/ppermute | solution.py:15
  31.0 1.4 %select_select_fusion.weight_ref = f32[8,128]{1,0:T(8,128)S(1)} fusion(f32[]{:T(128)} %bitcast.2, f32[]{:T(128)} %bitcast.1, pred[128]{0:T(512)(128)(4,1)S(1)} %get-tuple-element.26, pred[128]{0:T(512)(128)(4,1)S(1)} %get-tuple-element.27, pred[8]{0:T(512)(128)(4,1)S(1)} %iota_compare_fusion), kind=kLoop, calls=%fused_computation.20 | loop fusion | flops 4096 | bytes 4368 | tf_op jit(solution)/shard_map/jit(_where)/select_n | solution.py:122
  32.4 0.0 collective-permute-done.4.refs_4_
  32.4 4.1 %collective-permute-done.5.refs_5_ = bf16[256,128]{1,0:T(8,128)(2,1)S(1)} collective-permute-done((bf16[256,128]{1,0:T(8,128)(2,1)S(1)}, bf16[256,128]{1,0:T(8,128)(2,1)S(1)}, u32[]{:S(2)}, u32[]{:S(2)}) %collective-permute-start.5) | collective-permute-done | bytes 65568 | tf_op jit(solution)/shard_map/ppermute | solution.py:15
  36.5 0.0 collective-permute-done.6.refs_6_
  36.5 0.0 collective-permute-done.7.refs_7_
  36.5 0.0 collective-permute-done.12.refs_13_
  36.5 3.1 %gram.1 = f32[4,16,128]{2,1,0:T(8,128)S(1)} custom-call(s32[1]{0:T(128)} %bitcast.me_ref, f32[8,128]{1,0:T(8,128)S(1)} %select_select_fusion.weight_ref, bf16[256,128]{1,0:T(8,128)(2,1)S(1)} %get-tuple-element.11.refs_0_, bf16[256,128]{1,0:T(8,128)(2,1)S(1)} %collective-permute-done.1.refs_1_, bf16[256,128]{1,0:T(8,128)(2,1)S(1)} %collective-permute-done.2.refs_2_, ...), custom_call_target="tpu_custom_call" | custom-call | tf_op jit(solution)/shard_map/gram/pallas_call | solution.py:127
  39.6 2.3 %collective-permute-start.13 = (f32[16,128]{1,0:T(8,128)S(1)}, f32[16,128]{1,0:T(8,128)S(1)}, u32[]{:S(2)}, u32[]{:S(2)}) collective-permute-start(f32[16,128]{1,0:T(8,128)S(1)} %get-tuple-element.16), channel_id=1, source_target_pairs={{0,12},{1,13},{2,14},{3,15},{4,8},{5,9},{6,10},{7,11},{8,4},{9,5},... | collective-permute-start | bytes 24584 | tf_op jit(solution)/shard_map/ppermute | solution.py:15
  41.9 2.0 %collective-permute-start.14 = (f32[16,128]{1,0:T(8,128)S(1)}, f32[16,128]{1,0:T(8,128)S(1)}, u32[]{:S(2)}, u32[]{:S(2)}) collective-permute-start(f32[16,128]{1,0:T(8,128)S(1)} %get-tuple-element.18), channel_id=1, source_target_pairs={{0,8},{1,9},{2,10},{3,11},{4,12},{5,13},{6,14},{7,15},{8,0},{9,1},... | collective-permute-start | bytes 24584 | tf_op jit(solution)/shard_map/ppermute | solution.py:15
  43.9 0.1 collective-permute-start.15
  44.0 1.1 %collective-permute-done.13 = f32[16,128]{1,0:T(8,128)S(1)} collective-permute-done((f32[16,128]{1,0:T(8,128)S(1)}, f32[16,128]{1,0:T(8,128)S(1)}, u32[]{:S(2)}, u32[]{:S(2)}) %collective-permute-start.13) | collective-permute-done | bytes 8224 | tf_op jit(solution)/shard_map/ppermute | solution.py:15
  45.1 1.4 %collective-permute-done.14 = f32[16,128]{1,0:T(8,128)S(1)} collective-permute-done((f32[16,128]{1,0:T(8,128)S(1)}, f32[16,128]{1,0:T(8,128)S(1)}, u32[]{:S(2)}, u32[]{:S(2)}) %collective-permute-start.14) | collective-permute-done | bytes 8224 | tf_op jit(solution)/shard_map/ppermute | solution.py:15
  46.5 1.1 %collective-permute-done.15 = f32[16,128]{1,0:T(8,128)S(1)} collective-permute-done((f32[16,128]{1,0:T(8,128)S(1)}, f32[16,128]{1,0:T(8,128)S(1)}, u32[]{:S(2)}, u32[]{:S(2)}) %collective-permute-start.15) | collective-permute-done | bytes 8224 | tf_op jit(solution)/shard_map/ppermute | solution.py:15
  47.6 0.9 %collective-permute-start.17 = (f32[3,128]{1,0:T(4,128)S(1)}, f32[3,128]{1,0:T(4,128)S(1)}, u32[]{:S(2)}, u32[]{:S(2)}) collective-permute-start(f32[3,128]{1,0:T(4,128)S(1)} %get-tuple-element.22), channel_id=1, source_target_pairs={{0,2},{1,3},{2,0},{3,1},{4,6},{5,7},{6,4},{7,5},{8,10},{9,11},{10,... | collective-permute-start | bytes 4616 | tf_op jit(solution)/shard_map/ppermute | solution.py:15
  48.6 0.0 collective-permute-start.18
  48.6 1.3 %collective-permute-start.16 = (f32[3,128]{1,0:T(4,128)S(1)}, f32[3,128]{1,0:T(4,128)S(1)}, u32[]{:S(2)}, u32[]{:S(2)}) collective-permute-start(f32[3,128]{1,0:T(4,128)S(1)} %concatenate.16), channel_id=1, source_target_pairs={{0,3},{1,2},{2,1},{3,0},{4,7},{5,6},{6,5},{7,4},{8,11},{9,10},{10,... | collective-permute-start | bytes 4616 | tf_op jit(solution)/shard_map/ppermute | solution.py:15
  49.9 1.4 %collective-permute-done.17 = f32[3,128]{1,0:T(4,128)S(1)} collective-permute-done((f32[3,128]{1,0:T(4,128)S(1)}, f32[3,128]{1,0:T(4,128)S(1)}, u32[]{:S(2)}, u32[]{:S(2)}) %collective-permute-start.17) | collective-permute-done | bytes 1568 | tf_op jit(solution)/shard_map/ppermute | solution.py:15
  51.3 0.0 collective-permute-done.18
  51.3 0.3 collective-permute-done.16
  51.6 0.2 fusion.7
  51.8 0.6 %fusion.6 = f32[2,32]{1,0:T(2,128)} fusion(f32[2,32]{1,0:T(2,128)S(1)} %get-tuple-element.3, s32[2]{0:T(128)S(1)} %iota_add_fusion), kind=kLoop, calls=%fused_computation.29 | loop fusion | flops 192 | bytes 520 | tf_op jit(solution)/shard_map/div | solution.py:153
  52.4 0.5 broadcast_multiply_fusion
  (14 shorter events, 0.2 us)
Async XLA Ops:
  0.6 7.0 %collective-permute-start.8 = (bf16[128,256]{1,0:T(8,128)(2,1)}, bf16[128,256]{1,0:T(8,128)(2,1)S(1)}, u32[]{:S(2)}, u32[]{:S(2)}) collective-permute-start(bf16[128,256]{1,0:T(8,128)(2,1)} %refs_8_.1), channel_id=1, source_target_pairs={{0,4},{1,5},{2,6},{3,7},{4,0},{5,1},{6,2},{7,3},{8,12},{9,13},{10,... | collective-permute-start | bytes 196616 | tf_op jit(solution)/shard_map/ppermute | solution.py:15
  3.7 7.5 %collective-permute-start.9 = (bf16[128,256]{1,0:T(8,128)(2,1)}, bf16[128,256]{1,0:T(8,128)(2,1)S(1)}, u32[]{:S(2)}, u32[]{:S(2)}) collective-permute-start(bf16[128,256]{1,0:T(8,128)(2,1)} %refs_8_.1), channel_id=1, source_target_pairs={{0,8},{1,9},{2,10},{3,11},{4,12},{5,13},{6,14},{7,15},{8,0},{9,1},... | collective-permute-start | bytes 196616 | tf_op jit(solution)/shard_map/ppermute | solution.py:15
  6.3 6.3 %collective-permute-start.10 = (bf16[128,256]{1,0:T(8,128)(2,1)}, bf16[128,256]{1,0:T(8,128)(2,1)S(1)}, u32[]{:S(2)}, u32[]{:S(2)}) collective-permute-start(bf16[128,256]{1,0:T(8,128)(2,1)} %refs_8_.1), channel_id=1, source_target_pairs={{0,12},{1,13},{2,14},{3,15},{4,8},{5,9},{6,10},{7,11},{8,4},{9,5},... | collective-permute-start | bytes 196616 | tf_op jit(solution)/shard_map/ppermute | solution.py:15
  6.3 6.3 %copy-start = (bf16[128,256]{1,0:T(8,128)(2,1)S(1)}, bf16[128,256]{1,0:T(8,128)(2,1)}, u32[]{:S(2)}) copy-start(bf16[128,256]{1,0:T(8,128)(2,1)} %refs_8_.1) | copy-start | bytes 196612
  12.7 6.5 %collective-permute-start.11 = (bf16[4,128,256]{2,1,0:T(8,128)(2,1)S(1)}, bf16[4,128,256]{2,1,0:T(8,128)(2,1)S(1)}, u32[]{:S(2)}, u32[]{:S(2)}) collective-permute-start(bf16[4,128,256]{2,1,0:T(8,128)(2,1)S(1)} %get-tuple-element.15), channel_id=1, source_target_pairs={{0,2},{1,3},{2,0},{3,1},{4,6},{5,7},{6,4},{7,5},{8,10},{9,11},{10,... | collective-permute-start | bytes 786440 | tf_op jit(solution)/shard_map/ppermute | solution.py:15
  14.3 5.0 %collective-permute-start = (bf16[8,128,128]{1,2,0:T(8,128)(2,1)S(1)}, bf16[8,128,128]{1,2,0:T(8,128)(2,1)S(1)}, u32[]{:S(2)}, u32[]{:S(2)}) collective-permute-start(bf16[8,128,128]{1,2,0:T(8,128)(2,1)S(1)} %get-tuple-element.13), channel_id=1, source_target_pairs={{0,1},{1,0},{2,3},{3,2},{4,5},{5,4},{6,7},{7,6},{8,9},{9,8},{10,11... | collective-permute-start | bytes 786440 | tf_op jit(solution)/shard_map/ppermute | solution.py:15
  14.4 0.7 %copy-start.1 = (bf16[2]{0:T(256)(128)(2,1)S(1)}, bf16[2]{0:T(256)(128)(2,1)}, u32[]{:S(2)}) copy-start(bf16[2]{0:T(256)(128)(2,1)} %param.5) | copy-start | bytes 16
  19.2 17.3 %collective-permute-start.12 = (bf16[2,4,128,256]{3,2,1,0:T(8,128)(2,1)S(1)}, bf16[2,4,128,256]{3,2,1,0:T(8,128)(2,1)S(1)}, u32[]{:S(2)}, u32[]{:S(2)}) collective-permute-start(bf16[2,4,128,256]{3,2,1,0:T(8,128)(2,1)S(1)} %pad_maximum_fusion.1), channel_id=1, source_target_pairs={{0,1},{1,0},{2,3},{3,2},{4,5},{5,4},{6,7},{7,6},{8,9},{9,8},{10,11... | collective-permute-start | bytes 1572872 | tf_op jit(solution)/shard_map/ppermute | solution.py:15
  19.7 5.6 %collective-permute-start.1 = (bf16[256,128]{1,0:T(8,128)(2,1)S(1)}, bf16[256,128]{1,0:T(8,128)(2,1)S(1)}, u32[]{:S(2)}, u32[]{:S(2)}) collective-permute-start(bf16[256,128]{1,0:T(8,128)(2,1)S(1)} %get-tuple-element.10), channel_id=1, source_target_pairs={{0,2},{1,3},{2,0},{3,1},{4,6},{5,7},{6,4},{7,5},{8,10},{9,11},{10,... | collective-permute-start | bytes 196616 | tf_op jit(solution)/shard_map/ppermute | solution.py:15
  21.3 5.9 %collective-permute-start.2 = (bf16[256,128]{1,0:T(8,128)(2,1)S(1)}, bf16[256,128]{1,0:T(8,128)(2,1)S(1)}, u32[]{:S(2)}, u32[]{:S(2)}) collective-permute-start(bf16[256,128]{1,0:T(8,128)(2,1)S(1)} %get-tuple-element.9), channel_id=1, source_target_pairs={{0,4},{1,5},{2,6},{3,7},{4,0},{5,1},{6,2},{7,3},{8,12},{9,13},{10,... | collective-permute-start | bytes 196616 | tf_op jit(solution)/shard_map/ppermute | solution.py:15
  22.0 6.9 %collective-permute-start.3 = (bf16[256,128]{1,0:T(8,128)(2,1)S(1)}, bf16[256,128]{1,0:T(8,128)(2,1)S(1)}, u32[]{:S(2)}, u32[]{:S(2)}) collective-permute-start(bf16[256,128]{1,0:T(8,128)(2,1)S(1)} %get-tuple-element.8), channel_id=1, source_target_pairs={{0,6},{1,7},{2,4},{3,5},{4,2},{5,3},{6,0},{7,1},{8,14},{9,15},{10,... | collective-permute-start | bytes 196616 | tf_op jit(solution)/shard_map/ppermute | solution.py:15
  23.2 9.1 %collective-permute-start.4 = (bf16[256,128]{1,0:T(8,128)(2,1)S(1)}, bf16[256,128]{1,0:T(8,128)(2,1)S(1)}, u32[]{:S(2)}, u32[]{:S(2)}) collective-permute-start(bf16[256,128]{1,0:T(8,128)(2,1)S(1)} %get-tuple-element.7), channel_id=1, source_target_pairs={{0,8},{1,9},{2,10},{3,11},{4,12},{5,13},{6,14},{7,15},{8,0},{9,1},... | collective-permute-start | bytes 196616 | tf_op jit(solution)/shard_map/ppermute | solution.py:15
  25.3 11.2 %collective-permute-start.5 = (bf16[256,128]{1,0:T(8,128)(2,1)S(1)}, bf16[256,128]{1,0:T(8,128)(2,1)S(1)}, u32[]{:S(2)}, u32[]{:S(2)}) collective-permute-start(bf16[256,128]{1,0:T(8,128)(2,1)S(1)} %get-tuple-element.6), channel_id=1, source_target_pairs={{0,10},{1,11},{2,8},{3,9},{4,14},{5,15},{6,12},{7,13},{8,2},{9,3},... | collective-permute-start | bytes 196616 | tf_op jit(solution)/shard_map/ppermute | solution.py:15
  27.2 9.3 %collective-permute-start.6 = (bf16[256,128]{1,0:T(8,128)(2,1)S(1)}, bf16[256,128]{1,0:T(8,128)(2,1)S(1)}, u32[]{:S(2)}, u32[]{:S(2)}) collective-permute-start(bf16[256,128]{1,0:T(8,128)(2,1)S(1)} %get-tuple-element.5), channel_id=1, source_target_pairs={{0,12},{1,13},{2,14},{3,15},{4,8},{5,9},{6,10},{7,11},{8,4},{9,5},... | collective-permute-start | bytes 196616 | tf_op jit(solution)/shard_map/ppermute | solution.py:15
  28.9 7.6 %collective-permute-start.7 = (bf16[256,128]{1,0:T(8,128)(2,1)S(1)}, bf16[256,128]{1,0:T(8,128)(2,1)S(1)}, u32[]{:S(2)}, u32[]{:S(2)}) collective-permute-start(bf16[256,128]{1,0:T(8,128)(2,1)S(1)} %get-tuple-element.4), channel_id=1, source_target_pairs={{0,14},{1,15},{2,12},{3,13},{4,10},{5,11},{6,8},{7,9},{8,6},{9,7},... | collective-permute-start | bytes 196616 | tf_op jit(solution)/shard_map/ppermute | solution.py:15
  39.6 5.5 %collective-permute-start.13 = (f32[16,128]{1,0:T(8,128)S(1)}, f32[16,128]{1,0:T(8,128)S(1)}, u32[]{:S(2)}, u32[]{:S(2)}) collective-permute-start(f32[16,128]{1,0:T(8,128)S(1)} %get-tuple-element.16), channel_id=1, source_target_pairs={{0,12},{1,13},{2,14},{3,15},{4,8},{5,9},{6,10},{7,11},{8,4},{9,5},... | collective-permute-start | bytes 24584 | tf_op jit(solution)/shard_map/ppermute | solution.py:15
  41.9 4.5 %collective-permute-start.14 = (f32[16,128]{1,0:T(8,128)S(1)}, f32[16,128]{1,0:T(8,128)S(1)}, u32[]{:S(2)}, u32[]{:S(2)}) collective-permute-start(f32[16,128]{1,0:T(8,128)S(1)} %get-tuple-element.18), channel_id=1, source_target_pairs={{0,8},{1,9},{2,10},{3,11},{4,12},{5,13},{6,14},{7,15},{8,0},{9,1},... | collective-permute-start | bytes 24584 | tf_op jit(solution)/shard_map/ppermute | solution.py:15
  43.9 3.7 %collective-permute-start.15 = (f32[16,128]{1,0:T(8,128)S(1)}, f32[16,128]{1,0:T(8,128)S(1)}, u32[]{:S(2)}, u32[]{:S(2)}) collective-permute-start(f32[16,128]{1,0:T(8,128)S(1)} %get-tuple-element.17), channel_id=1, source_target_pairs={{0,4},{1,5},{2,6},{3,7},{4,0},{5,1},{6,2},{7,3},{8,12},{9,13},{10,... | collective-permute-start | bytes 24584 | tf_op jit(solution)/shard_map/ppermute | solution.py:15
  47.6 3.7 %collective-permute-start.17 = (f32[3,128]{1,0:T(4,128)S(1)}, f32[3,128]{1,0:T(4,128)S(1)}, u32[]{:S(2)}, u32[]{:S(2)}) collective-permute-start(f32[3,128]{1,0:T(4,128)S(1)} %get-tuple-element.22), channel_id=1, source_target_pairs={{0,2},{1,3},{2,0},{3,1},{4,6},{5,7},{6,4},{7,5},{8,10},{9,11},{10,... | collective-permute-start | bytes 4616 | tf_op jit(solution)/shard_map/ppermute | solution.py:15
  48.6 2.7 %collective-permute-start.18 = (f32[3,128]{1,0:T(4,128)S(1)}, f32[3,128]{1,0:T(4,128)S(1)}, u32[]{:S(2)}, u32[]{:S(2)}) collective-permute-start(f32[3,128]{1,0:T(4,128)S(1)} %get-tuple-element.23), channel_id=1, source_target_pairs={{0,1},{1,0},{2,3},{3,2},{4,5},{5,4},{6,7},{7,6},{8,9},{9,8},{10,11... | collective-permute-start | bytes 4616 | tf_op jit(solution)/shard_map/ppermute | solution.py:15
  48.6 3.0 %collective-permute-start.16 = (f32[3,128]{1,0:T(4,128)S(1)}, f32[3,128]{1,0:T(4,128)S(1)}, u32[]{:S(2)}, u32[]{:S(2)}) collective-permute-start(f32[3,128]{1,0:T(4,128)S(1)} %concatenate.16), channel_id=1, source_target_pairs={{0,3},{1,2},{2,1},{3,0},{4,7},{5,6},{6,5},{7,4},{8,11},{9,10},{10,... | collective-permute-start | bytes 4616 | tf_op jit(solution)/shard_map/ppermute | solution.py:15

commit v2 on v0

v2 whole, which is shorter than its diff:
```python
import functools

import jax
import jax.numpy as jnp
from jax import lax
from jax.experimental import pallas as pl
from jax.experimental.pallas import tpu as pltpu
from jax.sharding import PartitionSpec as P

LANES = 128


def swapped(value, distance):
    count = lax.axis_size("ex")
    return lax.ppermute(value, "ex", [(i, i ^ distance) for i in range(count)])


def dot_t(a, b):
    return lax.dot_general(a, b, (((1,), (1,)), ((), ())), preferred_element_type=jnp.float32)


def three_parts(value, axis):
    high = value.astype(jnp.bfloat16)
    rest = value - high.astype(jnp.float32)
    middle = rest.astype(jnp.bfloat16)
    low = (rest - middle.astype(jnp.float32)).astype(jnp.bfloat16)
    return jnp.concatenate([high, middle, low], axis=axis)


def global_example(slot, place, far, local_count):
    distance, within = slot // local_count, slot % local_count
    return (2 * jnp.bitwise_xor(place[0], distance) + jnp.bitwise_xor(place[1], far)) * local_count + within


def order_kernel(local_count, seq_length, place, weight, own_spread, far_spread, gather_ref, weight_ref):
    for far, ref in enumerate((own_spread, far_spread)):
        token = lax.broadcasted_iota(jnp.int32, ref.shape, 0)
        lane = lax.broadcasted_iota(jnp.int32, ref.shape, 1)
        ref[...] = (global_example(token // seq_length, place, far, local_count) == lane).astype(ref.dtype)
    own = 2 * local_count
    row = lax.broadcasted_iota(jnp.int32, gather_ref.shape, 0)
    slot = lax.broadcasted_iota(jnp.int32, gather_ref.shape, 1)
    example = global_example(slot // 8 * own + slot % 8, place, 0, local_count)
    gather_ref[...] = ((example == row) & (slot % 8 < own)).astype(gather_ref.dtype)
    lane = lax.broadcasted_iota(jnp.int32, weight_ref.shape, 1) - (2 * place[0] + place[1]) * local_count
    weights = jnp.zeros(weight_ref.shape, jnp.float32)
    for k in range(local_count):
        weights = jnp.where(lane == k, weight[k], weights)
    weight_ref[...] = weights


def pair_sums(seq_length, rows_x, rows_c, far_x, far_c, spread, gather, sums_ref):
    groups, held, columns = sums_ref.shape
    span = columns // groups
    own = span // seq_length
    sums_ref[...] = jnp.zeros_like(sums_ref)

    def block(i, j, scale=None):
        product = dot_t(rows_x[i], far_x[j]) * dot_t(rows_c[i], far_c[j])
        summed = jnp.sum(product.reshape(own, seq_length, span), axis=1)
        if scale is not None:
            summed = summed * scale
        if isinstance(j, int):
            sums_ref[i, :own, j * span : (j + 1) * span] = summed
        else:
            sums_ref[i, :own, pl.ds(pl.multiple_of(j * span, span), span)] = summed

    if groups <= 4:
        for i in range(groups):
            block(i, i, 0.5)
            for j in range(i + 1, groups):
                block(i, j)
    else:

        @pl.loop(0, groups)
        def _(i):
            block(i, i, 0.5)

            @pl.loop(i + 1, groups)
            def _(j):
                block(i, j)

    count = groups * held
    parts = jnp.dot(
        three_parts(sums_ref[...].reshape(count, columns), 0), spread[...], preferred_element_type=jnp.float32
    )
    by_lane = parts[:count] + (parts[count : 2 * count] + parts[2 * count :])
    parts = jnp.dot(gather[...], three_parts(by_lane, 1), preferred_element_type=jnp.float32)
    return parts[:, :LANES] + (parts[:, LANES : 2 * LANES] + parts[:, 2 * LANES :])


def own_kernel(seq_length, x_ref, c_ref, spread, gather, out_ref, sums_ref):
    out_ref[...] = pair_sums(seq_length, x_ref, c_ref, x_ref, c_ref, spread, gather, sums_ref)


def far_kernel(
    seq_length, local_count, x_ref, c_ref, far_x, far_c, spread, gather, weight_ref, own_ref, out_ref, sums_ref
):
    half = own_ref[...] + pair_sums(seq_length, x_ref, c_ref, far_x, far_c, spread, gather, sums_ref)
    gram = half + half.T
    devices = out_ref.shape[0]
    out_ref[...] = jnp.broadcast_to(weight_ref[...], out_ref.shape)
    out_ref[:, :local_count] = gram[: devices * local_count].reshape(devices, local_count, LANES)


def output_kernel(local_count, kernel_scale, norm_scale, place, sums_ref, kernel_ref, norms_ref):
    total = jnp.sum(sums_ref[...], axis=0)
    weights = total[local_count : local_count + 1]
    shape = (local_count, LANES)
    own = (2 * place[0] + place[1]) * local_count + lax.broadcasted_iota(jnp.int32, shape, 0)
    lane = lax.broadcasted_iota(jnp.int32, shape, 1)
    mine = jnp.sum(jnp.where(lane == own, weights, 0.0), axis=1, keepdims=True)
    grams = total[:local_count] * (mine * weights)
    kernel_ref[...] = (jnp.where(lane < own, grams, 0.0) / kernel_scale)[:, : kernel_ref.shape[1]]
    norms = jnp.where(lane == own, grams, 0.0) / norm_scale
    square = jnp.concatenate([norms, jnp.zeros((LANES - local_count, LANES), jnp.float32)]).T
    norms_ref[...] = jnp.sum(square, axis=0, keepdims=True)[:, :local_count]


def body(layer_input, cotangent, example_weight):
    devices = lax.axis_size("ex")
    me = lax.axis_index("ex")
    chips, planes = devices // 2, devices // 4
    chip, core = me // 2, me % 2
    local_count = example_weight.shape[0]
    tokens, width = layer_input.shape
    seq_length = tokens // local_count
    heads = cotangent.shape[1]
    window = width * heads
    chip_width = width // chips
    weight = example_weight.astype(jnp.float32)

    smem = pl.BlockSpec(memory_space=pltpu.SMEM)
    vmem = pl.BlockSpec(memory_space=pltpu.VMEM)
    params = pltpu.CompilerParams(vmem_limit_bytes=24 * 1024 * 1024)

    array = jax.ShapeDtypeStruct
    place = jnp.stack([chip, core]).astype(jnp.int32)
    shapes = [array((chips * tokens, LANES), jnp.bfloat16)] * 2
    shapes += [array((LANES, planes * 8), jnp.bfloat16), array((8, LANES), jnp.float32)]
    own_spread, far_spread, gather, weight_row = pl.pallas_call(
        functools.partial(order_kernel, local_count, seq_length),
        out_shape=shapes,
        in_specs=[smem] * 2,
        out_specs=[vmem] * len(shapes),
        compiler_params=params,
        name="order_kernel",
    )(place, weight)

    cot = {0: cotangent}
    for z in range(planes - 1, 0, -1):
        cot[z] = swapped(cotangent, 4 * z)
    def columns(distance):
        return lax.dynamic_slice_in_dim(layer_input, (chip ^ distance) * chip_width, chip_width, 1)

    over_y = swapped(jnp.stack([columns(2 * z + 1) for z in range(planes)]), 2)
    over_y, order = lax.optimization_barrier((over_y, (own_spread, far_spread, gather, weight_row)))
    own_spread, far_spread, gather, weight_row = order
    mine = {}
    for z in range(planes - 1, -1, -1):
        part = jnp.concatenate([columns(2 * z), over_y[z]])
        mine[z] = swapped(part, 4 * z) if z else part
    over_z = jnp.stack([cot[z] for z in range(planes)])
    over_zy = swapped(over_z, 2)
    own_c = jnp.stack([over_z, over_zy], axis=1).reshape(planes, 2 * tokens, heads)
    far_c = jnp.stack([swapped(over_z, 1), swapped(over_zy, 1)], axis=1).reshape(planes, 2 * tokens, heads)
    own_x = jnp.stack([mine[z] for z in range(planes)])
    far_x = swapped(own_x, 1)

    sums = [pltpu.VMEM((planes, 8, chips * tokens), jnp.float32)]
    own = pl.pallas_call(
        functools.partial(own_kernel, seq_length),
        out_shape=array((LANES, LANES), jnp.float32),
        in_specs=[vmem] * 4,
        out_specs=vmem,
        scratch_shapes=sums,
        compiler_params=params,
        name="own_kernel",
    )(own_x, own_c, own_spread, gather)
    partial = pl.pallas_call(
        functools.partial(far_kernel, seq_length, local_count),
        out_shape=array((devices, 8, LANES), jnp.float32),
        in_specs=[vmem] * 8,
        out_specs=vmem,
        scratch_shapes=sums,
        compiler_params=params,
        name="far_kernel",
    )(own_x, own_c, far_x, far_c, far_spread, gather, weight_row, own)

    received = lax.all_to_all(partial, "ex", split_axis=0, concat_axis=0, tiled=True)
    scales = (seq_length * window**0.5, float(seq_length * window))
    count = devices * local_count
    kernel, sq_norms = pl.pallas_call(
        functools.partial(output_kernel, local_count, *scales),
        out_shape=[array((local_count, count), jnp.float32), array((1, local_count), jnp.float32)],
        in_specs=[smem, vmem],
        out_specs=[vmem] * 2,
        compiler_params=params,
        name="output_kernel",
    )(place, received)
    return (kernel, sq_norms.reshape(local_count))


def solution(mesh):
    placed = (P(("grp", "ex"), None), P(("grp", "ex"), None), P("ex"))
    return jax.shard_map(
        body,
        mesh=mesh,
        in_specs=placed,
        out_specs=(P(("grp", "ex"), None), P(("grp", "ex"))),
        check_vma=False,
    )
```

time: 122 us -> 42.9 us (0.35)
  waiting for transfers between devices: 97.4 us -> 8.73 us
  blocking collectives: 0 us -> 12.1 us
  starting transfers between devices: 7.81 us -> 14.2 us
  local copies, waits for them, and re-layouts: 6.72 us -> 1.87 us
  Pallas kernels: 0 us -> 4.59 us
  matrix products: 3.97 us -> 0 us
  other arithmetic: 4.04 us -> 0.37 us
    ppermute x24 -> x11, waiting for transfers between devices: 93.3 us -> 8.73 us  [swapped(): return lax.ppermute(value, 'ex', [(i, i ^ distance) for i in range(count)])]
    all_to_all x0 -> x1, blocking collectives: none -> 12.1 us  [body(): lax.all_to_all(partial, 'ex', split_axis=0, concat_axis=0, tiled=True)]
    ppermute x24 -> x11, starting transfers between devices: 4.36 us -> 14.2 us  [swapped(): return lax.ppermute(value, 'ex', [(i, i ^ distance) for i in range(count)])]
    pallas_call x0 -> x4, Pallas kernels: none -> 4.59 us  [the longest x1 1.26 us: body(): pl.pallas_call(functools.partial(output_kernel, local_count, *scales), ou...]
    all_to_all x1 -> x0, waiting for transfers between devices: 4.13 us -> none  [body(): lax.all_to_all(slot_sums, 'ex', split_axis=0, concat_axis=0, tiled=True)]
    dot_general x18 -> x0, matrix products: 3.97 us -> none  [the longest x9 2.82 us: pair_block(): jnp.einsum('td,ud->tu', own_input, far_input, preferred_element_type=jnp....]
    all_to_all x1 -> x0, starting transfers between devices: 3.45 us -> none  [body(): lax.all_to_all(slot_sums, 'ex', split_axis=0, concat_axis=0, tiled=True)]
    reduce_sum x9 -> x0, other arithmetic: 1.51 us -> none  [pair_block(): summed = jnp.sum(products, axis=(1, 3))]
  transfers between devices with their start and end apart: 25 -> 11, of which waited for: 9 -> 5; matrix products, arithmetic and copies ran while one was open for 3% -> 1% of each run, Pallas kernels for 0% -> 5%
where the time goes in v2:
time: 42.9 us; the launch traced here: 42.7 us
  starting transfers between devices  14.2 us (33%)
  blocking collectives  12.1 us (28%)
  waiting for transfers between devices  8.73 us (20%)
  Pallas kernels  4.59 us (11%)
  local copies, waits for them, and re-layouts  1.87 us (4%)
  between operations  0.83 us (2%)
    ppermute x11, starting transfers between devices, swapped(): return lax.ppermute(value, 'ex', [(i, i ^ distance) for i in range(count)])  14.2 us
    all_to_all x1, blocking collectives, body(): lax.all_to_all(partial, 'ex', split_axis=0, concat_axis=0, tiled=True)  12.1 us
    ppermute x11, waiting for transfers between devices, swapped(): return lax.ppermute(value, 'ex', [(i, i ^ distance) for i in range(count)])  8.73 us
    pallas_call x1, Pallas kernels, body(): pl.pallas_call(functools.partial(output_kernel, local_count, *scales), ou...  1.26 us
    pallas_call x1, Pallas kernels, body(): pl.pallas_call(functools.partial(far_kernel, seq_length, local_count), ou...  1.24 us
    pallas_call x1, Pallas kernels, body(): pl.pallas_call(functools.partial(own_kernel, seq_length), out_shape=array...  1.18 us
    dynamic_slice x1, local copies, waits for them, and re-layouts, columns(): lax.dynamic_slice_in_dim(layer_input, (chip ^ distance) * chip_width, chi...  1.12 us
    pallas_call x1, Pallas kernels, body(): pl.pallas_call(functools.partial(order_kernel, local_count, seq_length),...  0.92 us
  transfers between devices with their start and end apart: 11, of which 5 were waited for; matrix products, arithmetic and copies ran while one was open for 1% of the time, Pallas kernels for 5%

profile of v2, /device:TPU:0, one launch (start us, length us, event | category | flops | bytes accessed | tf_op | source)
XLA Modules:
  0.0 42.7 jit_solution(9326431985597287862)
XLA Ops:
  0.7 1.1 %constant_dynamic-slice_fusion.3 = (bf16[128,256]{1,0:T(8,128)(2,1)S(1)}, bf16[128,256]{1,0:T(8,128)(2,1)S(1)}, bf16[1,128,256]{2,1,0:T(8,128)(2,1)S(1)}, bf16[1...) fusion(bf16[128,2048]{1,0:T(8,128)(2,1)} %param.3, ...), kind=kLoop, calls=%fused_computation.20 | loop fusion | bytes 1048608 | tf_op jit(solution)/shard_map/dynamic_slice | solution.py:154
  1.8 0.0 copy-start
  1.9 3.0 %collective-permute-start = (bf16[4,128,256]{2,1,0:T(8,128)(2,1)S(1)}, bf16[4,128,256]{2,1,0:T(8,128)(2,1)S(1)}, u32[]{:S(2)}, u32[]{:S(2)}) collective-permute-start(bf16[4,128,256]{2,1,0:T(8,128)(2,1)S(1)} %pad_maximum_fusion.3), channel_id=1, source_target_pairs={{0,2},{1,3},{2,0},{3,1},{4,6},{5,7},{6,4},{7,5},{8,10},{9,11},{10,... | collective-permute-start | bytes 786440 | tf_op jit(solution)/shard_map/ppermute | solution.py:15
  4.9 0.0 copy-done
  4.9 1.6 %collective-permute-start.4 = (bf16[128,256]{1,0:T(8,128)(2,1)S(1)}, bf16[128,256]{1,0:T(8,128)(2,1)S(1)}, u32[]{:S(2)}, u32[]{:S(2)}) collective-permute-start(bf16[128,256]{1,0:T(8,128)(2,1)S(1)} %copy-done), channel_id=1, source_target_pairs={{0,4},{1,5},{2,6},{3,7},{4,0},{5,1},{6,2},{7,3},{8,12},{9,13},{10,... | collective-permute-start | bytes 196616 | tf_op jit(solution)/shard_map/ppermute | solution.py:15
  6.5 2.5 %collective-permute-start.6 = (bf16[128,256]{1,0:T(8,128)(2,1)S(1)}, bf16[128,256]{1,0:T(8,128)(2,1)S(1)}, u32[]{:S(2)}, u32[]{:S(2)}) collective-permute-start(bf16[128,256]{1,0:T(8,128)(2,1)S(1)} %copy-done), channel_id=1, source_target_pairs={{0,12},{1,13},{2,14},{3,15},{4,8},{5,9},{6,10},{7,11},{8,4},{9,5},... | collective-permute-start | bytes 196616 | tf_op jit(solution)/shard_map/ppermute | solution.py:15
  9.0 0.1 collective-permute-start.5
  9.1 0.0 copy-start.1
  9.1 0.7 %copy-done.1 = bf16[2]{0:T(256)(128)(2,1)S(1)} copy-done((bf16[2]{0:T(256)(128)(2,1)S(1)}, bf16[2]{0:T(256)(128)(2,1)}, u32[]{:S(2)}) %copy-start.1) | copy-done | bytes 28
  9.7 0.1 pad_add_fusion.place
  9.8 0.9 %order_kernel.1 = (bf16[1024,128]{1,0:T(8,128)(2,1)S(1)}, bf16[1024,128]{1,0:T(8,128)(2,1)S(1)}, bf16[128,32]{1,0:T(8,128)(2,1)S(1)}, f32[8,128]{1,0:T(8,128)S(1)}) custom-call(s32[2]{0:T(128)S(1)} %pad_add_fusion.place, f32[2]{0:T(128)S(1)} %convert_element_type.3.weight), custom_call_target="tpu_custom_call" | custom-call | tf_op jit(solution)/shard_map/order_kernel/pallas_call | solution.py:141
  10.7 0.5 %collective-permute-done = bf16[4,128,256]{2,1,0:T(8,128)(2,1)S(1)} collective-permute-done((bf16[4,128,256]{2,1,0:T(8,128)(2,1)S(1)}, bf16[4,128,256]{2,1,0:T(8,128)(2,1)S(1)}, u32[]{:S(2)}, u32[]{:S(2)}) %collective-permute-start) | collective-permute-done | bytes 262176 | tf_op jit(solution)/shard_map/ppermute | solution.py:15
  11.2 1.9 %collective-permute-start.1 = (bf16[256,256]{1,0:T(8,128)(2,1)S(1)}, bf16[256,256]{1,0:T(8,128)(2,1)S(1)}, u32[]{:S(2)}, u32[]{:S(2)}) collective-permute-start(bf16[256,256]{1,0:T(8,128)(2,1)S(1)} %pad_maximum_fusion.5), channel_id=1, source_target_pairs={{0,4},{1,5},{2,6},{3,7},{4,0},{5,1},{6,2},{7,3},{8,12},{9,13},{10,... | collective-permute-start | bytes 393224 | tf_op jit(solution)/shard_map/ppermute | solution.py:15
  13.1 2.7 %collective-permute-start.2 = (bf16[256,256]{1,0:T(8,128)(2,1)S(1)}, bf16[256,256]{1,0:T(8,128)(2,1)S(1)}, u32[]{:S(2)}, u32[]{:S(2)}) collective-permute-start(bf16[256,256]{1,0:T(8,128)(2,1)S(1)} %pad_maximum_fusion.6), channel_id=1, source_target_pairs={{0,8},{1,9},{2,10},{3,11},{4,12},{5,13},{6,14},{7,15},{8,0},{9,1},... | collective-permute-start | bytes 393224 | tf_op jit(solution)/shard_map/ppermute | solution.py:15
  15.8 0.0 collective-permute-done.4
  15.8 0.1 collective-permute-start.3
  15.9 0.0 collective-permute-done.6
  15.9 0.0 collective-permute-done.5
  16.0 1.8 %collective-permute-start.7 = (bf16[4,128,256]{2,1,0:T(8,128)(2,1)S(1)}, bf16[4,128,256]{2,1,0:T(8,128)(2,1)S(1)}, u32[]{:S(2)}, u32[]{:S(2)}) collective-permute-start(bf16[4,128,256]{2,1,0:T(8,128)(2,1)S(1)} %get-tuple-element.33), channel_id=1, source_target_pairs={{0,2},{1,3},{2,0},{3,1},{4,6},{5,7},{6,4},{7,5},{8,10},{9,11},{10,... | collective-permute-start | bytes 786440 | tf_op jit(solution)/shard_map/ppermute | solution.py:15
  17.7 1.6 %collective-permute-done.1 = bf16[256,256]{1,0:T(8,128)(2,1)S(1)} collective-permute-done((bf16[256,256]{1,0:T(8,128)(2,1)S(1)}, bf16[256,256]{1,0:T(8,128)(2,1)S(1)}, u32[]{:S(2)}, u32[]{:S(2)}) %collective-permute-start.1) | collective-permute-done | bytes 131104 | tf_op jit(solution)/shard_map/ppermute | solution.py:15
  19.3 5.9 %collective-permute-done.2 = bf16[256,256]{1,0:T(8,128)(2,1)S(1)} collective-permute-done((bf16[256,256]{1,0:T(8,128)(2,1)S(1)}, bf16[256,256]{1,0:T(8,128)(2,1)S(1)}, u32[]{:S(2)}, u32[]{:S(2)}) %collective-permute-start.2) | collective-permute-done | bytes 131104 | tf_op jit(solution)/shard_map/ppermute | solution.py:15
  25.2 0.0 collective-permute-done.3
  25.2 0.1 pad_maximum_fusion.x_ref
  25.3 0.1 collective-permute-start.8
  25.4 0.5 %collective-permute-start.9 = (bf16[4,128,256]{2,1,0:T(8,128)(2,1)S(1)}, bf16[4,128,256]{2,1,0:T(8,128)(2,1)S(1)}, u32[]{:S(2)}, u32[]{:S(2)}) collective-permute-start(bf16[4,128,256]{2,1,0:T(8,128)(2,1)S(1)} %get-tuple-element.33), channel_id=1, source_target_pairs={{0,1},{1,0},{2,3},{3,2},{4,5},{5,4},{6,7},{7,6},{8,9},{9,8},{10,11... | collective-permute-start | bytes 786440 | tf_op jit(solution)/shard_map/ppermute | solution.py:15
  25.8 0.0 collective-permute-done.7
  25.9 0.1 collective-permute-start.10
  25.9 0.1 pad_maximum_fusion.1
  26.0 1.2 %own_kernel.1.own_ref = f32[128,128]{1,0:T(8,128)S(1)} custom-call(bf16[4,256,256]{2,1,0:T(8,128)(2,1)S(1)} %pad_maximum_fusion.x_ref, bf16[4,256,256]{2,1,0:T(8,128)(2,1)S(1)} %bitcast.35, bf16[1024,128]{1,0:T(8,128)(2,1)S(1)} %get-tuple-element.21.spread, bf16[128,32]{1,0:T(8,128)(2,1)S(1)} %get-tuple-element.19.gather), custom_call_target="tpu_custom_call" | custom-call | tf_op jit(solution)/shard_map/own_kernel/pallas_call | solution.py:171
  27.2 0.4 collective-permute-done.9
  27.6 0.4 collective-permute-done.10
  28.0 0.1 pad_maximum_fusion.2
  28.1 0.0 collective-permute-done.8.far_x
  28.1 1.2 %far_kernel.1 = f32[16,8,128]{2,1,0:T(8,128)S(1)} custom-call(bf16[4,256,256]{2,1,0:T(8,128)(2,1)S(1)} %pad_maximum_fusion.x_ref, bf16[4,256,256]{2,1,0:T(8,128)(2,1)S(1)} %bitcast.36, bf16[4,256,256]{2,1,0:T(8,128)(2,1)S(1)} %collective-permute-done.8.far_x, bf16[4,256,256]{2,1,0:T(8,128)(2,1)S(1)} %bitcast.37, ...), custom_call_target="tpu_custom_call" | custom-call | tf_op jit(solution)/shard_map/far_kernel/pallas_call | solution.py:180
  29.3 12.1 %all_to_all.5.sums_ref = f32[16,8,128]{2,1,0:T(8,128)S(1)} all-to-all(f32[16,8,128]{2,1,0:T(8,128)S(1)} %far_kernel.1), channel_id=1, replica_groups=mesh['grp'=2,'ex'=16] {'ex'}, dimensions={0} | all-to-all | bytes 131072 | tf_op jit(solution)/shard_map/all_to_all | solution.py:190
  41.4 1.3 %output_kernel.1 = (f32[2,32]{1,0:T(2,128)}, f32[1,2]{1,0:T(1,128)}) custom-call(s32[2]{0:T(128)S(1)} %pad_add_fusion.place, f32[16,8,128]{2,1,0:T(8,128)S(1)} %all_to_all.5.sums_ref), custom_call_target="tpu_custom_call" | custom-call | tf_op jit(solution)/shard_map/output_kernel/pallas_call | solution.py:193
  (10 shorter events, 0.2 us)
Async XLA Ops:
  1.8 3.1 %copy-start = (bf16[128,256]{1,0:T(8,128)(2,1)S(1)}, bf16[128,256]{1,0:T(8,128)(2,1)}, u32[]{:S(2)}) copy-start(bf16[128,256]{1,0:T(8,128)(2,1)} %param.4) | copy-start | bytes 196612
  1.9 9.3 %collective-permute-start = (bf16[4,128,256]{2,1,0:T(8,128)(2,1)S(1)}, bf16[4,128,256]{2,1,0:T(8,128)(2,1)S(1)}, u32[]{:S(2)}, u32[]{:S(2)}) collective-permute-start(bf16[4,128,256]{2,1,0:T(8,128)(2,1)S(1)} %pad_maximum_fusion.3), channel_id=1, source_target_pairs={{0,2},{1,3},{2,0},{3,1},{4,6},{5,7},{6,4},{7,5},{8,10},{9,11},{10,... | collective-permute-start | bytes 786440 | tf_op jit(solution)/shard_map/ppermute | solution.py:15
  4.9 10.9 %collective-permute-start.4 = (bf16[128,256]{1,0:T(8,128)(2,1)S(1)}, bf16[128,256]{1,0:T(8,128)(2,1)S(1)}, u32[]{:S(2)}, u32[]{:S(2)}) collective-permute-start(bf16[128,256]{1,0:T(8,128)(2,1)S(1)} %copy-done), channel_id=1, source_target_pairs={{0,4},{1,5},{2,6},{3,7},{4,0},{5,1},{6,2},{7,3},{8,12},{9,13},{10,... | collective-permute-start | bytes 196616 | tf_op jit(solution)/shard_map/ppermute | solution.py:15
  6.5 9.4 %collective-permute-start.6 = (bf16[128,256]{1,0:T(8,128)(2,1)S(1)}, bf16[128,256]{1,0:T(8,128)(2,1)S(1)}, u32[]{:S(2)}, u32[]{:S(2)}) collective-permute-start(bf16[128,256]{1,0:T(8,128)(2,1)S(1)} %copy-done), channel_id=1, source_target_pairs={{0,12},{1,13},{2,14},{3,15},{4,8},{5,9},{6,10},{7,11},{8,4},{9,5},... | collective-permute-start | bytes 196616 | tf_op jit(solution)/shard_map/ppermute | solution.py:15
  9.0 6.9 %collective-permute-start.5 = (bf16[128,256]{1,0:T(8,128)(2,1)S(1)}, bf16[128,256]{1,0:T(8,128)(2,1)S(1)}, u32[]{:S(2)}, u32[]{:S(2)}) collective-permute-start(bf16[128,256]{1,0:T(8,128)(2,1)S(1)} %copy-done), channel_id=1, source_target_pairs={{0,8},{1,9},{2,10},{3,11},{4,12},{5,13},{6,14},{7,15},{8,0},{9,1},... | collective-permute-start | bytes 196616 | tf_op jit(solution)/shard_map/ppermute | solution.py:15
  9.1 0.7 %copy-start.1 = (bf16[2]{0:T(256)(128)(2,1)S(1)}, bf16[2]{0:T(256)(128)(2,1)}, u32[]{:S(2)}) copy-start(bf16[2]{0:T(256)(128)(2,1)} %param.5) | copy-start | bytes 16
  11.2 8.1 %collective-permute-start.1 = (bf16[256,256]{1,0:T(8,128)(2,1)S(1)}, bf16[256,256]{1,0:T(8,128)(2,1)S(1)}, u32[]{:S(2)}, u32[]{:S(2)}) collective-permute-start(bf16[256,256]{1,0:T(8,128)(2,1)S(1)} %pad_maximum_fusion.5), channel_id=1, source_target_pairs={{0,4},{1,5},{2,6},{3,7},{4,0},{5,1},{6,2},{7,3},{8,12},{9,13},{10,... | collective-permute-start | bytes 393224 | tf_op jit(solution)/shard_map/ppermute | solution.py:15
  13.1 12.1 %collective-permute-start.2 = (bf16[256,256]{1,0:T(8,128)(2,1)S(1)}, bf16[256,256]{1,0:T(8,128)(2,1)S(1)}, u32[]{:S(2)}, u32[]{:S(2)}) collective-permute-start(bf16[256,256]{1,0:T(8,128)(2,1)S(1)} %pad_maximum_fusion.6), channel_id=1, source_target_pairs={{0,8},{1,9},{2,10},{3,11},{4,12},{5,13},{6,14},{7,15},{8,0},{9,1},... | collective-permute-start | bytes 393224 | tf_op jit(solution)/shard_map/ppermute | solution.py:15
  15.8 9.4 %collective-permute-start.3 = (bf16[256,256]{1,0:T(8,128)(2,1)S(1)}, bf16[256,256]{1,0:T(8,128)(2,1)S(1)}, u32[]{:S(2)}, u32[]{:S(2)}) collective-permute-start(bf16[256,256]{1,0:T(8,128)(2,1)S(1)} %pad_maximum_fusion.7), channel_id=1, source_target_pairs={{0,12},{1,13},{2,14},{3,15},{4,8},{5,9},{6,10},{7,11},{8,4},{9,5},... | collective-permute-start | bytes 393224 | tf_op jit(solution)/shard_map/ppermute | solution.py:15
  16.0 9.9 %collective-permute-start.7 = (bf16[4,128,256]{2,1,0:T(8,128)(2,1)S(1)}, bf16[4,128,256]{2,1,0:T(8,128)(2,1)S(1)}, u32[]{:S(2)}, u32[]{:S(2)}) collective-permute-start(bf16[4,128,256]{2,1,0:T(8,128)(2,1)S(1)} %get-tuple-element.33), channel_id=1, source_target_pairs={{0,2},{1,3},{2,0},{3,1},{4,6},{5,7},{6,4},{7,5},{8,10},{9,11},{10,... | collective-permute-start | bytes 786440 | tf_op jit(solution)/shard_map/ppermute | solution.py:15
  25.3 2.8 %collective-permute-start.8 = (bf16[4,256,256]{2,1,0:T(8,128)(2,1)S(1)}, bf16[4,256,256]{2,1,0:T(8,128)(2,1)S(1)}, u32[]{:S(2)}, u32[]{:S(2)}) collective-permute-start(bf16[4,256,256]{2,1,0:T(8,128)(2,1)S(1)} %pad_maximum_fusion.x_ref), channel_id=1, source_target_pairs={{0,1},{1,0},{2,3},{3,2},{4,5},{5,4},{6,7},{7,6},{8,9},{9,8},{10,11... | collective-permute-start | bytes 1572872 | tf_op jit(solution)/shard_map/ppermute | solution.py:15
  25.4 2.3 %collective-permute-start.9 = (bf16[4,128,256]{2,1,0:T(8,128)(2,1)S(1)}, bf16[4,128,256]{2,1,0:T(8,128)(2,1)S(1)}, u32[]{:S(2)}, u32[]{:S(2)}) collective-permute-start(bf16[4,128,256]{2,1,0:T(8,128)(2,1)S(1)} %get-tuple-element.33), channel_id=1, source_target_pairs={{0,1},{1,0},{2,3},{3,2},{4,5},{5,4},{6,7},{7,6},{8,9},{9,8},{10,11... | collective-permute-start | bytes 786440 | tf_op jit(solution)/shard_map/ppermute | solution.py:15
  25.9 2.1 %collective-permute-start.10 = (bf16[4,128,256]{2,1,0:T(8,128)(2,1)S(1)}, bf16[4,128,256]{2,1,0:T(8,128)(2,1)S(1)}, u32[]{:S(2)}, u32[]{:S(2)}) collective-permute-start(bf16[4,128,256]{2,1,0:T(8,128)(2,1)S(1)} %collective-permute-done.7), channel_id=1, source_target_pairs={{0,1},{1,0},{2,3},{3,2},{4,5},{5,4},{6,7},{7,6},{8,9},{9,8},{10,11... | collective-permute-start | bytes 786440 | tf_op jit(solution)/shard_map/ppermute | solution.py:15

commit v3 on v2

--- a/solution.py
+++ b/solution.py
@@ -33,10 +33,12 @@
 
 
 def order_kernel(local_count, seq_length, place, weight, own_spread, far_spread, gather_ref, weight_ref):
+    examples = own_spread.shape[0] // seq_length
+    lane = lax.broadcasted_iota(jnp.int32, (seq_length, LANES), 1)
     for far, ref in enumerate((own_spread, far_spread)):
-        token = lax.broadcasted_iota(jnp.int32, ref.shape, 0)
-        lane = lax.broadcasted_iota(jnp.int32, ref.shape, 1)
-        ref[...] = (global_example(token // seq_length, place, far, local_count) == lane).astype(ref.dtype)
+        for slot in range(examples):
+            example = global_example(slot, place, far, local_count)
+            ref[slot * seq_length : (slot + 1) * seq_length] = (lane == example).astype(ref.dtype)
     own = 2 * local_count
     row = lax.broadcasted_iota(jnp.int32, gather_ref.shape, 0)
     slot = lax.broadcasted_iota(jnp.int32, gather_ref.shape, 1)
@@ -99,7 +101,7 @@
     half = own_ref[...] + pair_sums(seq_length, x_ref, c_ref, far_x, far_c, spread, gather, sums_ref)
     gram = half + half.T
     devices = out_ref.shape[0]
-    out_ref[...] = jnp.broadcast_to(weight_ref[...], out_ref.shape)
+    out_ref[...] = jnp.broadcast_to(weight_ref[: out_ref.shape[1]], out_ref.shape)
     out_ref[:, :local_count] = gram[: devices * local_count].reshape(devices, local_count, LANES)
 
 
@@ -107,14 +109,15 @@
     total = jnp.sum(sums_ref[...], axis=0)
     weights = total[local_count : local_count + 1]
     shape = (local_count, LANES)
-    own = (2 * place[0] + place[1]) * local_count + lax.broadcasted_iota(jnp.int32, shape, 0)
+    first = (2 * place[0] + place[1]) * local_count
+    own = first + lax.broadcasted_iota(jnp.int32, shape, 0)
     lane = lax.broadcasted_iota(jnp.int32, shape, 1)
     mine = jnp.sum(jnp.where(lane == own, weights, 0.0), axis=1, keepdims=True)
     grams = total[:local_count] * (mine * weights)
     kernel_ref[...] = (jnp.where(lane < own, grams, 0.0) / kernel_scale)[:, : kernel_ref.shape[1]]
-    norms = jnp.where(lane == own, grams, 0.0) / norm_scale
-    square = jnp.concatenate([norms, jnp.zeros((LANES - local_count, LANES), jnp.float32)]).T
-    norms_ref[...] = jnp.sum(square, axis=0, keepdims=True)[:, :local_count]
+    norms = jnp.sum(jnp.where(lane == own, grams, 0.0), axis=0, keepdims=True) / norm_scale
+    norms = jnp.broadcast_to(norms, (8, LANES))
+    norms_ref[...] = pltpu.roll(norms, LANES - first, 1)[:1, :local_count]
 
 
 def body(layer_input, cotangent, example_weight):
@@ -153,12 +156,16 @@
     def columns(distance):
         return lax.dynamic_slice_in_dim(layer_input, (chip ^ distance) * chip_width, chip_width, 1)
 
-    over_y = swapped(jnp.stack([columns(2 * z + 1) for z in range(planes)]), 2)
-    over_y, order = lax.optimization_barrier((over_y, (own_spread, far_spread, gather, weight_row)))
+    moved = swapped(jnp.stack([columns(2 * z + 1) for z in range(1, planes)]), 2)
+    moved, order = lax.optimization_barrier((moved, (own_spread, far_spread, gather, weight_row)))
     own_spread, far_spread, gather, weight_row = order
+    over_y = {z: moved[z - 1] for z in range(1, planes)}
+    over_y[0] = swapped(columns(1), 2)
     mine = {}
-    for z in range(planes - 1, -1, -1):
+    for z in [z for z in range(2, planes)] + [1, 0]:
         part = jnp.concatenate([columns(2 * z), over_y[z]])
+        if z == 1 and planes > 2:
+            part, cot[planes - 1] = lax.optimization_barrier((part, cot[planes - 1]))
         mine[z] = swapped(part, 4 * z) if z else part
     over_z = jnp.stack([cot[z] for z in range(planes)])
     over_zy = swapped(over_z, 2)
@@ -179,7 +186,7 @@
     )(own_x, own_c, own_spread, gather)
     partial = pl.pallas_call(
         functools.partial(far_kernel, seq_length, local_count),
-        out_shape=array((devices, 8, LANES), jnp.float32),
+        out_shape=array((devices, 4, LANES), jnp.float32),
         in_specs=[vmem] * 8,
         out_specs=vmem,
         scratch_shapes=sums,

time: 42.9 us -> 41.2 us (0.960)
  waiting for transfers between devices: 8.73 us -> 7.54 us
    ppermute x11 -> x12, waiting for transfers between devices: 8.73 us -> 7.54 us  [swapped(): return lax.ppermute(value, 'ex', [(i, i ^ distance) for i in range(count)])]
    ppermute x11 -> x12, starting transfers between devices: 14.2 us -> 14.2 us  [swapped(): return lax.ppermute(value, 'ex', [(i, i ^ distance) for i in range(count)])]
  transfers between devices with their start and end apart: 11 -> 12, of which waited for: 5 -> 4; matrix products, arithmetic and copies ran while one was open for 1% -> 1% of each run, Pallas kernels for 5% -> 4%
where the time goes in v3:
time: 41.2 us; the launch traced here: 41 us
  starting transfers between devices  14.2 us (34%)
  blocking collectives  12 us (29%)
  waiting for transfers between devices  7.54 us (18%)
  Pallas kernels  4.24 us (10%)
  local copies, waits for them, and re-layouts  1.87 us (5%)
  between operations  0.83 us (2%)
    ppermute x12, starting transfers between devices, swapped(): return lax.ppermute(value, 'ex', [(i, i ^ distance) for i in range(count)])  14.2 us
    all_to_all x1, blocking collectives, body(): lax.all_to_all(partial, 'ex', split_axis=0, concat_axis=0, tiled=True)  12 us
    ppermute x12, waiting for transfers between devices, swapped(): return lax.ppermute(value, 'ex', [(i, i ^ distance) for i in range(count)])  7.54 us
    pallas_call x1, Pallas kernels, body(): pl.pallas_call(functools.partial(far_kernel, seq_length, local_count), ou...  1.24 us
    pallas_call x1, Pallas kernels, body(): pl.pallas_call(functools.partial(output_kernel, local_count, *scales), ou...  1.22 us
    pallas_call x1, Pallas kernels, body(): pl.pallas_call(functools.partial(own_kernel, seq_length), out_shape=array...  1.18 us
    dynamic_slice x1, local copies, waits for them, and re-layouts, columns(): lax.dynamic_slice_in_dim(layer_input, (chip ^ distance) * chip_width, chi...  1.12 us
  transfers between devices with their start and end apart: 12, of which 4 were waited for; matrix products, arithmetic and copies ran while one was open for 1% of the time, Pallas kernels for 4%

profile of v3, /device:TPU:0, one launch (start us, length us, event | category | flops | bytes accessed | tf_op | source)
XLA Modules:
  0.0 41.0 jit_solution(14088859254857248715)
XLA Ops:
  0.7 1.1 %constant_dynamic-slice_fusion.4 = (bf16[128,256]{1,0:T(8,128)(2,1)S(1)}, bf16[1,128,256]{2,1,0:T(8,128)(2,1)S(1)}, bf16[1,128,256]{2,1,0:T(8,128)(2,1)S(1)}, bf...) fusion(bf16[128,2048]{1,0:T(8,128)(2,1)} %param.3, ...), kind=kLoop, calls=%fused_computation.19 | loop fusion | bytes 1048608 | tf_op jit(solution)/shard_map/dynamic_slice | solution.py:157
  1.8 0.0 copy-start
  1.9 3.0 %collective-permute-start.1 = (bf16[3,128,256]{2,1,0:T(8,128)(2,1)S(1)}, bf16[3,128,256]{2,1,0:T(8,128)(2,1)S(1)}, u32[]{:S(2)}, u32[]{:S(2)}) collective-permute-start(bf16[3,128,256]{2,1,0:T(8,128)(2,1)S(1)} %pad_maximum_fusion.4), channel_id=1, source_target_pairs={{0,2},{1,3},{2,0},{3,1},{4,6},{5,7},{6,4},{7,5},{8,10},{9,11},{10,... | collective-permute-start | bytes 589832 | tf_op jit(solution)/shard_map/ppermute | solution.py:15
  4.9 0.0 copy-done
  4.9 3.6 %collective-permute-start.2 = (bf16[128,256]{1,0:T(8,128)(2,1)S(1)}, bf16[128,256]{1,0:T(8,128)(2,1)S(1)}, u32[]{:S(2)}, u32[]{:S(2)}) collective-permute-start(bf16[128,256]{1,0:T(8,128)(2,1)S(1)} %copy-done), channel_id=1, source_target_pairs={{0,12},{1,13},{2,14},{3,15},{4,8},{5,9},{6,10},{7,11},{8,4},{9,5},... | collective-permute-start | bytes 196616 | tf_op jit(solution)/shard_map/ppermute | solution.py:15
  8.5 0.0 collective-permute-start.7
  8.5 0.8 %collective-permute-start.6 = (bf16[128,256]{1,0:T(8,128)(2,1)S(1)}, bf16[128,256]{1,0:T(8,128)(2,1)S(1)}, u32[]{:S(2)}, u32[]{:S(2)}) collective-permute-start(bf16[128,256]{1,0:T(8,128)(2,1)S(1)} %copy-done), channel_id=1, source_target_pairs={{0,4},{1,5},{2,6},{3,7},{4,0},{5,1},{6,2},{7,3},{8,12},{9,13},{10,... | collective-permute-start | bytes 196616 | tf_op jit(solution)/shard_map/ppermute | solution.py:15
  9.3 0.7 %collective-permute-start = (bf16[128,256]{1,0:T(8,128)(2,1)S(1)}, bf16[128,256]{1,0:T(8,128)(2,1)S(1)}, u32[]{:S(2)}, u32[]{:S(2)}) collective-permute-start(bf16[128,256]{1,0:T(8,128)(2,1)S(1)} %get-tuple-element.33), channel_id=1, source_target_pairs={{0,2},{1,3},{2,0},{3,1},{4,6},{5,7},{6,4},{7,5},{8,10},{9,11},{10,... | collective-permute-start | bytes 196616 | tf_op jit(solution)/shard_map/ppermute | solution.py:15
  10.0 0.0 copy-start.1
  10.0 0.7 %copy-done.1 = bf16[2]{0:T(256)(128)(2,1)S(1)} copy-done((bf16[2]{0:T(256)(128)(2,1)S(1)}, bf16[2]{0:T(256)(128)(2,1)}, u32[]{:S(2)}) %copy-start.1) | copy-done | bytes 28
  10.7 0.1 pad_add_fusion.place
  10.7 0.6 %order_kernel.1 = (bf16[1024,128]{1,0:T(8,128)(2,1)S(1)}, bf16[1024,128]{1,0:T(8,128)(2,1)S(1)}, bf16[128,32]{1,0:T(8,128)(2,1)S(1)}, f32[8,128]{1,0:T(8,128)S(1)}) custom-call(s32[2]{0:T(128)S(1)} %pad_add_fusion.place, f32[2]{0:T(128)S(1)} %convert_element_type.3.weight), custom_call_target="tpu_custom_call" | custom-call | tf_op jit(solution)/shard_map/order_kernel/pallas_call | solution.py:144
  11.3 0.0 collective-permute-done.1
  11.4 0.4 collective-permute-done.2
  11.8 2.2 %collective-permute-start.4 = (bf16[256,256]{1,0:T(8,128)(2,1)S(1)}, bf16[256,256]{1,0:T(8,128)(2,1)S(1)}, u32[]{:S(2)}, u32[]{:S(2)}) collective-permute-start(bf16[256,256]{1,0:T(8,128)(2,1)S(1)} %pad_maximum_fusion.6), channel_id=1, source_target_pairs={{0,8},{1,9},{2,10},{3,11},{4,12},{5,13},{6,14},{7,15},{8,0},{9,1},... | collective-permute-start | bytes 393224 | tf_op jit(solution)/shard_map/ppermute | solution.py:15
  14.0 1.6 %collective-permute-start.5 = (bf16[256,256]{1,0:T(8,128)(2,1)S(1)}, bf16[256,256]{1,0:T(8,128)(2,1)S(1)}, u32[]{:S(2)}, u32[]{:S(2)}) collective-permute-start(bf16[256,256]{1,0:T(8,128)(2,1)S(1)} %pad_maximum_fusion.7), channel_id=1, source_target_pairs={{0,12},{1,13},{2,14},{3,15},{4,8},{5,9},{6,10},{7,11},{8,4},{9,5},... | collective-permute-start | bytes 393224 | tf_op jit(solution)/shard_map/ppermute | solution.py:15
  15.6 0.0 collective-permute-done
  15.6 0.6 %collective-permute-start.3 = (bf16[256,256]{1,0:T(8,128)(2,1)S(1)}, bf16[256,256]{1,0:T(8,128)(2,1)S(1)}, u32[]{:S(2)}, u32[]{:S(2)}) collective-permute-start(bf16[256,256]{1,0:T(8,128)(2,1)S(1)} %pad_maximum_fusion.5), channel_id=1, source_target_pairs={{0,4},{1,5},{2,6},{3,7},{4,0},{5,1},{6,2},{7,3},{8,12},{9,13},{10,... | collective-permute-start | bytes 393224 | tf_op jit(solution)/shard_map/ppermute | solution.py:15
  16.2 0.0 collective-permute-done.7
  16.2 0.0 collective-permute-done.6
  16.3 1.0 %collective-permute-start.8 = (bf16[4,128,256]{2,1,0:T(8,128)(2,1)S(1)}, bf16[4,128,256]{2,1,0:T(8,128)(2,1)S(1)}, u32[]{:S(2)}, u32[]{:S(2)}) collective-permute-start(bf16[4,128,256]{2,1,0:T(8,128)(2,1)S(1)} %get-tuple-element.37), channel_id=1, source_target_pairs={{0,2},{1,3},{2,0},{3,1},{4,6},{5,7},{6,4},{7,5},{8,10},{9,11},{10,... | collective-permute-start | bytes 786440 | tf_op jit(solution)/shard_map/ppermute | solution.py:15
  17.3 6.4 %collective-permute-done.4 = bf16[256,256]{1,0:T(8,128)(2,1)S(1)} collective-permute-done((bf16[256,256]{1,0:T(8,128)(2,1)S(1)}, bf16[256,256]{1,0:T(8,128)(2,1)S(1)}, u32[]{:S(2)}, u32[]{:S(2)}) %collective-permute-start.4) | collective-permute-done | bytes 131104 | tf_op jit(solution)/shard_map/ppermute | solution.py:15
  23.6 0.0 collective-permute-done.5
  23.7 0.0 collective-permute-done.3
  23.7 0.1 pad_maximum_fusion.x_ref
  23.7 0.1 collective-permute-start.9
  23.8 0.5 %collective-permute-start.10 = (bf16[4,128,256]{2,1,0:T(8,128)(2,1)S(1)}, bf16[4,128,256]{2,1,0:T(8,128)(2,1)S(1)}, u32[]{:S(2)}, u32[]{:S(2)}) collective-permute-start(bf16[4,128,256]{2,1,0:T(8,128)(2,1)S(1)} %get-tuple-element.37), channel_id=1, source_target_pairs={{0,1},{1,0},{2,3},{3,2},{4,5},{5,4},{6,7},{7,6},{8,9},{9,8},{10,11... | collective-permute-start | bytes 786440 | tf_op jit(solution)/shard_map/ppermute | solution.py:15
  24.3 0.0 collective-permute-done.8
  24.3 0.1 collective-permute-start.11
  24.4 0.1 pad_maximum_fusion.1
  24.5 1.2 %own_kernel.1.own_ref = f32[128,128]{1,0:T(8,128)S(1)} custom-call(bf16[4,256,256]{2,1,0:T(8,128)(2,1)S(1)} %pad_maximum_fusion.x_ref, bf16[4,256,256]{2,1,0:T(8,128)(2,1)S(1)} %bitcast.31, bf16[1024,128]{1,0:T(8,128)(2,1)S(1)} %get-tuple-element.25.spread, bf16[128,32]{1,0:T(8,128)(2,1)S(1)} %get-tuple-element.23.gather), custom_call_target="tpu_custom_call" | custom-call | tf_op jit(solution)/shard_map/own_kernel/pallas_call | solution.py:178
  25.7 0.4 collective-permute-done.10
  26.1 0.4 collective-permute-done.11
  26.5 0.1 pad_maximum_fusion.2
  26.6 0.0 collective-permute-done.9.far_x
  26.6 1.2 %far_kernel.1 = f32[16,4,128]{2,1,0:T(4,128)S(1)} custom-call(bf16[4,256,256]{2,1,0:T(8,128)(2,1)S(1)} %pad_maximum_fusion.x_ref, bf16[4,256,256]{2,1,0:T(8,128)(2,1)S(1)} %bitcast.32, bf16[4,256,256]{2,1,0:T(8,128)(2,1)S(1)} %collective-permute-done.9.far_x, bf16[4,256,256]{2,1,0:T(8,128)(2,1)S(1)} %bitcast.33, ...), custom_call_target="tpu_custom_call" | custom-call | tf_op jit(solution)/shard_map/far_kernel/pallas_call | solution.py:187
  27.8 12.0 %all_to_all.5.sums_ref = f32[16,4,128]{2,1,0:T(4,128)S(1)} all-to-all(f32[16,4,128]{2,1,0:T(4,128)S(1)} %far_kernel.1), channel_id=1, replica_groups=mesh['grp'=2,'ex'=16] {'ex'}, dimensions={0} | all-to-all | bytes 65536 | tf_op jit(solution)/shard_map/all_to_all | solution.py:197
  39.8 1.2 %output_kernel.1 = (f32[2,32]{1,0:T(2,128)}, f32[1,2]{1,0:T(1,128)}) custom-call(s32[2]{0:T(128)S(1)} %pad_add_fusion.place, f32[16,4,128]{2,1,0:T(4,128)S(1)} %all_to_all.5.sums_ref), custom_call_target="tpu_custom_call" | custom-call | tf_op jit(solution)/shard_map/output_kernel/pallas_call | solution.py:200
  (10 shorter events, 0.2 us)
Async XLA Ops:
  1.8 3.1 %copy-start = (bf16[128,256]{1,0:T(8,128)(2,1)S(1)}, bf16[128,256]{1,0:T(8,128)(2,1)}, u32[]{:S(2)}) copy-start(bf16[128,256]{1,0:T(8,128)(2,1)} %param.4) | copy-start | bytes 196612
  1.9 9.5 %collective-permute-start.1 = (bf16[3,128,256]{2,1,0:T(8,128)(2,1)S(1)}, bf16[3,128,256]{2,1,0:T(8,128)(2,1)S(1)}, u32[]{:S(2)}, u32[]{:S(2)}) collective-permute-start(bf16[3,128,256]{2,1,0:T(8,128)(2,1)S(1)} %pad_maximum_fusion.4), channel_id=1, source_target_pairs={{0,2},{1,3},{2,0},{3,1},{4,6},{5,7},{6,4},{7,5},{8,10},{9,11},{10,... | collective-permute-start | bytes 589832 | tf_op jit(solution)/shard_map/ppermute | solution.py:15
  4.9 6.9 %collective-permute-start.2 = (bf16[128,256]{1,0:T(8,128)(2,1)S(1)}, bf16[128,256]{1,0:T(8,128)(2,1)S(1)}, u32[]{:S(2)}, u32[]{:S(2)}) collective-permute-start(bf16[128,256]{1,0:T(8,128)(2,1)S(1)} %copy-done), channel_id=1, source_target_pairs={{0,12},{1,13},{2,14},{3,15},{4,8},{5,9},{6,10},{7,11},{8,4},{9,5},... | collective-permute-start | bytes 196616 | tf_op jit(solution)/shard_map/ppermute | solution.py:15
  8.5 7.7 %collective-permute-start.7 = (bf16[128,256]{1,0:T(8,128)(2,1)S(1)}, bf16[128,256]{1,0:T(8,128)(2,1)S(1)}, u32[]{:S(2)}, u32[]{:S(2)}) collective-permute-start(bf16[128,256]{1,0:T(8,128)(2,1)S(1)} %copy-done), channel_id=1, source_target_pairs={{0,8},{1,9},{2,10},{3,11},{4,12},{5,13},{6,14},{7,15},{8,0},{9,1},... | collective-permute-start | bytes 196616 | tf_op jit(solution)/shard_map/ppermute | solution.py:15
  8.5 7.7 %collective-permute-start.6 = (bf16[128,256]{1,0:T(8,128)(2,1)S(1)}, bf16[128,256]{1,0:T(8,128)(2,1)S(1)}, u32[]{:S(2)}, u32[]{:S(2)}) collective-permute-start(bf16[128,256]{1,0:T(8,128)(2,1)S(1)} %copy-done), channel_id=1, source_target_pairs={{0,4},{1,5},{2,6},{3,7},{4,0},{5,1},{6,2},{7,3},{8,12},{9,13},{10,... | collective-permute-start | bytes 196616 | tf_op jit(solution)/shard_map/ppermute | solution.py:15
  9.3 6.3 %collective-permute-start = (bf16[128,256]{1,0:T(8,128)(2,1)S(1)}, bf16[128,256]{1,0:T(8,128)(2,1)S(1)}, u32[]{:S(2)}, u32[]{:S(2)}) collective-permute-start(bf16[128,256]{1,0:T(8,128)(2,1)S(1)} %get-tuple-element.33), channel_id=1, source_target_pairs={{0,2},{1,3},{2,0},{3,1},{4,6},{5,7},{6,4},{7,5},{8,10},{9,11},{10,... | collective-permute-start | bytes 196616 | tf_op jit(solution)/shard_map/ppermute | solution.py:15
  10.0 0.7 %copy-start.1 = (bf16[2]{0:T(256)(128)(2,1)S(1)}, bf16[2]{0:T(256)(128)(2,1)}, u32[]{:S(2)}) copy-start(bf16[2]{0:T(256)(128)(2,1)} %param.5) | copy-start | bytes 16
  11.8 11.9 %collective-permute-start.4 = (bf16[256,256]{1,0:T(8,128)(2,1)S(1)}, bf16[256,256]{1,0:T(8,128)(2,1)S(1)}, u32[]{:S(2)}, u32[]{:S(2)}) collective-permute-start(bf16[256,256]{1,0:T(8,128)(2,1)S(1)} %pad_maximum_fusion.6), channel_id=1, source_target_pairs={{0,8},{1,9},{2,10},{3,11},{4,12},{5,13},{6,14},{7,15},{8,0},{9,1},... | collective-permute-start | bytes 393224 | tf_op jit(solution)/shard_map/ppermute | solution.py:15
  14.0 9.7 %collective-permute-start.5 = (bf16[256,256]{1,0:T(8,128)(2,1)S(1)}, bf16[256,256]{1,0:T(8,128)(2,1)S(1)}, u32[]{:S(2)}, u32[]{:S(2)}) collective-permute-start(bf16[256,256]{1,0:T(8,128)(2,1)S(1)} %pad_maximum_fusion.7), channel_id=1, source_target_pairs={{0,12},{1,13},{2,14},{3,15},{4,8},{5,9},{6,10},{7,11},{8,4},{9,5},... | collective-permute-start | bytes 393224 | tf_op jit(solution)/shard_map/ppermute | solution.py:15
  15.6 8.1 %collective-permute-start.3 = (bf16[256,256]{1,0:T(8,128)(2,1)S(1)}, bf16[256,256]{1,0:T(8,128)(2,1)S(1)}, u32[]{:S(2)}, u32[]{:S(2)}) collective-permute-start(bf16[256,256]{1,0:T(8,128)(2,1)S(1)} %pad_maximum_fusion.5), channel_id=1, source_target_pairs={{0,4},{1,5},{2,6},{3,7},{4,0},{5,1},{6,2},{7,3},{8,12},{9,13},{10,... | collective-permute-start | bytes 393224 | tf_op jit(solution)/shard_map/ppermute | solution.py:15
  16.3 8.0 %collective-permute-start.8 = (bf16[4,128,256]{2,1,0:T(8,128)(2,1)S(1)}, bf16[4,128,256]{2,1,0:T(8,128)(2,1)S(1)}, u32[]{:S(2)}, u32[]{:S(2)}) collective-permute-start(bf16[4,128,256]{2,1,0:T(8,128)(2,1)S(1)} %get-tuple-element.37), channel_id=1, source_target_pairs={{0,2},{1,3},{2,0},{3,1},{4,6},{5,7},{6,4},{7,5},{8,10},{9,11},{10,... | collective-permute-start | bytes 786440 | tf_op jit(solution)/shard_map/ppermute | solution.py:15
  23.7 2.8 %collective-permute-start.9 = (bf16[4,256,256]{2,1,0:T(8,128)(2,1)S(1)}, bf16[4,256,256]{2,1,0:T(8,128)(2,1)S(1)}, u32[]{:S(2)}, u32[]{:S(2)}) collective-permute-start(bf16[4,256,256]{2,1,0:T(8,128)(2,1)S(1)} %pad_maximum_fusion.x_ref), channel_id=1, source_target_pairs={{0,1},{1,0},{2,3},{3,2},{4,5},{5,4},{6,7},{7,6},{8,9},{9,8},{10,11... | collective-permute-start | bytes 1572872 | tf_op jit(solution)/shard_map/ppermute | solution.py:15
  23.8 2.3 %collective-permute-start.10 = (bf16[4,128,256]{2,1,0:T(8,128)(2,1)S(1)}, bf16[4,128,256]{2,1,0:T(8,128)(2,1)S(1)}, u32[]{:S(2)}, u32[]{:S(2)}) collective-permute-start(bf16[4,128,256]{2,1,0:T(8,128)(2,1)S(1)} %get-tuple-element.37), channel_id=1, source_target_pairs={{0,1},{1,0},{2,3},{3,2},{4,5},{5,4},{6,7},{7,6},{8,9},{9,8},{10,11... | collective-permute-start | bytes 786440 | tf_op jit(solution)/shard_map/ppermute | solution.py:15
  24.3 2.1 %collective-permute-start.11 = (bf16[4,128,256]{2,1,0:T(8,128)(2,1)S(1)}, bf16[4,128,256]{2,1,0:T(8,128)(2,1)S(1)}, u32[]{:S(2)}, u32[]{:S(2)}) collective-permute-start(bf16[4,128,256]{2,1,0:T(8,128)(2,1)S(1)} %collective-permute-done.8), channel_id=1, source_target_pairs={{0,1},{1,0},{2,3},{3,2},{4,5},{5,4},{6,7},{7,6},{8,9},{9,8},{10,11... | collective-permute-start | bytes 786440 | tf_op jit(solution)/shard_map/ppermute | solution.py:15

commit v4 on v3

--- a/solution.py
+++ b/solution.py
@@ -32,7 +32,9 @@
     return (2 * jnp.bitwise_xor(place[0], distance) + jnp.bitwise_xor(place[1], far)) * local_count + within
 
 
-def order_kernel(local_count, seq_length, place, weight, own_spread, far_spread, gather_ref, weight_ref):
+def order_kernel(
+    local_count, seq_length, place, weight, own_spread, far_spread, gather_ref, weight_ref, below_ref, own_ref
+):
     examples = own_spread.shape[0] // seq_length
     lane = lax.broadcasted_iota(jnp.int32, (seq_length, LANES), 1)
     for far, ref in enumerate((own_spread, far_spread)):
@@ -49,6 +51,10 @@
     for k in range(local_count):
         weights = jnp.where(lane == k, weight[k], weights)
     weight_ref[...] = weights
+    own = (2 * place[0] + place[1]) * local_count + lax.broadcasted_iota(jnp.int32, below_ref.shape, 0)
+    lane = lax.broadcasted_iota(jnp.int32, below_ref.shape, 1)
+    below_ref[...] = (lane < own).astype(jnp.float32)
+    own_ref[...] = (lane == own).astype(jnp.float32)
 
 
 def pair_sums(seq_length, rows_x, rows_c, far_x, far_c, spread, gather, sums_ref):
@@ -105,19 +111,17 @@
     out_ref[:, :local_count] = gram[: devices * local_count].reshape(devices, local_count, LANES)
 
 
-def output_kernel(local_count, kernel_scale, norm_scale, place, sums_ref, kernel_ref, norms_ref):
+def output_kernel(local_count, kernel_scale, norm_scale, below, diagonal, sums_ref, kernel_ref, norms_ref):
     total = jnp.sum(sums_ref[...], axis=0)
     weights = total[local_count : local_count + 1]
+    own = diagonal[:local_count]
+    mine = jnp.sum(own * weights, axis=1, keepdims=True)
+    grams = total[:local_count] * (mine * weights)
+    kernel_ref[...] = ((grams * below[:local_count]) / kernel_scale)[:, : kernel_ref.shape[1]]
+    norms = jnp.sum(grams * own, axis=1, keepdims=True) / norm_scale
     shape = (local_count, LANES)
-    first = (2 * place[0] + place[1]) * local_count
-    own = first + lax.broadcasted_iota(jnp.int32, shape, 0)
-    lane = lax.broadcasted_iota(jnp.int32, shape, 1)
-    mine = jnp.sum(jnp.where(lane == own, weights, 0.0), axis=1, keepdims=True)
-    grams = total[:local_count] * (mine * weights)
-    kernel_ref[...] = (jnp.where(lane < own, grams, 0.0) / kernel_scale)[:, : kernel_ref.shape[1]]
-    norms = jnp.sum(jnp.where(lane == own, grams, 0.0), axis=0, keepdims=True) / norm_scale
-    norms = jnp.broadcast_to(norms, (8, LANES))
-    norms_ref[...] = pltpu.roll(norms, LANES - first, 1)[:1, :local_count]
+    row, lane = (lax.broadcasted_iota(jnp.int32, shape, axis) for axis in (0, 1))
+    norms_ref[...] = jnp.sum(jnp.where(row == lane, norms, 0.0), axis=0, keepdims=True)[:, :local_count]
 
 
 def body(layer_input, cotangent, example_weight):
@@ -139,17 +143,6 @@
 
     array = jax.ShapeDtypeStruct
     place = jnp.stack([chip, core]).astype(jnp.int32)
-    shapes = [array((chips * tokens, LANES), jnp.bfloat16)] * 2
-    shapes += [array((LANES, planes * 8), jnp.bfloat16), array((8, LANES), jnp.float32)]
-    own_spread, far_spread, gather, weight_row = pl.pallas_call(
-        functools.partial(order_kernel, local_count, seq_length),
-        out_shape=shapes,
-        in_specs=[smem] * 2,
-        out_specs=[vmem] * len(shapes),
-        compiler_params=params,
-        name="order_kernel",
-    )(place, weight)
-
     cot = {0: cotangent}
     for z in range(planes - 1, 0, -1):
         cot[z] = swapped(cotangent, 4 * z)
@@ -157,22 +150,36 @@
         return lax.dynamic_slice_in_dim(layer_input, (chip ^ distance) * chip_width, chip_width, 1)
 
     moved = swapped(jnp.stack([columns(2 * z + 1) for z in range(1, planes)]), 2)
-    moved, order = lax.optimization_barrier((moved, (own_spread, far_spread, gather, weight_row)))
-    own_spread, far_spread, gather, weight_row = order
+    moved, place, weight = lax.optimization_barrier((moved, place, weight))
     over_y = {z: moved[z - 1] for z in range(1, planes)}
-    over_y[0] = swapped(columns(1), 2)
+    shapes = [array((chips * tokens, LANES), jnp.bfloat16)] * 2
+    shapes += [array((LANES, planes * 8), jnp.bfloat16)] + [array((8, LANES), jnp.float32)] * 3
+    order = pl.pallas_call(
+        functools.partial(order_kernel, local_count, seq_length),
+        out_shape=shapes,
+        in_specs=[smem] * 2,
+        out_specs=[vmem] * len(shapes),
+        compiler_params=params,
+        name="order_kernel",
+    )(place, weight)
+
     mine = {}
-    for z in [z for z in range(2, planes)] + [1, 0]:
+    for z in range(planes - 1, 0, -1):
         part = jnp.concatenate([columns(2 * z), over_y[z]])
         if z == 1 and planes > 2:
             part, cot[planes - 1] = lax.optimization_barrier((part, cot[planes - 1]))
-        mine[z] = swapped(part, 4 * z) if z else part
+        if z == 1:
+            part, order = lax.optimization_barrier((part, order))
+        mine[z] = swapped(part, 4 * z)
     over_z = jnp.stack([cot[z] for z in range(planes)])
     over_zy = swapped(over_z, 2)
+    mine[0] = jnp.concatenate([columns(0), swapped(columns(1), 2)])
+    other_z, other_zy = swapped(over_z, 1), swapped(over_zy, 1)
     own_c = jnp.stack([over_z, over_zy], axis=1).reshape(planes, 2 * tokens, heads)
-    far_c = jnp.stack([swapped(over_z, 1), swapped(over_zy, 1)], axis=1).reshape(planes, 2 * tokens, heads)
+    far_c = jnp.stack([other_z, other_zy], axis=1).reshape(planes, 2 * tokens, heads)
+    own_spread, far_spread, gather, weight_row, below, diagonal = order
     own_x = jnp.stack([mine[z] for z in range(planes)])
-    far_x = swapped(own_x, 1)
+    far_x = jnp.concatenate([swapped(own_x[:1], 1), swapped(own_x[1:], 1)])
 
     sums = [pltpu.VMEM((planes, 8, chips * tokens), jnp.float32)]
     own = pl.pallas_call(
@@ -200,11 +207,11 @@
     kernel, sq_norms = pl.pallas_call(
         functools.partial(output_kernel, local_count, *scales),
         out_shape=[array((local_count, count), jnp.float32), array((1, local_count), jnp.float32)],
-        in_specs=[smem, vmem],
+        in_specs=[vmem] * 3,
         out_specs=[vmem] * 2,
         compiler_params=params,
         name="output_kernel",
-    )(place, received)
+    )(below, diagonal, received)
     return (kernel, sq_norms.reshape(local_count))
 
 

time: 41.2 us -> 40.6 us (0.985)
  starting transfers between devices: 14.2 us -> 16 us
  blocking collectives: 12 us -> 10.5 us
  waiting for transfers between devices: 7.54 us -> 6.92 us
  Pallas kernels: 4.24 us -> 3.71 us
    ppermute x12 -> x13, starting transfers between devices: 14.2 us -> 16 us  [swapped(): return lax.ppermute(value, 'ex', [(i, i ^ distance) for i in range(count)])]
    all_to_all x1, blocking collectives: 12 us -> 10.5 us  [body(): lax.all_to_all(partial, 'ex', split_axis=0, concat_axis=0, tiled=True)]
    ppermute x12 -> x13, waiting for transfers between devices: 7.54 us -> 6.92 us  [swapped(): return lax.ppermute(value, 'ex', [(i, i ^ distance) for i in range(count)])]
    pallas_call x1, Pallas kernels: 1.22 us -> 0.69 us  [body(): pl.pallas_call(functools.partial(output_kernel, local_count, *scales), ou...]
  transfers between devices with their start and end apart: 12 -> 13, of which waited for: 4 -> 4; matrix products, arithmetic and copies ran while one was open for 1% -> 1% of each run, Pallas kernels for 4% -> 4%
where the time goes in v4:
time: 40.6 us; the launch traced here: 40.4 us
  starting transfers between devices  16 us (39%)
  blocking collectives  10.5 us (26%)
  waiting for transfers between devices  6.92 us (17%)
  Pallas kernels  3.71 us (9%)
  local copies, waits for them, and re-layouts  1.87 us (5%)
  between operations  0.83 us (2%)
  other arithmetic  0.45 us (1%)
    ppermute x13, starting transfers between devices, swapped(): return lax.ppermute(value, 'ex', [(i, i ^ distance) for i in range(count)])  16 us
    all_to_all x1, blocking collectives, body(): lax.all_to_all(partial, 'ex', split_axis=0, concat_axis=0, tiled=True)  10.5 us
    ppermute x13, waiting for transfers between devices, swapped(): return lax.ppermute(value, 'ex', [(i, i ^ distance) for i in range(count)])  6.92 us
    pallas_call x1, Pallas kernels, body(): pl.pallas_call(functools.partial(far_kernel, seq_length, local_count), ou...  1.24 us
    pallas_call x1, Pallas kernels, body(): pl.pallas_call(functools.partial(own_kernel, seq_length), out_shape=array...  1.18 us
    dynamic_slice x1, local copies, waits for them, and re-layouts, columns(): lax.dynamic_slice_in_dim(layer_input, (chip ^ distance) * chip_width, chi...  1.12 us
  transfers between devices with their start and end apart: 13, of which 4 were waited for; matrix products, arithmetic and copies ran while one was open for 1% of the time, Pallas kernels for 4%

profile of v4, /device:TPU:0, one launch (start us, length us, event | category | flops | bytes accessed | tf_op | source)
XLA Modules:
  0.0 40.4 jit_solution(561028370844615052)
XLA Ops:
  0.7 1.1 %constant_dynamic-slice_fusion.3 = (bf16[128,256]{1,0:T(8,128)(2,1)S(1)}, bf16[128,256]{1,0:T(8,128)(2,1)S(1)}, bf16[1,128,256]{2,1,0:T(8,128)(2,1)S(1)}, bf16[1...) fusion(bf16[128,2048]{1,0:T(8,128)(2,1)} %param.3, ...), kind=kLoop, calls=%fused_computation.20 | loop fusion | bytes 1048608 | tf_op jit(solution)/shard_map/dynamic_slice | solution.py:150
  1.8 0.0 copy-start
  1.9 3.0 %collective-permute-start = (bf16[3,128,256]{2,1,0:T(8,128)(2,1)S(1)}, bf16[3,128,256]{2,1,0:T(8,128)(2,1)S(1)}, u32[]{:S(2)}, u32[]{:S(2)}) collective-permute-start(bf16[3,128,256]{2,1,0:T(8,128)(2,1)S(1)} %pad_maximum_fusion.6), channel_id=1, source_target_pairs={{0,2},{1,3},{2,0},{3,1},{4,6},{5,7},{6,4},{7,5},{8,10},{9,11},{10,... | collective-permute-start | bytes 589832 | tf_op jit(solution)/shard_map/ppermute | solution.py:15
  4.9 0.0 copy-done
  4.9 3.6 %collective-permute-start.1 = (bf16[128,256]{1,0:T(8,128)(2,1)S(1)}, bf16[128,256]{1,0:T(8,128)(2,1)S(1)}, u32[]{:S(2)}, u32[]{:S(2)}) collective-permute-start(bf16[128,256]{1,0:T(8,128)(2,1)S(1)} %copy-done), channel_id=1, source_target_pairs={{0,12},{1,13},{2,14},{3,15},{4,8},{5,9},{6,10},{7,11},{8,4},{9,5},... | collective-permute-start | bytes 196616 | tf_op jit(solution)/shard_map/ppermute | solution.py:15
  8.5 0.0 collective-permute-start.7
  8.5 0.8 %collective-permute-start.6 = (bf16[128,256]{1,0:T(8,128)(2,1)S(1)}, bf16[128,256]{1,0:T(8,128)(2,1)S(1)}, u32[]{:S(2)}, u32[]{:S(2)}) collective-permute-start(bf16[128,256]{1,0:T(8,128)(2,1)S(1)} %copy-done), channel_id=1, source_target_pairs={{0,4},{1,5},{2,6},{3,7},{4,0},{5,1},{6,2},{7,3},{8,12},{9,13},{10,... | collective-permute-start | bytes 196616 | tf_op jit(solution)/shard_map/ppermute | solution.py:15
  9.3 0.0 copy-start.1
  9.3 0.7 %copy-done.1 = bf16[2]{0:T(256)(128)(2,1)S(1)} copy-done((bf16[2]{0:T(256)(128)(2,1)S(1)}, bf16[2]{0:T(256)(128)(2,1)}, u32[]{:S(2)}) %copy-start.1) | copy-done | bytes 28
  9.9 0.1 pad_add_fusion.place
  10.0 0.0 collective-permute-done
  10.1 1.7 %collective-permute-done.1 = bf16[128,256]{1,0:T(8,128)(2,1)S(1)} collective-permute-done((bf16[128,256]{1,0:T(8,128)(2,1)S(1)}, bf16[128,256]{1,0:T(8,128)(2,1)S(1)}, u32[]{:S(2)}, u32[]{:S(2)}) %collective-permute-start.1) | collective-permute-done | bytes 65568 | tf_op jit(solution)/shard_map/ppermute | solution.py:15
  11.8 3.7 %collective-permute-start.5 = (bf16[256,256]{1,0:T(8,128)(2,1)S(1)}, bf16[256,256]{1,0:T(8,128)(2,1)S(1)}, u32[]{:S(2)}, u32[]{:S(2)}) collective-permute-start(bf16[256,256]{1,0:T(8,128)(2,1)S(1)} %pad_maximum_fusion.9), channel_id=1, source_target_pairs={{0,12},{1,13},{2,14},{3,15},{4,8},{5,9},{6,10},{7,11},{8,4},{9,5},... | collective-permute-start | bytes 393224 | tf_op jit(solution)/shard_map/ppermute | solution.py:15
  15.5 0.0 collective-permute-done.7
  15.5 0.0 collective-permute-done.6
  15.5 0.7 %collective-permute-start.8 = (bf16[4,128,256]{2,1,0:T(8,128)(2,1)S(1)}, bf16[4,128,256]{2,1,0:T(8,128)(2,1)S(1)}, u32[]{:S(2)}, u32[]{:S(2)}) collective-permute-start(bf16[4,128,256]{2,1,0:T(8,128)(2,1)S(1)} %get-tuple-element.51), channel_id=1, source_target_pairs={{0,2},{1,3},{2,0},{3,1},{4,6},{5,7},{6,4},{7,5},{8,10},{9,11},{10,... | collective-permute-start | bytes 786440 | tf_op jit(solution)/shard_map/ppermute | solution.py:15
  16.2 1.1 %collective-permute-start.4 = (bf16[256,256]{1,0:T(8,128)(2,1)S(1)}, bf16[256,256]{1,0:T(8,128)(2,1)S(1)}, u32[]{:S(2)}, u32[]{:S(2)}) collective-permute-start(bf16[256,256]{1,0:T(8,128)(2,1)S(1)} %pad_maximum_fusion.8), channel_id=1, source_target_pairs={{0,8},{1,9},{2,10},{3,11},{4,12},{5,13},{6,14},{7,15},{8,0},{9,1},... | collective-permute-start | bytes 393224 | tf_op jit(solution)/shard_map/ppermute | solution.py:15
  17.3 0.6 %order_kernel.1 = (bf16[1024,128]{1,0:T(8,128)(2,1)S(1)}, bf16[1024,128]{1,0:T(8,128)(2,1)S(1)}, bf16[128,32]{1,0:T(8,128)(2,1)S(1)}, f32[8,128]{1,0:T(8,128)S(1...) custom-call(s32[2]{0:T(128)S(1)} %pad_add_fusion.place, f32[2]{0:T(128)S(1)} %convert_element_type.3.weight), custom_call_target="tpu_custom_call" | custom-call | tf_op jit(solution)/shard_map/order_kernel/pallas_call | solution.py:157
  17.9 1.4 %collective-permute-start.3 = (bf16[256,256]{1,0:T(8,128)(2,1)S(1)}, bf16[256,256]{1,0:T(8,128)(2,1)S(1)}, u32[]{:S(2)}, u32[]{:S(2)}) collective-permute-start(bf16[256,256]{1,0:T(8,128)(2,1)S(1)} %pad_maximum_fusion.7), channel_id=1, source_target_pairs={{0,4},{1,5},{2,6},{3,7},{4,0},{5,1},{6,2},{7,3},{8,12},{9,13},{10,... | collective-permute-start | bytes 393224 | tf_op jit(solution)/shard_map/ppermute | solution.py:15
  19.3 1.1 %collective-permute-start.2 = (bf16[128,256]{1,0:T(8,128)(2,1)S(1)}, bf16[128,256]{1,0:T(8,128)(2,1)S(1)}, u32[]{:S(2)}, u32[]{:S(2)}) collective-permute-start(bf16[128,256]{1,0:T(8,128)(2,1)S(1)} %get-tuple-element.43), channel_id=1, source_target_pairs={{0,2},{1,3},{2,0},{3,1},{4,6},{5,7},{6,4},{7,5},{8,10},{9,11},{10,... | collective-permute-start | bytes 196616 | tf_op jit(solution)/shard_map/ppermute | solution.py:15
  20.4 0.0 collective-permute-done.5
  20.4 0.0 collective-permute-start.11
  20.4 4.8 %collective-permute-done.4 = bf16[256,256]{1,0:T(8,128)(2,1)S(1)} collective-permute-done((bf16[256,256]{1,0:T(8,128)(2,1)S(1)}, bf16[256,256]{1,0:T(8,128)(2,1)S(1)}, u32[]{:S(2)}, u32[]{:S(2)}) %collective-permute-start.4) | collective-permute-done | bytes 131104 | tf_op jit(solution)/shard_map/ppermute | solution.py:15
  25.2 0.3 collective-permute-done.3
  25.5 0.1 collective-permute-start.10
  25.6 0.0 collective-permute-done.8
  25.6 0.5 %collective-permute-start.12 = (bf16[4,128,256]{2,1,0:T(8,128)(2,1)S(1)}, bf16[4,128,256]{2,1,0:T(8,128)(2,1)S(1)}, u32[]{:S(2)}, u32[]{:S(2)}) collective-permute-start(bf16[4,128,256]{2,1,0:T(8,128)(2,1)S(1)} %collective-permute-done.8), channel_id=1, source_target_pairs={{0,1},{1,0},{2,3},{3,2},{4,5},{5,4},{6,7},{7,6},{8,9},{9,8},{10,11... | collective-permute-start | bytes 786440 | tf_op jit(solution)/shard_map/ppermute | solution.py:15
  26.1 0.0 collective-permute-done.2
  26.1 0.2 collective-permute-start.9
  26.2 0.1 pad_maximum_fusion.x_ref
  26.3 0.1 pad_maximum_fusion.1
  26.4 1.2 %own_kernel.1.own_ref = f32[128,128]{1,0:T(8,128)S(1)} custom-call(bf16[4,256,256]{2,1,0:T(8,128)(2,1)S(1)} %pad_maximum_fusion.x_ref, bf16[4,256,256]{2,1,0:T(8,128)(2,1)S(1)} %bitcast.31, bf16[1024,128]{1,0:T(8,128)(2,1)S(1)} %get-tuple-element.39.spread, bf16[128,32]{1,0:T(8,128)(2,1)S(1)} %get-tuple-element.37.gather), custom_call_target="tpu_custom_call" | custom-call | tf_op jit(solution)/shard_map/own_kernel/pallas_call | solution.py:185
  27.6 0.0 collective-permute-done.11
  27.6 0.0 collective-permute-done.12
  27.6 0.1 pad_maximum_fusion.3
  27.7 0.1 collective-permute-done.9
  27.8 0.0 collective-permute-done.10
  27.9 1.2 %far_kernel.1 = f32[16,4,128]{2,1,0:T(4,128)S(1)} custom-call(bf16[4,256,256]{2,1,0:T(8,128)(2,1)S(1)} %pad_maximum_fusion.x_ref, bf16[4,256,256]{2,1,0:T(8,128)(2,1)S(1)} %bitcast.32, bf16[4,256,256]{2,1,0:T(8,128)(2,1)S(1)} %pad_maximum_fusion.2.far_x, bf16[4,256,256]{2,1,0:T(8,128)(2,1)S(1)} %bitcast.33, bf16[1024,128]{1,0:T(8,128)(2,1)S(1)} %get-tuple-element.36.spread, ...), custom_call_target="tpu_custom_call" | custom-call | tf_op jit(solution)/shard_map/far_kernel/pallas_call | solution.py:194
  29.1 10.5 %all_to_all.5.sums_ref = f32[16,4,128]{2,1,0:T(4,128)S(1)} all-to-all(f32[16,4,128]{2,1,0:T(4,128)S(1)} %far_kernel.1), channel_id=1, replica_groups=mesh['grp'=2,'ex'=16] {'ex'}, dimensions={0} | all-to-all | bytes 65536 | tf_op jit(solution)/shard_map/all_to_all | solution.py:204
  39.7 0.7 %output_kernel.1 = (f32[2,32]{1,0:T(2,128)}, f32[1,2]{1,0:T(1,128)}) custom-call(f32[8,128]{1,0:T(8,128)S(1)} %get-tuple-element.32.below, f32[8,128]{1,0:T(8,128)S(1)} %get-tuple-element.33.diagonal, f32[16,4,128]{2,1,0:T(4,128)S(1)} %all_to_all.5.sums_ref), custom_call_target="tpu_custom_call" | custom-call | tf_op jit(solution)/shard_map/output_kernel/pallas_call | solution.py:207
  (12 shorter events, 0.3 us)
Async XLA Ops:
  1.8 3.1 %copy-start = (bf16[128,256]{1,0:T(8,128)(2,1)S(1)}, bf16[128,256]{1,0:T(8,128)(2,1)}, u32[]{:S(2)}) copy-start(bf16[128,256]{1,0:T(8,128)(2,1)} %param.4) | copy-start | bytes 196612
  1.9 8.2 %collective-permute-start = (bf16[3,128,256]{2,1,0:T(8,128)(2,1)S(1)}, bf16[3,128,256]{2,1,0:T(8,128)(2,1)S(1)}, u32[]{:S(2)}, u32[]{:S(2)}) collective-permute-start(bf16[3,128,256]{2,1,0:T(8,128)(2,1)S(1)} %pad_maximum_fusion.6), channel_id=1, source_target_pairs={{0,2},{1,3},{2,0},{3,1},{4,6},{5,7},{6,4},{7,5},{8,10},{9,11},{10,... | collective-permute-start | bytes 589832 | tf_op jit(solution)/shard_map/ppermute | solution.py:15
  4.9 6.9 %collective-permute-start.1 = (bf16[128,256]{1,0:T(8,128)(2,1)S(1)}, bf16[128,256]{1,0:T(8,128)(2,1)S(1)}, u32[]{:S(2)}, u32[]{:S(2)}) collective-permute-start(bf16[128,256]{1,0:T(8,128)(2,1)S(1)} %copy-done), channel_id=1, source_target_pairs={{0,12},{1,13},{2,14},{3,15},{4,8},{5,9},{6,10},{7,11},{8,4},{9,5},... | collective-permute-start | bytes 196616 | tf_op jit(solution)/shard_map/ppermute | solution.py:15
  8.5 7.0 %collective-permute-start.7 = (bf16[128,256]{1,0:T(8,128)(2,1)S(1)}, bf16[128,256]{1,0:T(8,128)(2,1)S(1)}, u32[]{:S(2)}, u32[]{:S(2)}) collective-permute-start(bf16[128,256]{1,0:T(8,128)(2,1)S(1)} %copy-done), channel_id=1, source_target_pairs={{0,8},{1,9},{2,10},{3,11},{4,12},{5,13},{6,14},{7,15},{8,0},{9,1},... | collective-permute-start | bytes 196616 | tf_op jit(solution)/shard_map/ppermute | solution.py:15
  8.5 7.0 %collective-permute-start.6 = (bf16[128,256]{1,0:T(8,128)(2,1)S(1)}, bf16[128,256]{1,0:T(8,128)(2,1)S(1)}, u32[]{:S(2)}, u32[]{:S(2)}) collective-permute-start(bf16[128,256]{1,0:T(8,128)(2,1)S(1)} %copy-done), channel_id=1, source_target_pairs={{0,4},{1,5},{2,6},{3,7},{4,0},{5,1},{6,2},{7,3},{8,12},{9,13},{10,... | collective-permute-start | bytes 196616 | tf_op jit(solution)/shard_map/ppermute | solution.py:15
  9.3 0.7 %copy-start.1 = (bf16[2]{0:T(256)(128)(2,1)S(1)}, bf16[2]{0:T(256)(128)(2,1)}, u32[]{:S(2)}) copy-start(bf16[2]{0:T(256)(128)(2,1)} %param.5) | copy-start | bytes 16
  11.8 8.6 %collective-permute-start.5 = (bf16[256,256]{1,0:T(8,128)(2,1)S(1)}, bf16[256,256]{1,0:T(8,128)(2,1)S(1)}, u32[]{:S(2)}, u32[]{:S(2)}) collective-permute-start(bf16[256,256]{1,0:T(8,128)(2,1)S(1)} %pad_maximum_fusion.9), channel_id=1, source_target_pairs={{0,12},{1,13},{2,14},{3,15},{4,8},{5,9},{6,10},{7,11},{8,4},{9,5},... | collective-permute-start | bytes 393224 | tf_op jit(solution)/shard_map/ppermute | solution.py:15
  15.5 10.0 %collective-permute-start.8 = (bf16[4,128,256]{2,1,0:T(8,128)(2,1)S(1)}, bf16[4,128,256]{2,1,0:T(8,128)(2,1)S(1)}, u32[]{:S(2)}, u32[]{:S(2)}) collective-permute-start(bf16[4,128,256]{2,1,0:T(8,128)(2,1)S(1)} %get-tuple-element.51), channel_id=1, source_target_pairs={{0,2},{1,3},{2,0},{3,1},{4,6},{5,7},{6,4},{7,5},{8,10},{9,11},{10,... | collective-permute-start | bytes 786440 | tf_op jit(solution)/shard_map/ppermute | solution.py:15
  16.2 8.9 %collective-permute-start.4 = (bf16[256,256]{1,0:T(8,128)(2,1)S(1)}, bf16[256,256]{1,0:T(8,128)(2,1)S(1)}, u32[]{:S(2)}, u32[]{:S(2)}) collective-permute-start(bf16[256,256]{1,0:T(8,128)(2,1)S(1)} %pad_maximum_fusion.8), channel_id=1, source_target_pairs={{0,8},{1,9},{2,10},{3,11},{4,12},{5,13},{6,14},{7,15},{8,0},{9,1},... | collective-permute-start | bytes 393224 | tf_op jit(solution)/shard_map/ppermute | solution.py:15
  17.9 7.5 %collective-permute-start.3 = (bf16[256,256]{1,0:T(8,128)(2,1)S(1)}, bf16[256,256]{1,0:T(8,128)(2,1)S(1)}, u32[]{:S(2)}, u32[]{:S(2)}) collective-permute-start(bf16[256,256]{1,0:T(8,128)(2,1)S(1)} %pad_maximum_fusion.7), channel_id=1, source_target_pairs={{0,4},{1,5},{2,6},{3,7},{4,0},{5,1},{6,2},{7,3},{8,12},{9,13},{10,... | collective-permute-start | bytes 393224 | tf_op jit(solution)/shard_map/ppermute | solution.py:15
  19.3 6.8 %collective-permute-start.2 = (bf16[128,256]{1,0:T(8,128)(2,1)S(1)}, bf16[128,256]{1,0:T(8,128)(2,1)S(1)}, u32[]{:S(2)}, u32[]{:S(2)}) collective-permute-start(bf16[128,256]{1,0:T(8,128)(2,1)S(1)} %get-tuple-element.43), channel_id=1, source_target_pairs={{0,2},{1,3},{2,0},{3,1},{4,6},{5,7},{6,4},{7,5},{8,10},{9,11},{10,... | collective-permute-start | bytes 196616 | tf_op jit(solution)/shard_map/ppermute | solution.py:15
  20.4 7.2 %collective-permute-start.11 = (bf16[4,128,256]{2,1,0:T(8,128)(2,1)S(1)}, bf16[4,128,256]{2,1,0:T(8,128)(2,1)S(1)}, u32[]{:S(2)}, u32[]{:S(2)}) collective-permute-start(bf16[4,128,256]{2,1,0:T(8,128)(2,1)S(1)} %get-tuple-element.51), channel_id=1, source_target_pairs={{0,1},{1,0},{2,3},{3,2},{4,5},{5,4},{6,7},{7,6},{8,9},{9,8},{10,11... | collective-permute-start | bytes 786440 | tf_op jit(solution)/shard_map/ppermute | solution.py:15
  25.5 2.4 %collective-permute-start.10 = (bf16[3,256,256]{2,1,0:T(8,128)(2,1)S(1)}, bf16[3,256,256]{2,1,0:T(8,128)(2,1)S(1)}, u32[]{:S(2)}, u32[]{:S(2)}) collective-permute-start(bf16[3,256,256]{2,1,0:T(8,128)(2,1)S(1)} %pad_maximum_fusion.4), channel_id=1, source_target_pairs={{0,1},{1,0},{2,3},{3,2},{4,5},{5,4},{6,7},{7,6},{8,9},{9,8},{10,11... | collective-permute-start | bytes 1179656 | tf_op jit(solution)/shard_map/ppermute | solution.py:15
  25.6 2.1 %collective-permute-start.12 = (bf16[4,128,256]{2,1,0:T(8,128)(2,1)S(1)}, bf16[4,128,256]{2,1,0:T(8,128)(2,1)S(1)}, u32[]{:S(2)}, u32[]{:S(2)}) collective-permute-start(bf16[4,128,256]{2,1,0:T(8,128)(2,1)S(1)} %collective-permute-done.8), channel_id=1, source_target_pairs={{0,1},{1,0},{2,3},{3,2},{4,5},{5,4},{6,7},{7,6},{8,9},{9,8},{10,11... | collective-permute-start | bytes 786440 | tf_op jit(solution)/shard_map/ppermute | solution.py:15
  26.1 1.8 %collective-permute-start.9 = (bf16[1,256,256]{2,1,0:T(8,128)(2,1)S(1)}, bf16[1,256,256]{2,1,0:T(8,128)(2,1)S(1)}, u32[]{:S(2)}, u32[]{:S(2)}) collective-permute-start(bf16[1,256,256]{2,1,0:T(8,128)(2,1)S(1)} %maximum_bitcast_fusion), channel_id=1, source_target_pairs={{0,1},{1,0},{2,3},{3,2},{4,5},{5,4},{6,7},{7,6},{8,9},{9,8},{10,11... | collective-permute-start | bytes 393224 | tf_op jit(solution)/shard_map/ppermute | solution.py:15

commit v5 on v4

--- a/solution.py
+++ b/solution.py
@@ -49,7 +49,7 @@
     lane = lax.broadcasted_iota(jnp.int32, weight_ref.shape, 1) - (2 * place[0] + place[1]) * local_count
     weights = jnp.zeros(weight_ref.shape, jnp.float32)
     for k in range(local_count):
-        weights = jnp.where(lane == k, weight[k], weights)
+        weights = jnp.where(lane == k, weight[:, k : k + 1].astype(jnp.float32), weights)
     weight_ref[...] = weights
     own = (2 * place[0] + place[1]) * local_count + lax.broadcasted_iota(jnp.int32, below_ref.shape, 0)
     lane = lax.broadcasted_iota(jnp.int32, below_ref.shape, 1)
@@ -135,7 +135,6 @@
     heads = cotangent.shape[1]
     window = width * heads
     chip_width = width // chips
-    weight = example_weight.astype(jnp.float32)
 
     smem = pl.BlockSpec(memory_space=pltpu.SMEM)
     vmem = pl.BlockSpec(memory_space=pltpu.VMEM)
@@ -150,36 +149,37 @@
         return lax.dynamic_slice_in_dim(layer_input, (chip ^ distance) * chip_width, chip_width, 1)
 
     moved = swapped(jnp.stack([columns(2 * z + 1) for z in range(1, planes)]), 2)
-    moved, place, weight = lax.optimization_barrier((moved, place, weight))
+    moved, place = lax.optimization_barrier((moved, place))
     over_y = {z: moved[z - 1] for z in range(1, planes)}
     shapes = [array((chips * tokens, LANES), jnp.bfloat16)] * 2
     shapes += [array((LANES, planes * 8), jnp.bfloat16)] + [array((8, LANES), jnp.float32)] * 3
     order = pl.pallas_call(
         functools.partial(order_kernel, local_count, seq_length),
         out_shape=shapes,
-        in_specs=[smem] * 2,
+        in_specs=[smem, vmem],
         out_specs=[vmem] * len(shapes),
         compiler_params=params,
         name="order_kernel",
-    )(place, weight)
+    )(place, example_weight.reshape(1, local_count))
 
     mine = {}
     for z in range(planes - 1, 0, -1):
         part = jnp.concatenate([columns(2 * z), over_y[z]])
         if z == 1 and planes > 2:
             part, cot[planes - 1] = lax.optimization_barrier((part, cot[planes - 1]))
-        if z == 1:
-            part, order = lax.optimization_barrier((part, order))
         mine[z] = swapped(part, 4 * z)
     over_z = jnp.stack([cot[z] for z in range(planes)])
     over_zy = swapped(over_z, 2)
-    mine[0] = jnp.concatenate([columns(0), swapped(columns(1), 2)])
-    other_z, other_zy = swapped(over_z, 1), swapped(over_zy, 1)
+    other_z = swapped(over_z, 1)
+    late, order = lax.optimization_barrier((columns(1), order))
+    over_zy, other_z = lax.optimization_barrier((over_zy, other_z))
+    mine[0] = jnp.concatenate([columns(0), swapped(late, 2)])
+    other_zy = swapped(over_zy, 1)
     own_c = jnp.stack([over_z, over_zy], axis=1).reshape(planes, 2 * tokens, heads)
     far_c = jnp.stack([other_z, other_zy], axis=1).reshape(planes, 2 * tokens, heads)
     own_spread, far_spread, gather, weight_row, below, diagonal = order
     own_x = jnp.stack([mine[z] for z in range(planes)])
-    far_x = jnp.concatenate([swapped(own_x[:1], 1), swapped(own_x[1:], 1)])
+    far_x = swapped(own_x, 1)
 
     sums = [pltpu.VMEM((planes, 8, chips * tokens), jnp.float32)]
     own = pl.pallas_call(

time: 40.6 us -> 40 us (0.985)
  starting transfers between devices: 16 us -> 14.1 us
  blocking collectives: 10.5 us -> 12.1 us
  local copies, waits for them, and re-layouts: 1.87 us -> 1.22 us
  waiting for transfers between devices: 6.92 us -> 7.51 us
    ppermute x13 -> x12, starting transfers between devices: 16 us -> 14.1 us  [swapped(): return lax.ppermute(value, 'ex', [(i, i ^ distance) for i in range(count)])]
    all_to_all x1, blocking collectives: 10.5 us -> 12.1 us  [body(): lax.all_to_all(partial, 'ex', split_axis=0, concat_axis=0, tiled=True)]
    unnamed x4, local copies, waits for them, and re-layouts: 0.66 us -> 0.01 us
    ppermute x13 -> x12, waiting for transfers between devices: 6.92 us -> 7.51 us  [swapped(): return lax.ppermute(value, 'ex', [(i, i ^ distance) for i in range(count)])]
  transfers between devices with their start and end apart: 13 -> 12, of which waited for: 4 -> 6; matrix products, arithmetic and copies ran while one was open for 1% -> 1% of each run, Pallas kernels for 4% -> 5%
where the time goes in v5:
time: 40 us; the launch traced here: 39.8 us
  starting transfers between devices  14.1 us (35%)
  blocking collectives  12.1 us (30%)
  waiting for transfers between devices  7.51 us (19%)
  Pallas kernels  3.76 us (9%)
  local copies, waits for them, and re-layouts  1.22 us (3%)
  between operations  0.82 us (2%)
    ppermute x12, starting transfers between devices, swapped(): return lax.ppermute(value, 'ex', [(i, i ^ distance) for i in range(count)])  14.1 us
    all_to_all x1, blocking collectives, body(): lax.all_to_all(partial, 'ex', split_axis=0, concat_axis=0, tiled=True)  12.1 us
    ppermute x12, waiting for transfers between devices, swapped(): return lax.ppermute(value, 'ex', [(i, i ^ distance) for i in range(count)])  7.51 us
    pallas_call x1, Pallas kernels, body(): pl.pallas_call(functools.partial(far_kernel, seq_length, local_count), ou...  1.24 us
    pallas_call x1, Pallas kernels, body(): pl.pallas_call(functools.partial(own_kernel, seq_length), out_shape=array...  1.18 us
    dynamic_slice x1, local copies, waits for them, and re-layouts, columns(): lax.dynamic_slice_in_dim(layer_input, (chip ^ distance) * chip_width, chi...  1.12 us
  transfers between devices with their start and end apart: 12, of which 6 were waited for; matrix products, arithmetic and copies ran while one was open for 1% of the time, Pallas kernels for 5%

profile of v5, /device:TPU:0, one launch (start us, length us, event | category | flops | bytes accessed | tf_op | source)
XLA Modules:
  0.0 39.8 jit_solution(12446405094527359451)
XLA Ops:
  0.7 1.1 %constant_dynamic-slice_fusion.3 = (bf16[128,256]{1,0:T(8,128)(2,1)S(1)}, bf16[128,256]{1,0:T(8,128)(2,1)S(1)}, bf16[1,128,256]{2,1,0:T(8,128)(2,1)S(1)}, bf16[1...) fusion(bf16[128,2048]{1,0:T(8,128)(2,1)} %param.3, ...), kind=kLoop, calls=%fused_computation.18 | loop fusion | bytes 1048608 | tf_op jit(solution)/shard_map/dynamic_slice | solution.py:149
  1.8 0.0 copy-start.1
  1.9 3.0 %collective-permute-start = (bf16[3,128,256]{2,1,0:T(8,128)(2,1)S(1)}, bf16[3,128,256]{2,1,0:T(8,128)(2,1)S(1)}, u32[]{:S(2)}, u32[]{:S(2)}) collective-permute-start(bf16[3,128,256]{2,1,0:T(8,128)(2,1)S(1)} %pad_maximum_fusion.4), channel_id=1, source_target_pairs={{0,2},{1,3},{2,0},{3,1},{4,6},{5,7},{6,4},{7,5},{8,10},{9,11},{10,... | collective-permute-start | bytes 589832 | tf_op jit(solution)/shard_map/ppermute | solution.py:15
  4.9 0.0 copy-done.1
  4.9 3.6 %collective-permute-start.2 = (bf16[128,256]{1,0:T(8,128)(2,1)S(1)}, bf16[128,256]{1,0:T(8,128)(2,1)S(1)}, u32[]{:S(2)}, u32[]{:S(2)}) collective-permute-start(bf16[128,256]{1,0:T(8,128)(2,1)S(1)} %copy-done.1), channel_id=1, source_target_pairs={{0,12},{1,13},{2,14},{3,15},{4,8},{5,9},{6,10},{7,11},{8,4},{9,5},... | collective-permute-start | bytes 196616 | tf_op jit(solution)/shard_map/ppermute | solution.py:15
  8.5 0.0 collective-permute-start.7
  8.5 0.8 %collective-permute-start.6 = (bf16[128,256]{1,0:T(8,128)(2,1)S(1)}, bf16[128,256]{1,0:T(8,128)(2,1)S(1)}, u32[]{:S(2)}, u32[]{:S(2)}) collective-permute-start(bf16[128,256]{1,0:T(8,128)(2,1)S(1)} %copy-done.1), channel_id=1, source_target_pairs={{0,4},{1,5},{2,6},{3,7},{4,0},{5,1},{6,2},{7,3},{8,12},{9,13},{10,... | collective-permute-start | bytes 196616 | tf_op jit(solution)/shard_map/ppermute | solution.py:15
  9.3 0.1 pad_add_fusion.place
  9.4 0.4 %collective-permute-done = bf16[3,128,256]{2,1,0:T(8,128)(2,1)S(1)} collective-permute-done((bf16[3,128,256]{2,1,0:T(8,128)(2,1)S(1)}, bf16[3,128,256]{2,1,0:T(8,128)(2,1)S(1)}, u32[]{:S(2)}, u32[]{:S(2)}) %collective-permute-start) | collective-permute-done | bytes 196640 | tf_op jit(solution)/shard_map/ppermute | solution.py:15
  9.8 1.9 %collective-permute-done.2 = bf16[128,256]{1,0:T(8,128)(2,1)S(1)} collective-permute-done((bf16[128,256]{1,0:T(8,128)(2,1)S(1)}, bf16[128,256]{1,0:T(8,128)(2,1)S(1)}, u32[]{:S(2)}, u32[]{:S(2)}) %collective-permute-start.2) | collective-permute-done | bytes 65568 | tf_op jit(solution)/shard_map/ppermute | solution.py:15
  11.8 2.2 %collective-permute-start.4 = (bf16[256,256]{1,0:T(8,128)(2,1)S(1)}, bf16[256,256]{1,0:T(8,128)(2,1)S(1)}, u32[]{:S(2)}, u32[]{:S(2)}) collective-permute-start(bf16[256,256]{1,0:T(8,128)(2,1)S(1)} %pad_maximum_fusion.6), channel_id=1, source_target_pairs={{0,8},{1,9},{2,10},{3,11},{4,12},{5,13},{6,14},{7,15},{8,0},{9,1},... | collective-permute-start | bytes 393224 | tf_op jit(solution)/shard_map/ppermute | solution.py:15
  14.0 0.0 copy-start
  14.0 1.6 %collective-permute-start.5 = (bf16[256,256]{1,0:T(8,128)(2,1)S(1)}, bf16[256,256]{1,0:T(8,128)(2,1)S(1)}, u32[]{:S(2)}, u32[]{:S(2)}) collective-permute-start(bf16[256,256]{1,0:T(8,128)(2,1)S(1)} %pad_maximum_fusion.7), channel_id=1, source_target_pairs={{0,12},{1,13},{2,14},{3,15},{4,8},{5,9},{6,10},{7,11},{8,4},{9,5},... | collective-permute-start | bytes 393224 | tf_op jit(solution)/shard_map/ppermute | solution.py:15
  15.6 0.6 %collective-permute-start.3 = (bf16[256,256]{1,0:T(8,128)(2,1)S(1)}, bf16[256,256]{1,0:T(8,128)(2,1)S(1)}, u32[]{:S(2)}, u32[]{:S(2)}) collective-permute-start(bf16[256,256]{1,0:T(8,128)(2,1)S(1)} %pad_maximum_fusion.5), channel_id=1, source_target_pairs={{0,4},{1,5},{2,6},{3,7},{4,0},{5,1},{6,2},{7,3},{8,12},{9,13},{10,... | collective-permute-start | bytes 393224 | tf_op jit(solution)/shard_map/ppermute | solution.py:15
  16.2 0.0 copy-done
  16.2 0.6 %order_kernel.1 = (bf16[1024,128]{1,0:T(8,128)(2,1)S(1)}, bf16[1024,128]{1,0:T(8,128)(2,1)S(1)}, bf16[128,32]{1,0:T(8,128)(2,1)S(1)}, f32[8,128]{1,0:T(8,128)S(1...) custom-call(s32[2]{0:T(128)S(1)} %pad_add_fusion.place, bf16[1,2]{1,0:T(2,128)(2,1)S(1)} %bitcast.35), custom_call_target="tpu_custom_call" | custom-call | tf_op jit(solution)/shard_map/order_kernel/pallas_call | solution.py:156
  16.9 0.0 collective-permute-done.7
  16.9 0.7 %collective-permute-start.1 = (bf16[128,256]{1,0:T(8,128)(2,1)S(1)}, bf16[128,256]{1,0:T(8,128)(2,1)S(1)}, u32[]{:S(2)}, u32[]{:S(2)}) collective-permute-start(bf16[128,256]{1,0:T(8,128)(2,1)S(1)} %get-tuple-element.32), channel_id=1, source_target_pairs={{0,2},{1,3},{2,0},{3,1},{4,6},{5,7},{6,4},{7,5},{8,10},{9,11},{10,... | collective-permute-start | bytes 196616 | tf_op jit(solution)/shard_map/ppermute | solution.py:15
  17.5 0.0 collective-permute-done.6
  17.6 1.5 %collective-permute-start.8 = (bf16[4,128,256]{2,1,0:T(8,128)(2,1)S(1)}, bf16[4,128,256]{2,1,0:T(8,128)(2,1)S(1)}, u32[]{:S(2)}, u32[]{:S(2)}) collective-permute-start(bf16[4,128,256]{2,1,0:T(8,128)(2,1)S(1)} %get-tuple-element.53), channel_id=1, source_target_pairs={{0,2},{1,3},{2,0},{3,1},{4,6},{5,7},{6,4},{7,5},{8,10},{9,11},{10,... | collective-permute-start | bytes 786440 | tf_op jit(solution)/shard_map/ppermute | solution.py:15
  19.1 2.1 %collective-permute-done.1 = bf16[128,256]{1,0:T(8,128)(2,1)S(1)} collective-permute-done((bf16[128,256]{1,0:T(8,128)(2,1)S(1)}, bf16[128,256]{1,0:T(8,128)(2,1)S(1)}, u32[]{:S(2)}, u32[]{:S(2)}) %collective-permute-start.1) | collective-permute-done | bytes 65568 | tf_op jit(solution)/shard_map/ppermute | solution.py:15
  21.2 0.0 collective-permute-start.9
  21.2 2.0 %collective-permute-done.4 = bf16[256,256]{1,0:T(8,128)(2,1)S(1)} collective-permute-done((bf16[256,256]{1,0:T(8,128)(2,1)S(1)}, bf16[256,256]{1,0:T(8,128)(2,1)S(1)}, u32[]{:S(2)}, u32[]{:S(2)}) %collective-permute-start.4) | collective-permute-done | bytes 131104 | tf_op jit(solution)/shard_map/ppermute | solution.py:15
  23.2 0.0 collective-permute-done.5
  23.2 0.0 collective-permute-done.3
  23.3 0.1 pad_maximum_fusion.x_ref
  23.3 0.1 collective-permute-start.10
  23.4 0.6 %collective-permute-done.8 = bf16[4,128,256]{2,1,0:T(8,128)(2,1)S(1)} collective-permute-done((bf16[4,128,256]{2,1,0:T(8,128)(2,1)S(1)}, bf16[4,128,256]{2,1,0:T(8,128)(2,1)S(1)}, u32[]{:S(2)}, u32[]{:S(2)}) %collective-permute-start.8) | collective-permute-done | bytes 262176 | tf_op jit(solution)/shard_map/ppermute | solution.py:15
  24.0 0.0 collective-permute-done.9
  24.0 0.0 collective-permute-start.11
  24.0 0.1 pad_maximum_fusion.1
  24.1 1.2 %own_kernel.1.own_ref = f32[128,128]{1,0:T(8,128)S(1)} custom-call(bf16[4,256,256]{2,1,0:T(8,128)(2,1)S(1)} %pad_maximum_fusion.x_ref, bf16[4,256,256]{2,1,0:T(8,128)(2,1)S(1)} %bitcast.32, bf16[1024,128]{1,0:T(8,128)(2,1)S(1)} %get-tuple-element.41.spread, bf16[128,32]{1,0:T(8,128)(2,1)S(1)} %get-tuple-element.39.gather), custom_call_target="tpu_custom_call" | custom-call | tf_op jit(solution)/shard_map/own_kernel/pallas_call | solution.py:185
  25.3 0.4 collective-permute-done.11
  25.7 0.1 pad_maximum_fusion.2
  25.8 0.0 collective-permute-done.10.far_x
  25.8 1.2 %far_kernel.1 = f32[16,4,128]{2,1,0:T(4,128)S(1)} custom-call(bf16[4,256,256]{2,1,0:T(8,128)(2,1)S(1)} %pad_maximum_fusion.x_ref, bf16[4,256,256]{2,1,0:T(8,128)(2,1)S(1)} %bitcast.33, bf16[4,256,256]{2,1,0:T(8,128)(2,1)S(1)} %collective-permute-done.10.far_x, bf16[4,256,256]{2,1,0:T(8,128)(2,1)S(1)} %bitcast.34, ...), custom_call_target="tpu_custom_call" | custom-call | tf_op jit(solution)/shard_map/far_kernel/pallas_call | solution.py:194
  27.0 12.1 %all_to_all.5.sums_ref = f32[16,4,128]{2,1,0:T(4,128)S(1)} all-to-all(f32[16,4,128]{2,1,0:T(4,128)S(1)} %far_kernel.1), channel_id=1, replica_groups=mesh['grp'=2,'ex'=16] {'ex'}, dimensions={0} | all-to-all | bytes 65536 | tf_op jit(solution)/shard_map/all_to_all | solution.py:204
  39.1 0.7 %output_kernel.1 = (f32[2,32]{1,0:T(2,128)}, f32[1,2]{1,0:T(1,128)}) custom-call(f32[8,128]{1,0:T(8,128)S(1)} %get-tuple-element.30.below, f32[8,128]{1,0:T(8,128)S(1)} %get-tuple-element.31.diagonal, f32[16,4,128]{2,1,0:T(4,128)S(1)} %all_to_all.5.sums_ref), custom_call_target="tpu_custom_call" | custom-call | tf_op jit(solution)/shard_map/output_kernel/pallas_call | solution.py:207
  (9 shorter events, 0.2 us)
Async XLA Ops:
  1.8 3.1 %copy-start.1 = (bf16[128,256]{1,0:T(8,128)(2,1)S(1)}, bf16[128,256]{1,0:T(8,128)(2,1)}, u32[]{:S(2)}) copy-start(bf16[128,256]{1,0:T(8,128)(2,1)} %param.4) | copy-start | bytes 196612
  1.9 7.9 %collective-permute-start = (bf16[3,128,256]{2,1,0:T(8,128)(2,1)S(1)}, bf16[3,128,256]{2,1,0:T(8,128)(2,1)S(1)}, u32[]{:S(2)}, u32[]{:S(2)}) collective-permute-start(bf16[3,128,256]{2,1,0:T(8,128)(2,1)S(1)} %pad_maximum_fusion.4), channel_id=1, source_target_pairs={{0,2},{1,3},{2,0},{3,1},{4,6},{5,7},{6,4},{7,5},{8,10},{9,11},{10,... | collective-permute-start | bytes 589832 | tf_op jit(solution)/shard_map/ppermute | solution.py:15
  4.9 6.9 %collective-permute-start.2 = (bf16[128,256]{1,0:T(8,128)(2,1)S(1)}, bf16[128,256]{1,0:T(8,128)(2,1)S(1)}, u32[]{:S(2)}, u32[]{:S(2)}) collective-permute-start(bf16[128,256]{1,0:T(8,128)(2,1)S(1)} %copy-done.1), channel_id=1, source_target_pairs={{0,12},{1,13},{2,14},{3,15},{4,8},{5,9},{6,10},{7,11},{8,4},{9,5},... | collective-permute-start | bytes 196616 | tf_op jit(solution)/shard_map/ppermute | solution.py:15
  8.5 8.4 %collective-permute-start.7 = (bf16[128,256]{1,0:T(8,128)(2,1)S(1)}, bf16[128,256]{1,0:T(8,128)(2,1)S(1)}, u32[]{:S(2)}, u32[]{:S(2)}) collective-permute-start(bf16[128,256]{1,0:T(8,128)(2,1)S(1)} %copy-done.1), channel_id=1, source_target_pairs={{0,8},{1,9},{2,10},{3,11},{4,12},{5,13},{6,14},{7,15},{8,0},{9,1},... | collective-permute-start | bytes 196616 | tf_op jit(solution)/shard_map/ppermute | solution.py:15
  8.5 9.1 %collective-permute-start.6 = (bf16[128,256]{1,0:T(8,128)(2,1)S(1)}, bf16[128,256]{1,0:T(8,128)(2,1)S(1)}, u32[]{:S(2)}, u32[]{:S(2)}) collective-permute-start(bf16[128,256]{1,0:T(8,128)(2,1)S(1)} %copy-done.1), channel_id=1, source_target_pairs={{0,4},{1,5},{2,6},{3,7},{4,0},{5,1},{6,2},{7,3},{8,12},{9,13},{10,... | collective-permute-start | bytes 196616 | tf_op jit(solution)/shard_map/ppermute | solution.py:15
  11.8 11.5 %collective-permute-start.4 = (bf16[256,256]{1,0:T(8,128)(2,1)S(1)}, bf16[256,256]{1,0:T(8,128)(2,1)S(1)}, u32[]{:S(2)}, u32[]{:S(2)}) collective-permute-start(bf16[256,256]{1,0:T(8,128)(2,1)S(1)} %pad_maximum_fusion.6), channel_id=1, source_target_pairs={{0,8},{1,9},{2,10},{3,11},{4,12},{5,13},{6,14},{7,15},{8,0},{9,1},... | collective-permute-start | bytes 393224 | tf_op jit(solution)/shard_map/ppermute | solution.py:15
  14.0 2.2 %copy-start = (bf16[2]{0:T(256)(128)(2,1)S(1)}, bf16[2]{0:T(256)(128)(2,1)}, u32[]{:S(2)}) copy-start(bf16[2]{0:T(256)(128)(2,1)} %param.5) | copy-start | bytes 16
  14.0 9.3 %collective-permute-start.5 = (bf16[256,256]{1,0:T(8,128)(2,1)S(1)}, bf16[256,256]{1,0:T(8,128)(2,1)S(1)}, u32[]{:S(2)}, u32[]{:S(2)}) collective-permute-start(bf16[256,256]{1,0:T(8,128)(2,1)S(1)} %pad_maximum_fusion.7), channel_id=1, source_target_pairs={{0,12},{1,13},{2,14},{3,15},{4,8},{5,9},{6,10},{7,11},{8,4},{9,5},... | collective-permute-start | bytes 393224 | tf_op jit(solution)/shard_map/ppermute | solution.py:15
  15.6 7.7 %collective-permute-start.3 = (bf16[256,256]{1,0:T(8,128)(2,1)S(1)}, bf16[256,256]{1,0:T(8,128)(2,1)S(1)}, u32[]{:S(2)}, u32[]{:S(2)}) collective-permute-start(bf16[256,256]{1,0:T(8,128)(2,1)S(1)} %pad_maximum_fusion.5), channel_id=1, source_target_pairs={{0,4},{1,5},{2,6},{3,7},{4,0},{5,1},{6,2},{7,3},{8,12},{9,13},{10,... | collective-permute-start | bytes 393224 | tf_op jit(solution)/shard_map/ppermute | solution.py:15
  16.9 4.3 %collective-permute-start.1 = (bf16[128,256]{1,0:T(8,128)(2,1)S(1)}, bf16[128,256]{1,0:T(8,128)(2,1)S(1)}, u32[]{:S(2)}, u32[]{:S(2)}) collective-permute-start(bf16[128,256]{1,0:T(8,128)(2,1)S(1)} %get-tuple-element.32), channel_id=1, source_target_pairs={{0,2},{1,3},{2,0},{3,1},{4,6},{5,7},{6,4},{7,5},{8,10},{9,11},{10,... | collective-permute-start | bytes 196616 | tf_op jit(solution)/shard_map/ppermute | solution.py:15
  17.6 6.4 %collective-permute-start.8 = (bf16[4,128,256]{2,1,0:T(8,128)(2,1)S(1)}, bf16[4,128,256]{2,1,0:T(8,128)(2,1)S(1)}, u32[]{:S(2)}, u32[]{:S(2)}) collective-permute-start(bf16[4,128,256]{2,1,0:T(8,128)(2,1)S(1)} %get-tuple-element.53), channel_id=1, source_target_pairs={{0,2},{1,3},{2,0},{3,1},{4,6},{5,7},{6,4},{7,5},{8,10},{9,11},{10,... | collective-permute-start | bytes 786440 | tf_op jit(solution)/shard_map/ppermute | solution.py:15
  21.2 2.8 %collective-permute-start.9 = (bf16[4,128,256]{2,1,0:T(8,128)(2,1)S(1)}, bf16[4,128,256]{2,1,0:T(8,128)(2,1)S(1)}, u32[]{:S(2)}, u32[]{:S(2)}) collective-permute-start(bf16[4,128,256]{2,1,0:T(8,128)(2,1)S(1)} %get-tuple-element.53), channel_id=1, source_target_pairs={{0,1},{1,0},{2,3},{3,2},{4,5},{5,4},{6,7},{7,6},{8,9},{9,8},{10,11... | collective-permute-start | bytes 786440 | tf_op jit(solution)/shard_map/ppermute | solution.py:15
  23.3 2.5 %collective-permute-start.10 = (bf16[4,256,256]{2,1,0:T(8,128)(2,1)S(1)}, bf16[4,256,256]{2,1,0:T(8,128)(2,1)S(1)}, u32[]{:S(2)}, u32[]{:S(2)}) collective-permute-start(bf16[4,256,256]{2,1,0:T(8,128)(2,1)S(1)} %pad_maximum_fusion.x_ref), channel_id=1, source_target_pairs={{0,1},{1,0},{2,3},{3,2},{4,5},{5,4},{6,7},{7,6},{8,9},{9,8},{10,11... | collective-permute-start | bytes 1572872 | tf_op jit(solution)/shard_map/ppermute | solution.py:15
  24.0 1.7 %collective-permute-start.11 = (bf16[4,128,256]{2,1,0:T(8,128)(2,1)S(1)}, bf16[4,128,256]{2,1,0:T(8,128)(2,1)S(1)}, u32[]{:S(2)}, u32[]{:S(2)}) collective-permute-start(bf16[4,128,256]{2,1,0:T(8,128)(2,1)S(1)} %collective-permute-done.8), channel_id=1, source_target_pairs={{0,1},{1,0},{2,3},{3,2},{4,5},{5,4},{6,7},{7,6},{8,9},{9,8},{10,11... | collective-permute-start | bytes 786440 | tf_op jit(solution)/shard_map/ppermute | solution.py:15

commit v6 on v5

--- a/solution.py
+++ b/solution.py
@@ -49,7 +49,7 @@
     lane = lax.broadcasted_iota(jnp.int32, weight_ref.shape, 1) - (2 * place[0] + place[1]) * local_count
     weights = jnp.zeros(weight_ref.shape, jnp.float32)
     for k in range(local_count):
-        weights = jnp.where(lane == k, weight[:, k : k + 1].astype(jnp.float32), weights)
+        weights = jnp.where(lane == k, weight[k], weights)
     weight_ref[...] = weights
     own = (2 * place[0] + place[1]) * local_count + lax.broadcasted_iota(jnp.int32, below_ref.shape, 0)
     lane = lax.broadcasted_iota(jnp.int32, below_ref.shape, 1)
@@ -135,6 +135,7 @@
     heads = cotangent.shape[1]
     window = width * heads
     chip_width = width // chips
+    weight = example_weight.astype(jnp.float32)
 
     smem = pl.BlockSpec(memory_space=pltpu.SMEM)
     vmem = pl.BlockSpec(memory_space=pltpu.VMEM)
@@ -149,18 +150,18 @@
         return lax.dynamic_slice_in_dim(layer_input, (chip ^ distance) * chip_width, chip_width, 1)
 
     moved = swapped(jnp.stack([columns(2 * z + 1) for z in range(1, planes)]), 2)
-    moved, place = lax.optimization_barrier((moved, place))
+    moved, place, weight = lax.optimization_barrier((moved, place, weight))
     over_y = {z: moved[z - 1] for z in range(1, planes)}
     shapes = [array((chips * tokens, LANES), jnp.bfloat16)] * 2
     shapes += [array((LANES, planes * 8), jnp.bfloat16)] + [array((8, LANES), jnp.float32)] * 3
     order = pl.pallas_call(
         functools.partial(order_kernel, local_count, seq_length),
         out_shape=shapes,
-        in_specs=[smem, vmem],
+        in_specs=[smem] * 2,
         out_specs=[vmem] * len(shapes),
         compiler_params=params,
         name="order_kernel",
-    )(place, example_weight.reshape(1, local_count))
+    )(place, weight)
 
     mine = {}
     for z in range(planes - 1, 0, -1):
@@ -171,7 +172,7 @@
     over_z = jnp.stack([cot[z] for z in range(planes)])
     over_zy = swapped(over_z, 2)
     other_z = swapped(over_z, 1)
-    late, order = lax.optimization_barrier((columns(1), order))
+    late, order, cot[1] = lax.optimization_barrier((columns(1), order, cot[1]))
     over_zy, other_z = lax.optimization_barrier((over_zy, other_z))
     mine[0] = jnp.concatenate([columns(0), swapped(late, 2)])
     other_zy = swapped(over_zy, 1)
@@ -189,6 +190,7 @@
         out_specs=vmem,
         scratch_shapes=sums,
         compiler_params=params,
+        cost_estimate=pl.CostEstimate(flops=1, bytes_accessed=0, transcendentals=0),
         name="own_kernel",
     )(own_x, own_c, own_spread, gather)
     partial = pl.pallas_call(
@@ -198,6 +200,7 @@
         out_specs=vmem,
         scratch_shapes=sums,
         compiler_params=params,
+        cost_estimate=pl.CostEstimate(flops=1, bytes_accessed=0, transcendentals=0),
         name="far_kernel",
     )(own_x, own_c, far_x, far_c, far_spread, gather, weight_row, own)
 

time: 40 us -> 40 us (level)
  blocking collectives: 12.1 us -> 10.6 us
  local copies, waits for them, and re-layouts: 1.22 us -> 1.87 us
  starting transfers between devices: 14.1 us -> 14.7 us
    all_to_all x1, blocking collectives: 12.1 us -> 10.6 us  [body(): lax.all_to_all(partial, 'ex', split_axis=0, concat_axis=0, tiled=True)]
    unnamed x4, local copies, waits for them, and re-layouts: 0.01 us -> 0.66 us
    ppermute x12, starting transfers between devices: 14.1 us -> 14.7 us  [swapped(): return lax.ppermute(value, 'ex', [(i, i ^ distance) for i in range(count)])]
  transfers between devices with their start and end apart: 12 -> 12, of which waited for: 6 -> 7; matrix products, arithmetic and copies ran while one was open for 1% -> 1% of each run, Pallas kernels for 5% -> 4%
where the time goes in v6:
time: 40 us; the launch traced here: 39.8 us
  starting transfers between devices  14.7 us (37%)
  blocking collectives  10.6 us (26%)
  waiting for transfers between devices  7.71 us (19%)
  Pallas kernels  3.7 us (9%)
  local copies, waits for them, and re-layouts  1.87 us (5%)
  between operations  0.81 us (2%)
    ppermute x12, starting transfers between devices, swapped(): return lax.ppermute(value, 'ex', [(i, i ^ distance) for i in range(count)])  14.7 us
    all_to_all x1, blocking collectives, body(): lax.all_to_all(partial, 'ex', split_axis=0, concat_axis=0, tiled=True)  10.6 us
    ppermute x12, waiting for transfers between devices, swapped(): return lax.ppermute(value, 'ex', [(i, i ^ distance) for i in range(count)])  7.71 us
    pallas_call x1, Pallas kernels, body(): pl.pallas_call(functools.partial(far_kernel, seq_length, local_count), ou...  1.24 us
    pallas_call x1, Pallas kernels, body(): pl.pallas_call(functools.partial(own_kernel, seq_length), out_shape=array...  1.18 us
    dynamic_slice x1, local copies, waits for them, and re-layouts, columns(): lax.dynamic_slice_in_dim(layer_input, (chip ^ distance) * chip_width, chi...  1.12 us
  transfers between devices with their start and end apart: 12, of which 7 were waited for; matrix products, arithmetic and copies ran while one was open for 1% of the time, Pallas kernels for 4%

profile of v6, /device:TPU:0, one launch (start us, length us, event | category | flops | bytes accessed | tf_op | source)
XLA Modules:
  0.0 39.8 jit_solution(361227951886329212)
XLA Ops:
  0.7 1.1 %constant_dynamic-slice_fusion.3 = (bf16[128,256]{1,0:T(8,128)(2,1)S(1)}, bf16[128,256]{1,0:T(8,128)(2,1)S(1)}, bf16[1,128,256]{2,1,0:T(8,128)(2,1)S(1)}, bf16[1...) fusion(bf16[128,2048]{1,0:T(8,128)(2,1)} %param.3, ...), kind=kLoop, calls=%fused_computation.18 | loop fusion | bytes 1048608 | tf_op jit(solution)/shard_map/dynamic_slice | solution.py:150
  1.8 0.0 copy-start
  1.9 3.0 %collective-permute-start = (bf16[3,128,256]{2,1,0:T(8,128)(2,1)S(1)}, bf16[3,128,256]{2,1,0:T(8,128)(2,1)S(1)}, u32[]{:S(2)}, u32[]{:S(2)}) collective-permute-start(bf16[3,128,256]{2,1,0:T(8,128)(2,1)S(1)} %pad_maximum_fusion.4), channel_id=1, source_target_pairs={{0,2},{1,3},{2,0},{3,1},{4,6},{5,7},{6,4},{7,5},{8,10},{9,11},{10,... | collective-permute-start | bytes 589832 | tf_op jit(solution)/shard_map/ppermute | solution.py:15
  4.9 0.0 copy-done
  4.9 3.6 %collective-permute-start.3 = (bf16[128,256]{1,0:T(8,128)(2,1)S(1)}, bf16[128,256]{1,0:T(8,128)(2,1)S(1)}, u32[]{:S(2)}, u32[]{:S(2)}) collective-permute-start(bf16[128,256]{1,0:T(8,128)(2,1)S(1)} %copy-done), channel_id=1, source_target_pairs={{0,12},{1,13},{2,14},{3,15},{4,8},{5,9},{6,10},{7,11},{8,4},{9,5},... | collective-permute-start | bytes 196616 | tf_op jit(solution)/shard_map/ppermute | solution.py:15
  8.5 0.0 collective-permute-start.1
  8.5 0.8 %collective-permute-start.7 = (bf16[128,256]{1,0:T(8,128)(2,1)S(1)}, bf16[128,256]{1,0:T(8,128)(2,1)S(1)}, u32[]{:S(2)}, u32[]{:S(2)}) collective-permute-start(bf16[128,256]{1,0:T(8,128)(2,1)S(1)} %copy-done), channel_id=1, source_target_pairs={{0,8},{1,9},{2,10},{3,11},{4,12},{5,13},{6,14},{7,15},{8,0},{9,1},... | collective-permute-start | bytes 196616 | tf_op jit(solution)/shard_map/ppermute | solution.py:15
  9.3 0.0 copy-start.1
  9.3 0.7 %copy-done.1 = bf16[2]{0:T(256)(128)(2,1)S(1)} copy-done((bf16[2]{0:T(256)(128)(2,1)S(1)}, bf16[2]{0:T(256)(128)(2,1)}, u32[]{:S(2)}) %copy-start.1) | copy-done | bytes 28
  9.9 0.1 pad_add_fusion.place
  10.0 0.0 collective-permute-done
  10.1 1.0 %collective-permute-done.3 = bf16[128,256]{1,0:T(8,128)(2,1)S(1)} collective-permute-done((bf16[128,256]{1,0:T(8,128)(2,1)S(1)}, bf16[128,256]{1,0:T(8,128)(2,1)S(1)}, u32[]{:S(2)}, u32[]{:S(2)}) %collective-permute-start.3) | collective-permute-done | bytes 65568 | tf_op jit(solution)/shard_map/ppermute | solution.py:15
  11.1 1.6 %collective-permute-start.5 = (bf16[256,256]{1,0:T(8,128)(2,1)S(1)}, bf16[256,256]{1,0:T(8,128)(2,1)S(1)}, u32[]{:S(2)}, u32[]{:S(2)}) collective-permute-start(bf16[256,256]{1,0:T(8,128)(2,1)S(1)} %pad_maximum_fusion.6), channel_id=1, source_target_pairs={{0,8},{1,9},{2,10},{3,11},{4,12},{5,13},{6,14},{7,15},{8,0},{9,1},... | collective-permute-start | bytes 393224 | tf_op jit(solution)/shard_map/ppermute | solution.py:15
  12.7 2.8 %collective-permute-start.6 = (bf16[256,256]{1,0:T(8,128)(2,1)S(1)}, bf16[256,256]{1,0:T(8,128)(2,1)S(1)}, u32[]{:S(2)}, u32[]{:S(2)}) collective-permute-start(bf16[256,256]{1,0:T(8,128)(2,1)S(1)} %pad_maximum_fusion.7), channel_id=1, source_target_pairs={{0,12},{1,13},{2,14},{3,15},{4,8},{5,9},{6,10},{7,11},{8,4},{9,5},... | collective-permute-start | bytes 393224 | tf_op jit(solution)/shard_map/ppermute | solution.py:15
  15.5 0.6 %collective-permute-start.4 = (bf16[256,256]{1,0:T(8,128)(2,1)S(1)}, bf16[256,256]{1,0:T(8,128)(2,1)S(1)}, u32[]{:S(2)}, u32[]{:S(2)}) collective-permute-start(bf16[256,256]{1,0:T(8,128)(2,1)S(1)} %pad_maximum_fusion.5), channel_id=1, source_target_pairs={{0,4},{1,5},{2,6},{3,7},{4,0},{5,1},{6,2},{7,3},{8,12},{9,13},{10,... | collective-permute-start | bytes 393224 | tf_op jit(solution)/shard_map/ppermute | solution.py:15
  16.2 0.6 %order_kernel.1 = (bf16[1024,128]{1,0:T(8,128)(2,1)S(1)}, bf16[1024,128]{1,0:T(8,128)(2,1)S(1)}, bf16[128,32]{1,0:T(8,128)(2,1)S(1)}, f32[8,128]{1,0:T(8,128)S(1...) custom-call(s32[2]{0:T(128)S(1)} %pad_add_fusion.place, f32[2]{0:T(128)S(1)} %convert_element_type.3.weight), custom_call_target="tpu_custom_call" | custom-call | tf_op jit(solution)/shard_map/order_kernel/pallas_call | solution.py:157
  16.7 0.0 collective-permute-done.1
  16.8 0.7 %collective-permute-start.2 = (bf16[128,256]{1,0:T(8,128)(2,1)S(1)}, bf16[128,256]{1,0:T(8,128)(2,1)S(1)}, u32[]{:S(2)}, u32[]{:S(2)}) collective-permute-start(bf16[128,256]{1,0:T(8,128)(2,1)S(1)} %get-tuple-element.34), channel_id=1, source_target_pairs={{0,2},{1,3},{2,0},{3,1},{4,6},{5,7},{6,4},{7,5},{8,10},{9,11},{10,... | collective-permute-start | bytes 196616 | tf_op jit(solution)/shard_map/ppermute | solution.py:15
  17.5 1.6 %collective-permute-done.7 = bf16[128,256]{1,0:T(8,128)(2,1)S(1)} collective-permute-done((bf16[128,256]{1,0:T(8,128)(2,1)S(1)}, bf16[128,256]{1,0:T(8,128)(2,1)S(1)}, u32[]{:S(2)}, u32[]{:S(2)}) %collective-permute-start.7) | collective-permute-done | bytes 65568 | tf_op jit(solution)/shard_map/ppermute | solution.py:15
  19.1 1.4 %collective-permute-start.8 = (bf16[4,128,256]{2,1,0:T(8,128)(2,1)S(1)}, bf16[4,128,256]{2,1,0:T(8,128)(2,1)S(1)}, u32[]{:S(2)}, u32[]{:S(2)}) collective-permute-start(bf16[4,128,256]{2,1,0:T(8,128)(2,1)S(1)} %get-tuple-element.55), channel_id=1, source_target_pairs={{0,2},{1,3},{2,0},{3,1},{4,6},{5,7},{6,4},{7,5},{8,10},{9,11},{10,... | collective-permute-start | bytes 786440 | tf_op jit(solution)/shard_map/ppermute | solution.py:15
  20.6 0.5 %collective-permute-done.2 = bf16[128,256]{1,0:T(8,128)(2,1)S(1)} collective-permute-done((bf16[128,256]{1,0:T(8,128)(2,1)S(1)}, bf16[128,256]{1,0:T(8,128)(2,1)S(1)}, u32[]{:S(2)}, u32[]{:S(2)}) %collective-permute-start.2) | collective-permute-done | bytes 65568 | tf_op jit(solution)/shard_map/ppermute | solution.py:15
  21.1 0.0 collective-permute-start.9
  21.1 2.6 %collective-permute-done.5 = bf16[256,256]{1,0:T(8,128)(2,1)S(1)} collective-permute-done((bf16[256,256]{1,0:T(8,128)(2,1)S(1)}, bf16[256,256]{1,0:T(8,128)(2,1)S(1)}, u32[]{:S(2)}, u32[]{:S(2)}) %collective-permute-start.5) | collective-permute-done | bytes 131104 | tf_op jit(solution)/shard_map/ppermute | solution.py:15
  23.7 0.0 collective-permute-done.6
  23.7 0.3 collective-permute-done.4
  24.0 0.1 pad_maximum_fusion.x_ref
  24.1 0.1 collective-permute-start.10
  24.2 1.4 %collective-permute-done.8 = bf16[4,128,256]{2,1,0:T(8,128)(2,1)S(1)} collective-permute-done((bf16[4,128,256]{2,1,0:T(8,128)(2,1)S(1)}, bf16[4,128,256]{2,1,0:T(8,128)(2,1)S(1)}, u32[]{:S(2)}, u32[]{:S(2)}) %collective-permute-start.8) | collective-permute-done | bytes 262176 | tf_op jit(solution)/shard_map/ppermute | solution.py:15
  25.6 0.0 collective-permute-done.9
  25.6 0.0 collective-permute-start.11
  25.6 0.1 pad_maximum_fusion.1
  25.7 1.2 %own_kernel.1.own_ref = f32[128,128]{1,0:T(8,128)S(1)} custom-call(bf16[4,256,256]{2,1,0:T(8,128)(2,1)S(1)} %pad_maximum_fusion.x_ref, bf16[4,256,256]{2,1,0:T(8,128)(2,1)S(1)} %bitcast.31, bf16[1024,128]{1,0:T(8,128)(2,1)S(1)} %get-tuple-element.43.spread, bf16[128,32]{1,0:T(8,128)(2,1)S(1)} %get-tuple-element.41.gather), custom_call_target="tpu_custom_call" | custom-call | flops 1 | tf_op jit(solution)/shard_map/own_kernel/pallas_call | solution.py:186
  26.8 0.3 collective-permute-done.11
  27.1 0.1 pad_maximum_fusion.2
  27.2 0.0 collective-permute-done.10.far_x
  27.2 1.2 %far_kernel.1 = f32[16,4,128]{2,1,0:T(4,128)S(1)} custom-call(bf16[4,256,256]{2,1,0:T(8,128)(2,1)S(1)} %pad_maximum_fusion.x_ref, bf16[4,256,256]{2,1,0:T(8,128)(2,1)S(1)} %bitcast.32, bf16[4,256,256]{2,1,0:T(8,128)(2,1)S(1)} %collective-permute-done.10.far_x, bf16[4,256,256]{2,1,0:T(8,128)(2,1)S(1)} %bitcast.33, ...), custom_call_target="tpu_custom_call" | custom-call | flops 1 | tf_op jit(solution)/shard_map/far_kernel/pallas_call | solution.py:196
  28.4 10.6 %all_to_all.5.sums_ref = f32[16,4,128]{2,1,0:T(4,128)S(1)} all-to-all(f32[16,4,128]{2,1,0:T(4,128)S(1)} %far_kernel.1), channel_id=1, replica_groups=mesh['grp'=2,'ex'=16] {'ex'}, dimensions={0} | all-to-all | bytes 65536 | tf_op jit(solution)/shard_map/all_to_all | solution.py:207
  39.1 0.7 %output_kernel.1 = (f32[2,32]{1,0:T(2,128)}, f32[1,2]{1,0:T(1,128)}) custom-call(f32[8,128]{1,0:T(8,128)S(1)} %get-tuple-element.32.below, f32[8,128]{1,0:T(8,128)S(1)} %get-tuple-element.33.diagonal, f32[16,4,128]{2,1,0:T(4,128)S(1)} %all_to_all.5.sums_ref), custom_call_target="tpu_custom_call" | custom-call | tf_op jit(solution)/shard_map/output_kernel/pallas_call | solution.py:210
  (10 shorter events, 0.2 us)
Async XLA Ops:
  1.8 3.1 %copy-start = (bf16[128,256]{1,0:T(8,128)(2,1)S(1)}, bf16[128,256]{1,0:T(8,128)(2,1)}, u32[]{:S(2)}) copy-start(bf16[128,256]{1,0:T(8,128)(2,1)} %param.4) | copy-start | bytes 196612
  1.9 8.2 %collective-permute-start = (bf16[3,128,256]{2,1,0:T(8,128)(2,1)S(1)}, bf16[3,128,256]{2,1,0:T(8,128)(2,1)S(1)}, u32[]{:S(2)}, u32[]{:S(2)}) collective-permute-start(bf16[3,128,256]{2,1,0:T(8,128)(2,1)S(1)} %pad_maximum_fusion.4), channel_id=1, source_target_pairs={{0,2},{1,3},{2,0},{3,1},{4,6},{5,7},{6,4},{7,5},{8,10},{9,11},{10,... | collective-permute-start | bytes 589832 | tf_op jit(solution)/shard_map/ppermute | solution.py:15
  4.9 6.2 %collective-permute-start.3 = (bf16[128,256]{1,0:T(8,128)(2,1)S(1)}, bf16[128,256]{1,0:T(8,128)(2,1)S(1)}, u32[]{:S(2)}, u32[]{:S(2)}) collective-permute-start(bf16[128,256]{1,0:T(8,128)(2,1)S(1)} %copy-done), channel_id=1, source_target_pairs={{0,12},{1,13},{2,14},{3,15},{4,8},{5,9},{6,10},{7,11},{8,4},{9,5},... | collective-permute-start | bytes 196616 | tf_op jit(solution)/shard_map/ppermute | solution.py:15
  8.5 8.3 %collective-permute-start.1 = (bf16[128,256]{1,0:T(8,128)(2,1)S(1)}, bf16[128,256]{1,0:T(8,128)(2,1)S(1)}, u32[]{:S(2)}, u32[]{:S(2)}) collective-permute-start(bf16[128,256]{1,0:T(8,128)(2,1)S(1)} %copy-done), channel_id=1, source_target_pairs={{0,4},{1,5},{2,6},{3,7},{4,0},{5,1},{6,2},{7,3},{8,12},{9,13},{10,... | collective-permute-start | bytes 196616 | tf_op jit(solution)/shard_map/ppermute | solution.py:15
  8.5 10.6 %collective-permute-start.7 = (bf16[128,256]{1,0:T(8,128)(2,1)S(1)}, bf16[128,256]{1,0:T(8,128)(2,1)S(1)}, u32[]{:S(2)}, u32[]{:S(2)}) collective-permute-start(bf16[128,256]{1,0:T(8,128)(2,1)S(1)} %copy-done), channel_id=1, source_target_pairs={{0,8},{1,9},{2,10},{3,11},{4,12},{5,13},{6,14},{7,15},{8,0},{9,1},... | collective-permute-start | bytes 196616 | tf_op jit(solution)/shard_map/ppermute | solution.py:15
  9.3 0.7 %copy-start.1 = (bf16[2]{0:T(256)(128)(2,1)S(1)}, bf16[2]{0:T(256)(128)(2,1)}, u32[]{:S(2)}) copy-start(bf16[2]{0:T(256)(128)(2,1)} %param.5) | copy-start | bytes 16
  11.1 12.6 %collective-permute-start.5 = (bf16[256,256]{1,0:T(8,128)(2,1)S(1)}, bf16[256,256]{1,0:T(8,128)(2,1)S(1)}, u32[]{:S(2)}, u32[]{:S(2)}) collective-permute-start(bf16[256,256]{1,0:T(8,128)(2,1)S(1)} %pad_maximum_fusion.6), channel_id=1, source_target_pairs={{0,8},{1,9},{2,10},{3,11},{4,12},{5,13},{6,14},{7,15},{8,0},{9,1},... | collective-permute-start | bytes 393224 | tf_op jit(solution)/shard_map/ppermute | solution.py:15
  12.7 10.9 %collective-permute-start.6 = (bf16[256,256]{1,0:T(8,128)(2,1)S(1)}, bf16[256,256]{1,0:T(8,128)(2,1)S(1)}, u32[]{:S(2)}, u32[]{:S(2)}) collective-permute-start(bf16[256,256]{1,0:T(8,128)(2,1)S(1)} %pad_maximum_fusion.7), channel_id=1, source_target_pairs={{0,12},{1,13},{2,14},{3,15},{4,8},{5,9},{6,10},{7,11},{8,4},{9,5},... | collective-permute-start | bytes 393224 | tf_op jit(solution)/shard_map/ppermute | solution.py:15
  15.5 8.5 %collective-permute-start.4 = (bf16[256,256]{1,0:T(8,128)(2,1)S(1)}, bf16[256,256]{1,0:T(8,128)(2,1)S(1)}, u32[]{:S(2)}, u32[]{:S(2)}) collective-permute-start(bf16[256,256]{1,0:T(8,128)(2,1)S(1)} %pad_maximum_fusion.5), channel_id=1, source_target_pairs={{0,4},{1,5},{2,6},{3,7},{4,0},{5,1},{6,2},{7,3},{8,12},{9,13},{10,... | collective-permute-start | bytes 393224 | tf_op jit(solution)/shard_map/ppermute | solution.py:15
  16.8 4.3 %collective-permute-start.2 = (bf16[128,256]{1,0:T(8,128)(2,1)S(1)}, bf16[128,256]{1,0:T(8,128)(2,1)S(1)}, u32[]{:S(2)}, u32[]{:S(2)}) collective-permute-start(bf16[128,256]{1,0:T(8,128)(2,1)S(1)} %get-tuple-element.34), channel_id=1, source_target_pairs={{0,2},{1,3},{2,0},{3,1},{4,6},{5,7},{6,4},{7,5},{8,10},{9,11},{10,... | collective-permute-start | bytes 196616 | tf_op jit(solution)/shard_map/ppermute | solution.py:15
  19.1 6.4 %collective-permute-start.8 = (bf16[4,128,256]{2,1,0:T(8,128)(2,1)S(1)}, bf16[4,128,256]{2,1,0:T(8,128)(2,1)S(1)}, u32[]{:S(2)}, u32[]{:S(2)}) collective-permute-start(bf16[4,128,256]{2,1,0:T(8,128)(2,1)S(1)} %get-tuple-element.55), channel_id=1, source_target_pairs={{0,2},{1,3},{2,0},{3,1},{4,6},{5,7},{6,4},{7,5},{8,10},{9,11},{10,... | collective-permute-start | bytes 786440 | tf_op jit(solution)/shard_map/ppermute | solution.py:15
  21.1 4.5 %collective-permute-start.9 = (bf16[4,128,256]{2,1,0:T(8,128)(2,1)S(1)}, bf16[4,128,256]{2,1,0:T(8,128)(2,1)S(1)}, u32[]{:S(2)}, u32[]{:S(2)}) collective-permute-start(bf16[4,128,256]{2,1,0:T(8,128)(2,1)S(1)} %get-tuple-element.55), channel_id=1, source_target_pairs={{0,1},{1,0},{2,3},{3,2},{4,5},{5,4},{6,7},{7,6},{8,9},{9,8},{10,11... | collective-permute-start | bytes 786440 | tf_op jit(solution)/shard_map/ppermute | solution.py:15
  24.1 3.1 %collective-permute-start.10 = (bf16[4,256,256]{2,1,0:T(8,128)(2,1)S(1)}, bf16[4,256,256]{2,1,0:T(8,128)(2,1)S(1)}, u32[]{:S(2)}, u32[]{:S(2)}) collective-permute-start(bf16[4,256,256]{2,1,0:T(8,128)(2,1)S(1)} %pad_maximum_fusion.x_ref), channel_id=1, source_target_pairs={{0,1},{1,0},{2,3},{3,2},{4,5},{5,4},{6,7},{7,6},{8,9},{9,8},{10,11... | collective-permute-start | bytes 1572872 | tf_op jit(solution)/shard_map/ppermute | solution.py:15
  25.6 1.5 %collective-permute-start.11 = (bf16[4,128,256]{2,1,0:T(8,128)(2,1)S(1)}, bf16[4,128,256]{2,1,0:T(8,128)(2,1)S(1)}, u32[]{:S(2)}, u32[]{:S(2)}) collective-permute-start(bf16[4,128,256]{2,1,0:T(8,128)(2,1)S(1)} %collective-permute-done.8), channel_id=1, source_target_pairs={{0,1},{1,0},{2,3},{3,2},{4,5},{5,4},{6,7},{7,6},{8,9},{9,8},{10,11... | collective-permute-start | bytes 786440 | tf_op jit(solution)/shard_map/ppermute | solution.py:15

commit v7 on v6

--- a/solution.py
+++ b/solution.py
@@ -57,7 +57,7 @@
     own_ref[...] = (lane == own).astype(jnp.float32)
 
 
-def pair_sums(seq_length, rows_x, rows_c, far_x, far_c, spread, gather, sums_ref):
+def pair_sums(seq_length, rows_x, rows_c, far_x, far_c, spread, sums_ref):
     groups, held, columns = sums_ref.shape
     span = columns // groups
     own = span // seq_length
@@ -92,19 +92,19 @@
     parts = jnp.dot(
         three_parts(sums_ref[...].reshape(count, columns), 0), spread[...], preferred_element_type=jnp.float32
     )
-    by_lane = parts[:count] + (parts[count : 2 * count] + parts[2 * count :])
-    parts = jnp.dot(gather[...], three_parts(by_lane, 1), preferred_element_type=jnp.float32)
-    return parts[:, :LANES] + (parts[:, LANES : 2 * LANES] + parts[:, 2 * LANES :])
-
-
-def own_kernel(seq_length, x_ref, c_ref, spread, gather, out_ref, sums_ref):
-    out_ref[...] = pair_sums(seq_length, x_ref, c_ref, x_ref, c_ref, spread, gather, sums_ref)
+    return parts[:count] + (parts[count : 2 * count] + parts[2 * count :])
+
+
+def own_kernel(seq_length, x_ref, c_ref, spread, out_ref, sums_ref):
+    out_ref[...] = pair_sums(seq_length, x_ref, c_ref, x_ref, c_ref, spread, sums_ref)
 
 
 def far_kernel(
     seq_length, local_count, x_ref, c_ref, far_x, far_c, spread, gather, weight_ref, own_ref, out_ref, sums_ref
 ):
-    half = own_ref[...] + pair_sums(seq_length, x_ref, c_ref, far_x, far_c, spread, gather, sums_ref)
+    by_lane = own_ref[...] + pair_sums(seq_length, x_ref, c_ref, far_x, far_c, spread, sums_ref)
+    parts = jnp.dot(gather[...], three_parts(by_lane, 1), preferred_element_type=jnp.float32)
+    half = parts[:, :LANES] + (parts[:, LANES : 2 * LANES] + parts[:, 2 * LANES :])
     gram = half + half.T
     devices = out_ref.shape[0]
     out_ref[...] = jnp.broadcast_to(weight_ref[: out_ref.shape[1]], out_ref.shape)
@@ -185,17 +185,17 @@
     sums = [pltpu.VMEM((planes, 8, chips * tokens), jnp.float32)]
     own = pl.pallas_call(
         functools.partial(own_kernel, seq_length),
-        out_shape=array((LANES, LANES), jnp.float32),
-        in_specs=[vmem] * 4,
+        out_shape=array((8 * planes, LANES), jnp.float32),
+        in_specs=[vmem] * 3,
         out_specs=vmem,
         scratch_shapes=sums,
         compiler_params=params,
         cost_estimate=pl.CostEstimate(flops=1, bytes_accessed=0, transcendentals=0),
         name="own_kernel",
-    )(own_x, own_c, own_spread, gather)
+    )(own_x, own_c, own_spread)
     partial = pl.pallas_call(
         functools.partial(far_kernel, seq_length, local_count),
-        out_shape=array((devices, 4, LANES), jnp.float32),
+        out_shape=array((devices, 3, LANES), jnp.float32),
         in_specs=[vmem] * 8,
         out_specs=vmem,
         scratch_shapes=sums,

time: 40 us -> 40 us (level)
  no operation moved by 1% of the time
where the time goes in v7:
time: 40 us; the launch traced here: 39.8 us
  starting transfers between devices  14.7 us (37%)
  blocking collectives  10.6 us (26%)
  waiting for transfers between devices  7.86 us (20%)
  Pallas kernels  3.55 us (9%)
  local copies, waits for them, and re-layouts  1.87 us (5%)
  between operations  0.81 us (2%)
    ppermute x12, starting transfers between devices, swapped(): return lax.ppermute(value, 'ex', [(i, i ^ distance) for i in range(count)])  14.7 us
    all_to_all x1, blocking collectives, body(): lax.all_to_all(partial, 'ex', split_axis=0, concat_axis=0, tiled=True)  10.6 us
    ppermute x12, waiting for transfers between devices, swapped(): return lax.ppermute(value, 'ex', [(i, i ^ distance) for i in range(count)])  7.86 us
    pallas_call x1, Pallas kernels, body(): pl.pallas_call(functools.partial(far_kernel, seq_length, local_count), ou...  1.24 us
    dynamic_slice x1, local copies, waits for them, and re-layouts, columns(): lax.dynamic_slice_in_dim(layer_input, (chip ^ distance) * chip_width, chi...  1.12 us
    pallas_call x1, Pallas kernels, body(): pl.pallas_call(functools.partial(own_kernel, seq_length), out_shape=array...  1.03 us
  transfers between devices with their start and end apart: 12, of which 7 were waited for; matrix products, arithmetic and copies ran while one was open for 1% of the time, Pallas kernels for 4%

profile of v7, /device:TPU:0, one launch (start us, length us, event | category | flops | bytes accessed | tf_op | source)
XLA Modules:
  0.0 39.8 jit_solution(773697317179835404)
XLA Ops:
  0.7 1.1 %constant_dynamic-slice_fusion.3 = (bf16[128,256]{1,0:T(8,128)(2,1)S(1)}, bf16[128,256]{1,0:T(8,128)(2,1)S(1)}, bf16[1,128,256]{2,1,0:T(8,128)(2,1)S(1)}, bf16[1...) fusion(bf16[128,2048]{1,0:T(8,128)(2,1)} %param.3, ...), kind=kLoop, calls=%fused_computation.18 | loop fusion | bytes 1048608 | tf_op jit(solution)/shard_map/dynamic_slice | solution.py:150
  1.8 0.0 copy-start
  1.9 3.0 %collective-permute-start = (bf16[3,128,256]{2,1,0:T(8,128)(2,1)S(1)}, bf16[3,128,256]{2,1,0:T(8,128)(2,1)S(1)}, u32[]{:S(2)}, u32[]{:S(2)}) collective-permute-start(bf16[3,128,256]{2,1,0:T(8,128)(2,1)S(1)} %pad_maximum_fusion.4), channel_id=1, source_target_pairs={{0,2},{1,3},{2,0},{3,1},{4,6},{5,7},{6,4},{7,5},{8,10},{9,11},{10,... | collective-permute-start | bytes 589832 | tf_op jit(solution)/shard_map/ppermute | solution.py:15
  4.9 0.0 copy-done
  4.9 3.6 %collective-permute-start.3 = (bf16[128,256]{1,0:T(8,128)(2,1)S(1)}, bf16[128,256]{1,0:T(8,128)(2,1)S(1)}, u32[]{:S(2)}, u32[]{:S(2)}) collective-permute-start(bf16[128,256]{1,0:T(8,128)(2,1)S(1)} %copy-done), channel_id=1, source_target_pairs={{0,12},{1,13},{2,14},{3,15},{4,8},{5,9},{6,10},{7,11},{8,4},{9,5},... | collective-permute-start | bytes 196616 | tf_op jit(solution)/shard_map/ppermute | solution.py:15
  8.5 0.0 collective-permute-start.1
  8.5 0.8 %collective-permute-start.7 = (bf16[128,256]{1,0:T(8,128)(2,1)S(1)}, bf16[128,256]{1,0:T(8,128)(2,1)S(1)}, u32[]{:S(2)}, u32[]{:S(2)}) collective-permute-start(bf16[128,256]{1,0:T(8,128)(2,1)S(1)} %copy-done), channel_id=1, source_target_pairs={{0,8},{1,9},{2,10},{3,11},{4,12},{5,13},{6,14},{7,15},{8,0},{9,1},... | collective-permute-start | bytes 196616 | tf_op jit(solution)/shard_map/ppermute | solution.py:15
  9.3 0.0 copy-start.1
  9.3 0.7 %copy-done.1 = bf16[2]{0:T(256)(128)(2,1)S(1)} copy-done((bf16[2]{0:T(256)(128)(2,1)S(1)}, bf16[2]{0:T(256)(128)(2,1)}, u32[]{:S(2)}) %copy-start.1) | copy-done | bytes 28
  9.9 0.1 pad_add_fusion.place
  10.0 0.0 collective-permute-done
  10.1 1.0 %collective-permute-done.3 = bf16[128,256]{1,0:T(8,128)(2,1)S(1)} collective-permute-done((bf16[128,256]{1,0:T(8,128)(2,1)S(1)}, bf16[128,256]{1,0:T(8,128)(2,1)S(1)}, u32[]{:S(2)}, u32[]{:S(2)}) %collective-permute-start.3) | collective-permute-done | bytes 65568 | tf_op jit(solution)/shard_map/ppermute | solution.py:15
  11.1 1.6 %collective-permute-start.5 = (bf16[256,256]{1,0:T(8,128)(2,1)S(1)}, bf16[256,256]{1,0:T(8,128)(2,1)S(1)}, u32[]{:S(2)}, u32[]{:S(2)}) collective-permute-start(bf16[256,256]{1,0:T(8,128)(2,1)S(1)} %pad_maximum_fusion.6), channel_id=1, source_target_pairs={{0,8},{1,9},{2,10},{3,11},{4,12},{5,13},{6,14},{7,15},{8,0},{9,1},... | collective-permute-start | bytes 393224 | tf_op jit(solution)/shard_map/ppermute | solution.py:15
  12.7 2.8 %collective-permute-start.6 = (bf16[256,256]{1,0:T(8,128)(2,1)S(1)}, bf16[256,256]{1,0:T(8,128)(2,1)S(1)}, u32[]{:S(2)}, u32[]{:S(2)}) collective-permute-start(bf16[256,256]{1,0:T(8,128)(2,1)S(1)} %pad_maximum_fusion.7), channel_id=1, source_target_pairs={{0,12},{1,13},{2,14},{3,15},{4,8},{5,9},{6,10},{7,11},{8,4},{9,5},... | collective-permute-start | bytes 393224 | tf_op jit(solution)/shard_map/ppermute | solution.py:15
  15.5 0.6 %collective-permute-start.4 = (bf16[256,256]{1,0:T(8,128)(2,1)S(1)}, bf16[256,256]{1,0:T(8,128)(2,1)S(1)}, u32[]{:S(2)}, u32[]{:S(2)}) collective-permute-start(bf16[256,256]{1,0:T(8,128)(2,1)S(1)} %pad_maximum_fusion.5), channel_id=1, source_target_pairs={{0,4},{1,5},{2,6},{3,7},{4,0},{5,1},{6,2},{7,3},{8,12},{9,13},{10,... | collective-permute-start | bytes 393224 | tf_op jit(solution)/shard_map/ppermute | solution.py:15
  16.2 0.6 %order_kernel.1 = (bf16[1024,128]{1,0:T(8,128)(2,1)S(1)}, bf16[1024,128]{1,0:T(8,128)(2,1)S(1)}, bf16[128,32]{1,0:T(8,128)(2,1)S(1)}, f32[8,128]{1,0:T(8,128)S(1...) custom-call(s32[2]{0:T(128)S(1)} %pad_add_fusion.place, f32[2]{0:T(128)S(1)} %convert_element_type.3.weight), custom_call_target="tpu_custom_call" | custom-call | tf_op jit(solution)/shard_map/order_kernel/pallas_call | solution.py:157
  16.7 0.0 collective-permute-done.1
  16.8 0.7 %collective-permute-start.2 = (bf16[128,256]{1,0:T(8,128)(2,1)S(1)}, bf16[128,256]{1,0:T(8,128)(2,1)S(1)}, u32[]{:S(2)}, u32[]{:S(2)}) collective-permute-start(bf16[128,256]{1,0:T(8,128)(2,1)S(1)} %get-tuple-element.34), channel_id=1, source_target_pairs={{0,2},{1,3},{2,0},{3,1},{4,6},{5,7},{6,4},{7,5},{8,10},{9,11},{10,... | collective-permute-start | bytes 196616 | tf_op jit(solution)/shard_map/ppermute | solution.py:15
  17.5 1.6 %collective-permute-done.7 = bf16[128,256]{1,0:T(8,128)(2,1)S(1)} collective-permute-done((bf16[128,256]{1,0:T(8,128)(2,1)S(1)}, bf16[128,256]{1,0:T(8,128)(2,1)S(1)}, u32[]{:S(2)}, u32[]{:S(2)}) %collective-permute-start.7) | collective-permute-done | bytes 65568 | tf_op jit(solution)/shard_map/ppermute | solution.py:15
  19.1 1.4 %collective-permute-start.8 = (bf16[4,128,256]{2,1,0:T(8,128)(2,1)S(1)}, bf16[4,128,256]{2,1,0:T(8,128)(2,1)S(1)}, u32[]{:S(2)}, u32[]{:S(2)}) collective-permute-start(bf16[4,128,256]{2,1,0:T(8,128)(2,1)S(1)} %get-tuple-element.55), channel_id=1, source_target_pairs={{0,2},{1,3},{2,0},{3,1},{4,6},{5,7},{6,4},{7,5},{8,10},{9,11},{10,... | collective-permute-start | bytes 786440 | tf_op jit(solution)/shard_map/ppermute | solution.py:15
  20.6 0.5 %collective-permute-done.2 = bf16[128,256]{1,0:T(8,128)(2,1)S(1)} collective-permute-done((bf16[128,256]{1,0:T(8,128)(2,1)S(1)}, bf16[128,256]{1,0:T(8,128)(2,1)S(1)}, u32[]{:S(2)}, u32[]{:S(2)}) %collective-permute-start.2) | collective-permute-done | bytes 65568 | tf_op jit(solution)/shard_map/ppermute | solution.py:15
  21.1 0.0 collective-permute-start.9
  21.1 2.6 %collective-permute-done.5 = bf16[256,256]{1,0:T(8,128)(2,1)S(1)} collective-permute-done((bf16[256,256]{1,0:T(8,128)(2,1)S(1)}, bf16[256,256]{1,0:T(8,128)(2,1)S(1)}, u32[]{:S(2)}, u32[]{:S(2)}) %collective-permute-start.5) | collective-permute-done | bytes 131104 | tf_op jit(solution)/shard_map/ppermute | solution.py:15
  23.7 0.0 collective-permute-done.6
  23.7 0.3 collective-permute-done.4
  24.0 0.1 pad_maximum_fusion.x_ref
  24.1 0.1 collective-permute-start.10
  24.2 1.4 %collective-permute-done.8 = bf16[4,128,256]{2,1,0:T(8,128)(2,1)S(1)} collective-permute-done((bf16[4,128,256]{2,1,0:T(8,128)(2,1)S(1)}, bf16[4,128,256]{2,1,0:T(8,128)(2,1)S(1)}, u32[]{:S(2)}, u32[]{:S(2)}) %collective-permute-start.8) | collective-permute-done | bytes 262176 | tf_op jit(solution)/shard_map/ppermute | solution.py:15
  25.6 0.0 collective-permute-done.9
  25.6 0.0 collective-permute-start.11
  25.6 0.1 pad_maximum_fusion.1
  25.7 1.0 %own_kernel.1.own_ref = f32[32,128]{1,0:T(8,128)S(1)} custom-call(bf16[4,256,256]{2,1,0:T(8,128)(2,1)S(1)} %pad_maximum_fusion.x_ref, bf16[4,256,256]{2,1,0:T(8,128)(2,1)S(1)} %bitcast.31, bf16[1024,128]{1,0:T(8,128)(2,1)S(1)} %get-tuple-element.43.spread), custom_call_target="tpu_custom_call" | custom-call | flops 1 | tf_op jit(solution)/shard_map/own_kernel/pallas_call | solution.py:186
  26.7 0.4 %collective-permute-done.11 = bf16[4,128,256]{2,1,0:T(8,128)(2,1)S(1)} collective-permute-done((bf16[4,128,256]{2,1,0:T(8,128)(2,1)S(1)}, bf16[4,128,256]{2,1,0:T(8,128)(2,1)S(1)}, u32[]{:S(2)}, u32[]{:S(2)}) %collective-permute-start.11) | collective-permute-done | bytes 262176 | tf_op jit(solution)/shard_map/ppermute | solution.py:15
  27.1 0.1 pad_maximum_fusion.2
  27.2 0.0 collective-permute-done.10.far_x
  27.2 1.2 %far_kernel.1 = f32[16,3,128]{2,1,0:T(4,128)S(1)} custom-call(bf16[4,256,256]{2,1,0:T(8,128)(2,1)S(1)} %pad_maximum_fusion.x_ref, bf16[4,256,256]{2,1,0:T(8,128)(2,1)S(1)} %bitcast.32, bf16[4,256,256]{2,1,0:T(8,128)(2,1)S(1)} %collective-permute-done.10.far_x, bf16[4,256,256]{2,1,0:T(8,128)(2,1)S(1)} %bitcast.33, ...), custom_call_target="tpu_custom_call" | custom-call | flops 1 | tf_op jit(solution)/shard_map/far_kernel/pallas_call | solution.py:196
  28.4 10.6 %all_to_all.5.sums_ref = f32[16,3,128]{2,1,0:T(4,128)S(1)} all-to-all(f32[16,3,128]{2,1,0:T(4,128)S(1)} %far_kernel.1), channel_id=1, replica_groups=mesh['grp'=2,'ex'=16] {'ex'}, dimensions={0} | all-to-all | bytes 49152 | tf_op jit(solution)/shard_map/all_to_all | solution.py:207
  39.1 0.7 %output_kernel.1 = (f32[2,32]{1,0:T(2,128)}, f32[1,2]{1,0:T(1,128)}) custom-call(f32[8,128]{1,0:T(8,128)S(1)} %get-tuple-element.32.below, f32[8,128]{1,0:T(8,128)S(1)} %get-tuple-element.33.diagonal, f32[16,3,128]{2,1,0:T(4,128)S(1)} %all_to_all.5.sums_ref), custom_call_target="tpu_custom_call" | custom-call | tf_op jit(solution)/shard_map/output_kernel/pallas_call | solution.py:210
  (10 shorter events, 0.2 us)
Async XLA Ops:
  1.8 3.1 %copy-start = (bf16[128,256]{1,0:T(8,128)(2,1)S(1)}, bf16[128,256]{1,0:T(8,128)(2,1)}, u32[]{:S(2)}) copy-start(bf16[128,256]{1,0:T(8,128)(2,1)} %param.4) | copy-start | bytes 196612
  1.9 8.2 %collective-permute-start = (bf16[3,128,256]{2,1,0:T(8,128)(2,1)S(1)}, bf16[3,128,256]{2,1,0:T(8,128)(2,1)S(1)}, u32[]{:S(2)}, u32[]{:S(2)}) collective-permute-start(bf16[3,128,256]{2,1,0:T(8,128)(2,1)S(1)} %pad_maximum_fusion.4), channel_id=1, source_target_pairs={{0,2},{1,3},{2,0},{3,1},{4,6},{5,7},{6,4},{7,5},{8,10},{9,11},{10,... | collective-permute-start | bytes 589832 | tf_op jit(solution)/shard_map/ppermute | solution.py:15
  4.9 6.2 %collective-permute-start.3 = (bf16[128,256]{1,0:T(8,128)(2,1)S(1)}, bf16[128,256]{1,0:T(8,128)(2,1)S(1)}, u32[]{:S(2)}, u32[]{:S(2)}) collective-permute-start(bf16[128,256]{1,0:T(8,128)(2,1)S(1)} %copy-done), channel_id=1, source_target_pairs={{0,12},{1,13},{2,14},{3,15},{4,8},{5,9},{6,10},{7,11},{8,4},{9,5},... | collective-permute-start | bytes 196616 | tf_op jit(solution)/shard_map/ppermute | solution.py:15
  8.5 8.3 %collective-permute-start.1 = (bf16[128,256]{1,0:T(8,128)(2,1)S(1)}, bf16[128,256]{1,0:T(8,128)(2,1)S(1)}, u32[]{:S(2)}, u32[]{:S(2)}) collective-permute-start(bf16[128,256]{1,0:T(8,128)(2,1)S(1)} %copy-done), channel_id=1, source_target_pairs={{0,4},{1,5},{2,6},{3,7},{4,0},{5,1},{6,2},{7,3},{8,12},{9,13},{10,... | collective-permute-start | bytes 196616 | tf_op jit(solution)/shard_map/ppermute | solution.py:15
  8.5 10.6 %collective-permute-start.7 = (bf16[128,256]{1,0:T(8,128)(2,1)S(1)}, bf16[128,256]{1,0:T(8,128)(2,1)S(1)}, u32[]{:S(2)}, u32[]{:S(2)}) collective-permute-start(bf16[128,256]{1,0:T(8,128)(2,1)S(1)} %copy-done), channel_id=1, source_target_pairs={{0,8},{1,9},{2,10},{3,11},{4,12},{5,13},{6,14},{7,15},{8,0},{9,1},... | collective-permute-start | bytes 196616 | tf_op jit(solution)/shard_map/ppermute | solution.py:15
  9.3 0.7 %copy-start.1 = (bf16[2]{0:T(256)(128)(2,1)S(1)}, bf16[2]{0:T(256)(128)(2,1)}, u32[]{:S(2)}) copy-start(bf16[2]{0:T(256)(128)(2,1)} %param.5) | copy-start | bytes 16
  11.1 12.6 %collective-permute-start.5 = (bf16[256,256]{1,0:T(8,128)(2,1)S(1)}, bf16[256,256]{1,0:T(8,128)(2,1)S(1)}, u32[]{:S(2)}, u32[]{:S(2)}) collective-permute-start(bf16[256,256]{1,0:T(8,128)(2,1)S(1)} %pad_maximum_fusion.6), channel_id=1, source_target_pairs={{0,8},{1,9},{2,10},{3,11},{4,12},{5,13},{6,14},{7,15},{8,0},{9,1},... | collective-permute-start | bytes 393224 | tf_op jit(solution)/shard_map/ppermute | solution.py:15
  12.7 10.9 %collective-permute-start.6 = (bf16[256,256]{1,0:T(8,128)(2,1)S(1)}, bf16[256,256]{1,0:T(8,128)(2,1)S(1)}, u32[]{:S(2)}, u32[]{:S(2)}) collective-permute-start(bf16[256,256]{1,0:T(8,128)(2,1)S(1)} %pad_maximum_fusion.7), channel_id=1, source_target_pairs={{0,12},{1,13},{2,14},{3,15},{4,8},{5,9},{6,10},{7,11},{8,4},{9,5},... | collective-permute-start | bytes 393224 | tf_op jit(solution)/shard_map/ppermute | solution.py:15
  15.5 8.5 %collective-permute-start.4 = (bf16[256,256]{1,0:T(8,128)(2,1)S(1)}, bf16[256,256]{1,0:T(8,128)(2,1)S(1)}, u32[]{:S(2)}, u32[]{:S(2)}) collective-permute-start(bf16[256,256]{1,0:T(8,128)(2,1)S(1)} %pad_maximum_fusion.5), channel_id=1, source_target_pairs={{0,4},{1,5},{2,6},{3,7},{4,0},{5,1},{6,2},{7,3},{8,12},{9,13},{10,... | collective-permute-start | bytes 393224 | tf_op jit(solution)/shard_map/ppermute | solution.py:15
  16.8 4.3 %collective-permute-start.2 = (bf16[128,256]{1,0:T(8,128)(2,1)S(1)}, bf16[128,256]{1,0:T(8,128)(2,1)S(1)}, u32[]{:S(2)}, u32[]{:S(2)}) collective-permute-start(bf16[128,256]{1,0:T(8,128)(2,1)S(1)} %get-tuple-element.34), channel_id=1, source_target_pairs={{0,2},{1,3},{2,0},{3,1},{4,6},{5,7},{6,4},{7,5},{8,10},{9,11},{10,... | collective-permute-start | bytes 196616 | tf_op jit(solution)/shard_map/ppermute | solution.py:15
  19.1 6.4 %collective-permute-start.8 = (bf16[4,128,256]{2,1,0:T(8,128)(2,1)S(1)}, bf16[4,128,256]{2,1,0:T(8,128)(2,1)S(1)}, u32[]{:S(2)}, u32[]{:S(2)}) collective-permute-start(bf16[4,128,256]{2,1,0:T(8,128)(2,1)S(1)} %get-tuple-element.55), channel_id=1, source_target_pairs={{0,2},{1,3},{2,0},{3,1},{4,6},{5,7},{6,4},{7,5},{8,10},{9,11},{10,... | collective-permute-start | bytes 786440 | tf_op jit(solution)/shard_map/ppermute | solution.py:15
  21.1 4.5 %collective-permute-start.9 = (bf16[4,128,256]{2,1,0:T(8,128)(2,1)S(1)}, bf16[4,128,256]{2,1,0:T(8,128)(2,1)S(1)}, u32[]{:S(2)}, u32[]{:S(2)}) collective-permute-start(bf16[4,128,256]{2,1,0:T(8,128)(2,1)S(1)} %get-tuple-element.55), channel_id=1, source_target_pairs={{0,1},{1,0},{2,3},{3,2},{4,5},{5,4},{6,7},{7,6},{8,9},{9,8},{10,11... | collective-permute-start | bytes 786440 | tf_op jit(solution)/shard_map/ppermute | solution.py:15
  24.1 3.1 %collective-permute-start.10 = (bf16[4,256,256]{2,1,0:T(8,128)(2,1)S(1)}, bf16[4,256,256]{2,1,0:T(8,128)(2,1)S(1)}, u32[]{:S(2)}, u32[]{:S(2)}) collective-permute-start(bf16[4,256,256]{2,1,0:T(8,128)(2,1)S(1)} %pad_maximum_fusion.x_ref), channel_id=1, source_target_pairs={{0,1},{1,0},{2,3},{3,2},{4,5},{5,4},{6,7},{7,6},{8,9},{9,8},{10,11... | collective-permute-start | bytes 1572872 | tf_op jit(solution)/shard_map/ppermute | solution.py:15
  25.6 1.5 %collective-permute-start.11 = (bf16[4,128,256]{2,1,0:T(8,128)(2,1)S(1)}, bf16[4,128,256]{2,1,0:T(8,128)(2,1)S(1)}, u32[]{:S(2)}, u32[]{:S(2)}) collective-permute-start(bf16[4,128,256]{2,1,0:T(8,128)(2,1)S(1)} %collective-permute-done.8), channel_id=1, source_target_pairs={{0,1},{1,0},{2,3},{3,2},{4,5},{5,4},{6,7},{7,6},{8,9},{9,8},{10,11... | collective-permute-start | bytes 786440 | tf_op jit(solution)/shard_map/ppermute | solution.py:15
